TPU v7x, 512 devices: a whole 4x8x8 slice. The times are simulated.
512 devices in a mesh: tm: 512 (over y, x, z, core).
Axes of the slice: x: 4, y: 8, z: 8, core: 2. Of those that a mesh axis runs over, the one named last changes fastest.
Arguments:
- initial: float32 [2, 64, 64], replicated, may hold values from 0 to 0.6
- coarse_guess: float32 [512, 2, 64, 64], P('tm'), may hold values from 0 to 0.6
- feed_rate: float32 [64, 64], replicated, may hold values from 0.02 to 0.08
- kill_rate: float32 [64, 64], replicated, may hold values from 0.03 to 0.07
Outputs:
- trajectory: float32 [2048, 2, 64, 64], P('tm')
- c_residual: float32 [512, 2, 64, 64], P('tm')
- group_coarse: float32 [512, 2, 64, 64], P('tm')
- level_defect: float32 [512, 2, 64, 64], P('tm')
All inputs are finite; a program needn't handle non-finite values.
Results may differ from a plain program's by a relative error of at most 0.0004.
Values sent between devices are 32-bit elements; how exact they have to be, the bound alone decides.
No kernel may reach another device: no remote copies, remote signals or barrier semaphores. Data moves between devices by JAX's collectives and lax.ppermute only.
A program may use at most 64 MiB of HBM per device.

v0:
```python
import jax
import jax.numpy as jnp
from jax import lax
from jax.sharding import PartitionSpec as P

STEPS_DEV = 4
GROUP = 16


diffusion = (0.2, 0.1)
interval_time = 0.03125
highest = lax.Precision.HIGHEST


def shifted_2(block, axis, distance):
    devices = range(lax.axis_size(axis))
    route = [(i - distance, i) for i in devices if i - distance in devices]
    return lax.ppermute(block, axis, route)


def cosine_basis(length):
    positions = jnp.arange(length, dtype=jnp.float32)
    angles = jnp.pi * (positions[:, None] + 0.5) * positions[None, :] / length
    weight = jnp.where(positions == 0, jnp.sqrt(1.0 / length), jnp.sqrt(2.0 / length))
    return jnp.cos(angles) * weight[None, :]


def eigen_values(length):
    positions = jnp.arange(length, dtype=jnp.float32)
    return -4.0 * jnp.sin(jnp.pi * positions / (2.0 * length)) ** 2


def make_tables(rows_first, rows_second):
    spectrum = eigen_values(rows_first)[:, None] + eigen_values(rows_second)[None, :]
    return (cosine_basis(rows_first), cosine_basis(rows_second), spectrum)


def advance(fields, feed_rate, kill_rate, time_step, tables):
    basis_rows, basis_cols, spectrum = tables
    substrate = fields[..., 0, :, :]
    catalyst = fields[..., 1, :, :]
    uptake = substrate * catalyst * catalyst
    substrate_new = substrate + time_step * (feed_rate * (1.0 - substrate) - uptake)
    catalyst_new = catalyst + time_step * (uptake - (feed_rate + kill_rate) * catalyst)
    reacted = jnp.stack([substrate_new, catalyst_new], axis=-3)
    spectral = jnp.matmul(
        jnp.matmul(basis_rows.T, reacted, precision=highest), basis_cols, precision=highest
    )
    diff_rates = jnp.array(diffusion, dtype=jnp.float32)
    spectral = spectral / (1.0 - time_step * diff_rates[:, None, None] * spectrum)
    return jnp.matmul(
        jnp.matmul(basis_rows, spectral, precision=highest), basis_cols.T, precision=highest
    )


def march(start_state, feed_rate, kill_rate, time_step, tables, count_steps):

    def turn(fields, unused):
        fields = advance(fields, feed_rate, kill_rate, time_step, tables)
        return (fields, fields)

    finished, visited = lax.scan(turn, start_state, None, length=count_steps)
    return (finished, visited)


def shards(initial, coarse_guess, feed_rate, kill_rate):
    tables = make_tables(initial.shape[1], initial.shape[2])
    fine_step = interval_time / STEPS_DEV
    coarse_step = interval_time * GROUP
    devices = lax.axis_size("tm")
    groups = devices // GROUP
    position = lax.axis_index("tm")
    leading = position == 0
    member = position % GROUP
    group_id = position // GROUP
    start_count = jnp.zeros((), jnp.int32)

    def evolve(fields, time_step):
        return advance(fields, feed_rate, kill_rate, time_step, tables)

    own_guess = coarse_guess[0]
    incoming = shifted_2(own_guess, "tm", 1)
    incoming = jnp.where(leading, initial, incoming)
    relaxed, unused = march(incoming, feed_rate, kill_rate, fine_step, tables, STEPS_DEV)
    shifted = shifted_2(relaxed, "tm", 1)
    shifted = jnp.where(leading, initial, shifted)
    arrived, unused = march(shifted, feed_rate, kill_rate, fine_step, tables, STEPS_DEV)
    c_residual = arrived - relaxed
    level_rhs = arrived - evolve(shifted, interval_time)

    def forward_turn(turn_number, state_pack):
        current, closing = state_pack
        received = shifted_2(current, "tm", 1)
        received = jnp.where(leading, initial, received)
        updated = evolve(received, interval_time) + level_rhs
        active = member == turn_number
        current = jnp.where(active & (member < GROUP - 1), updated, current)
        closing = jnp.where(active, updated, closing)
        return (current, closing)

    current, closing = lax.fori_loop(0, GROUP, forward_turn, (relaxed, jnp.zeros_like(relaxed)))
    handed = evolve(relaxed, coarse_step)
    is_closer = member == GROUP - 1
    slot_ids = jnp.arange(groups, dtype=jnp.int32)
    add_here = ((slot_ids == group_id) & is_closer).astype(jnp.float32)
    take_next = ((slot_ids == group_id + 1) & is_closer).astype(jnp.float32)
    slot_terms = (
        add_here[:, None, None, None] * closing[None]
        - take_next[:, None, None, None] * handed[None]
    )
    coarse_rhs = lax.psum(slot_terms, "tm")
    coarse_rhs = coarse_rhs.at[0].add(-evolve(initial, coarse_step))

    def coarse_turn(state_pack, right_side):
        fields, earlier, mine_value, counter = state_pack
        fields = evolve(fields, coarse_step) + right_side
        earlier = jnp.where(counter == group_id - 1, fields, earlier)
        mine_value = jnp.where(counter == group_id, fields, mine_value)
        return ((fields, earlier, mine_value, counter + 1), None)

    packed, unused = lax.scan(
        coarse_turn, (initial, initial, initial, start_count), coarse_rhs, unroll=4
    )
    earlier = packed[1]
    mine_value = packed[2]
    seeded = jnp.where(member == GROUP - 1, mine_value, jnp.zeros_like(mine_value))

    def back_turn(turn_number, state_pack):
        current, finishing = state_pack
        received = shifted_2(current, "tm", 1)
        received = jnp.where(leading, initial, received)
        updated = evolve(received, interval_time) + level_rhs
        active = member == turn_number
        current = jnp.where(active & (member < GROUP - 1), updated, current)
        finishing = jnp.where(active, updated, finishing)
        return (current, finishing)

    corrected, finishing = lax.fori_loop(0, GROUP, back_turn, (seeded, jnp.zeros_like(seeded)))
    level_defect = jnp.where(
        member == GROUP - 1, finishing - mine_value, jnp.zeros_like(mine_value)
    )
    prior_state = shifted_2(corrected, "tm", 1)
    prior_state = jnp.where(leading, initial, prior_state)
    unused, interior = march(prior_state, feed_rate, kill_rate, fine_step, tables, STEPS_DEV - 1)
    trajectory = jnp.concatenate([interior, corrected[None]], axis=0)
    return (trajectory, c_residual[None], mine_value[None], level_defect[None])


def solution(mesh):
    in_specs = (P(), P("tm", None, None, None), P(), P())
    out_specs = (
        P("tm", None, None, None),
        P("tm", None, None, None),
        P("tm", None, None, None),
        P("tm", None, None, None),
    )
    return jax.shard_map(shards, mesh=mesh, in_specs=in_specs, out_specs=out_specs, check_vma=False)
```

profile of v0, /device:TPU:32, one launch (start us, length us, event | category | flops | bytes accessed | tf_op | source)
XLA Modules:
  0.0 857.5 jit_solution(8190128386309178813)
XLA Ops:
  10.5 11.3 %collective-permute-done.2 = f32[2,64,64]{2,1,0:T(8,128)S(1)} collective-permute-done((f32[2,64,64]{2,1,0:T(8,128)}, f32[2,64,64]{2,1,0:T(8,128)S(1)}, u32[]{:S(2)}, u32[]{:S(2)}) %collective-permute-start.2) | collective-permute-done | bytes 32800 | tf_op jit(solution)/shard_map/ppermute | solution.py:18
  21.9 12.4 %while.118 = (s32[]{:T(128)}, f32[2,64,64]{2,1,0:T(8,128)S(1)}, f32[64,64]{1,0:T(8,128)}, f32[1,64,64]{2,1,0:T(8,128)S(1)}, f32[64]{0:T(128)S(1)}, /*index=5*/f3...) while((s32[]{:T(128)}, f32[2,64,64]{2,1,0:T(8,128)S(1)}, ...), condition=%wide.region_1.2_spmd.clone.clone.clone, body=%wide.region_0.1_spmd.sunk.clone.clone.clone.sunk | while | flops 25296896 | bytes 395621 | solution.py:62
  36.3 9.0 %collective-permute-done.3 = f32[2,64,64]{2,1,0:T(8,128)S(1)} collective-permute-done((f32[2,64,64]{2,1,0:T(8,128)S(1)}, f32[2,64,64]{2,1,0:T(8,128)S(1)}, u32[]{:S(2)}, u32[]{:S(2)}) %collective-permute-start.3) | collective-permute-done | bytes 32800 | tf_op jit(solution)/shard_map/ppermute | solution.py:18
  47.4 12.4 %while.119 = (s32[]{:T(128)}, f32[2,64,64]{2,1,0:T(8,128)S(1)}, f32[64,64]{1,0:T(8,128)}, f32[1,64,64]{2,1,0:T(8,128)S(1)}, f32[64]{0:T(128)S(1)}, /*index=5*/f3...) while((s32[]{:T(128)}, f32[2,64,64]{2,1,0:T(8,128)S(1)}, ...), condition=%wide.region_3.4_spmd.clone.clone.clone, body=%wide.region_2.3_spmd.sunk.clone.clone.clone.sunk | while | flops 25296896 | bytes 395621 | solution.py:62
  61.9 214.7 %while.122 = (s32[]{:T(128)}, f32[2,64,64]{2,1,0:T(8,128)S(1)}, f32[2,64,64]{2,1,0:T(8,128)S(1)}, s32[]{:T(128)}, pred[]{:T(512)}, /*index=5*/pred[]{:T(512)}, f...) while((s32[]{:T(128)}, f32[2,64,64]{2,1,0:T(8,128)S(1)}, ...), condition=%wide.region_5.6_spmd.clone.clone.clone, body=%wide.region_4.5_spmd.sunk.clone.clone.clone.sunk | while | flops 25337860 | bytes 756190 | solution.py:101
  63.9 9.0 %collective-permute-done = f32[2,64,64]{2,1,0:T(8,128)S(1)} collective-permute-done((f32[2,64,64]{2,1,0:T(8,128)S(1)}, f32[2,64,64]{2,1,0:T(8,128)S(1)}, u32[]{:S(2)}, u32[]{:S(2)}) %collective-permute-start) | collective-permute-done | bytes 32800 | tf_op jit(solution)/shard_map/while/body/eval_jaxpr/ppermute | solution.py:18
  77.4 9.0 %collective-permute-done = f32[2,64,64]{2,1,0:T(8,128)S(1)} collective-permute-done((f32[2,64,64]{2,1,0:T(8,128)S(1)}, f32[2,64,64]{2,1,0:T(8,128)S(1)}, u32[]{:S(2)}, u32[]{:S(2)}) %collective-permute-start) | collective-permute-done | bytes 32800 | tf_op jit(solution)/shard_map/while/body/eval_jaxpr/ppermute | solution.py:18
  88.8 1.9 collective-permute-start
  90.8 9.0 %collective-permute-done = f32[2,64,64]{2,1,0:T(8,128)S(1)} collective-permute-done((f32[2,64,64]{2,1,0:T(8,128)S(1)}, f32[2,64,64]{2,1,0:T(8,128)S(1)}, u32[]{:S(2)}, u32[]{:S(2)}) %collective-permute-start) | collective-permute-done | bytes 32800 | tf_op jit(solution)/shard_map/while/body/eval_jaxpr/ppermute | solution.py:18
  102.2 1.9 collective-permute-start
  104.2 9.0 %collective-permute-done = f32[2,64,64]{2,1,0:T(8,128)S(1)} collective-permute-done((f32[2,64,64]{2,1,0:T(8,128)S(1)}, f32[2,64,64]{2,1,0:T(8,128)S(1)}, u32[]{:S(2)}, u32[]{:S(2)}) %collective-permute-start) | collective-permute-done | bytes 32800 | tf_op jit(solution)/shard_map/while/body/eval_jaxpr/ppermute | solution.py:18
  117.6 9.0 %collective-permute-done = f32[2,64,64]{2,1,0:T(8,128)S(1)} collective-permute-done((f32[2,64,64]{2,1,0:T(8,128)S(1)}, f32[2,64,64]{2,1,0:T(8,128)S(1)}, u32[]{:S(2)}, u32[]{:S(2)}) %collective-permute-start) | collective-permute-done | bytes 32800 | tf_op jit(solution)/shard_map/while/body/eval_jaxpr/ppermute | solution.py:18
  131.0 9.0 %collective-permute-done = f32[2,64,64]{2,1,0:T(8,128)S(1)} collective-permute-done((f32[2,64,64]{2,1,0:T(8,128)S(1)}, f32[2,64,64]{2,1,0:T(8,128)S(1)}, u32[]{:S(2)}, u32[]{:S(2)}) %collective-permute-start) | collective-permute-done | bytes 32800 | tf_op jit(solution)/shard_map/while/body/eval_jaxpr/ppermute | solution.py:18
  144.5 9.0 %collective-permute-done = f32[2,64,64]{2,1,0:T(8,128)S(1)} collective-permute-done((f32[2,64,64]{2,1,0:T(8,128)S(1)}, f32[2,64,64]{2,1,0:T(8,128)S(1)}, u32[]{:S(2)}, u32[]{:S(2)}) %collective-permute-start) | collective-permute-done | bytes 32800 | tf_op jit(solution)/shard_map/while/body/eval_jaxpr/ppermute | solution.py:18
  157.9 9.0 %collective-permute-done = f32[2,64,64]{2,1,0:T(8,128)S(1)} collective-permute-done((f32[2,64,64]{2,1,0:T(8,128)S(1)}, f32[2,64,64]{2,1,0:T(8,128)S(1)}, u32[]{:S(2)}, u32[]{:S(2)}) %collective-permute-start) | collective-permute-done | bytes 32800 | tf_op jit(solution)/shard_map/while/body/eval_jaxpr/ppermute | solution.py:18
  171.3 9.0 %collective-permute-done = f32[2,64,64]{2,1,0:T(8,128)S(1)} collective-permute-done((f32[2,64,64]{2,1,0:T(8,128)S(1)}, f32[2,64,64]{2,1,0:T(8,128)S(1)}, u32[]{:S(2)}, u32[]{:S(2)}) %collective-permute-start) | collective-permute-done | bytes 32800 | tf_op jit(solution)/shard_map/while/body/eval_jaxpr/ppermute | solution.py:18
  184.7 9.0 %collective-permute-done = f32[2,64,64]{2,1,0:T(8,128)S(1)} collective-permute-done((f32[2,64,64]{2,1,0:T(8,128)S(1)}, f32[2,64,64]{2,1,0:T(8,128)S(1)}, u32[]{:S(2)}, u32[]{:S(2)}) %collective-permute-start) | collective-permute-done | bytes 32800 | tf_op jit(solution)/shard_map/while/body/eval_jaxpr/ppermute | solution.py:18
  198.1 9.0 %collective-permute-done = f32[2,64,64]{2,1,0:T(8,128)S(1)} collective-permute-done((f32[2,64,64]{2,1,0:T(8,128)S(1)}, f32[2,64,64]{2,1,0:T(8,128)S(1)}, u32[]{:S(2)}, u32[]{:S(2)}) %collective-permute-start) | collective-permute-done | bytes 32800 | tf_op jit(solution)/shard_map/while/body/eval_jaxpr/ppermute | solution.py:18
  211.6 9.0 %collective-permute-done = f32[2,64,64]{2,1,0:T(8,128)S(1)} collective-permute-done((f32[2,64,64]{2,1,0:T(8,128)S(1)}, f32[2,64,64]{2,1,0:T(8,128)S(1)}, u32[]{:S(2)}, u32[]{:S(2)}) %collective-permute-start) | collective-permute-done | bytes 32800 | tf_op jit(solution)/shard_map/while/body/eval_jaxpr/ppermute | solution.py:18
  223.0 1.9 collective-permute-start
  225.0 9.0 %collective-permute-done = f32[2,64,64]{2,1,0:T(8,128)S(1)} collective-permute-done((f32[2,64,64]{2,1,0:T(8,128)S(1)}, f32[2,64,64]{2,1,0:T(8,128)S(1)}, u32[]{:S(2)}, u32[]{:S(2)}) %collective-permute-start) | collective-permute-done | bytes 32800 | tf_op jit(solution)/shard_map/while/body/eval_jaxpr/ppermute | solution.py:18
  238.4 9.0 %collective-permute-done = f32[2,64,64]{2,1,0:T(8,128)S(1)} collective-permute-done((f32[2,64,64]{2,1,0:T(8,128)S(1)}, f32[2,64,64]{2,1,0:T(8,128)S(1)}, u32[]{:S(2)}, u32[]{:S(2)}) %collective-permute-start) | collective-permute-done | bytes 32800 | tf_op jit(solution)/shard_map/while/body/eval_jaxpr/ppermute | solution.py:18
  251.8 9.0 %collective-permute-done = f32[2,64,64]{2,1,0:T(8,128)S(1)} collective-permute-done((f32[2,64,64]{2,1,0:T(8,128)S(1)}, f32[2,64,64]{2,1,0:T(8,128)S(1)}, u32[]{:S(2)}, u32[]{:S(2)}) %collective-permute-start) | collective-permute-done | bytes 32800 | tf_op jit(solution)/shard_map/while/body/eval_jaxpr/ppermute | solution.py:18
  265.2 9.0 %collective-permute-done = f32[2,64,64]{2,1,0:T(8,128)S(1)} collective-permute-done((f32[2,64,64]{2,1,0:T(8,128)S(1)}, f32[2,64,64]{2,1,0:T(8,128)S(1)}, u32[]{:S(2)}, u32[]{:S(2)}) %collective-permute-start) | collective-permute-done | bytes 32800 | tf_op jit(solution)/shard_map/while/body/eval_jaxpr/ppermute | solution.py:18
  279.8 270.3 %all-reduce.2.cloned.1.call-done = f32[32,2,64,64]{3,2,1,0:T(8,128)} async-done(((f32[32,2,64,64]{3,2,1,0:T(8,128)}), f32[32,2,64,64]{3,2,1,0:T(8,128)}) %all-reduce.2.cloned.1.call-update) | async-done | bytes 1048592 | tf_op jit(solution)/shard_map/psum | solution.py:111
  551.9 79.2 %while.121 = (s32[]{:T(128)}, f32[2,64,64]{2,1,0:T(8,128)S(1)}, f32[2,64,64]{2,1,0:T(8,128)S(1)}, f32[64,64]{1,0:T(8,128)S(1)}, f32[1,64,64]{2,1,0:T(8,128)S(1)}...) while((s32[]{:T(128)}, f32[2,64,64]{2,1,0:T(8,128)S(1)}, ...), condition=%wide.region_8.9_spmd.clone.clone.clone.clone.clone, body=%wide.region_7.8_spmd.sunk.clone.clone.clone.clone.clone.clone.sunk | while | flops 101240832 | bytes 1827429 | solution.py:121
  631.2 202.6 %while.123 = (s32[]{:T(128)}, f32[2,64,64]{2,1,0:T(8,128)S(1)}, f32[2,64,64]{2,1,0:T(8,128)S(1)}, s32[]{:T(128)}, pred[]{:T(512)}, /*index=5*/pred[]{:T(512)}, f...) while((s32[]{:T(128)}, f32[2,64,64]{2,1,0:T(8,128)S(1)}, ...), condition=%wide.region_10.11_spmd.clone.clone.clone, body=%wide.region_9.10_spmd.sunk.clone.clone.clone.sunk | while | flops 25337860 | bytes 756190 | solution.py:138
  633.2 9.0 %collective-permute-done.1 = f32[2,64,64]{2,1,0:T(8,128)S(1)} collective-permute-done((f32[2,64,64]{2,1,0:T(8,128)S(1)}, f32[2,64,64]{2,1,0:T(8,128)S(1)}, u32[]{:S(2)}, u32[]{:S(2)}) %collective-permute-start.1) | collective-permute-done | bytes 32800 | tf_op jit(solution)/shard_map/while/body/eval_jaxpr/ppermute | solution.py:18
  643.8 1.9 collective-permute-start.1
  645.8 9.0 %collective-permute-done.1 = f32[2,64,64]{2,1,0:T(8,128)S(1)} collective-permute-done((f32[2,64,64]{2,1,0:T(8,128)S(1)}, f32[2,64,64]{2,1,0:T(8,128)S(1)}, u32[]{:S(2)}, u32[]{:S(2)}) %collective-permute-start.1) | collective-permute-done | bytes 32800 | tf_op jit(solution)/shard_map/while/body/eval_jaxpr/ppermute | solution.py:18
  656.5 1.9 collective-permute-start.1
  658.5 9.0 %collective-permute-done.1 = f32[2,64,64]{2,1,0:T(8,128)S(1)} collective-permute-done((f32[2,64,64]{2,1,0:T(8,128)S(1)}, f32[2,64,64]{2,1,0:T(8,128)S(1)}, u32[]{:S(2)}, u32[]{:S(2)}) %collective-permute-start.1) | collective-permute-done | bytes 32800 | tf_op jit(solution)/shard_map/while/body/eval_jaxpr/ppermute | solution.py:18
  671.2 9.0 %collective-permute-done.1 = f32[2,64,64]{2,1,0:T(8,128)S(1)} collective-permute-done((f32[2,64,64]{2,1,0:T(8,128)S(1)}, f32[2,64,64]{2,1,0:T(8,128)S(1)}, u32[]{:S(2)}, u32[]{:S(2)}) %collective-permute-start.1) | collective-permute-done | bytes 32800 | tf_op jit(solution)/shard_map/while/body/eval_jaxpr/ppermute | solution.py:18
  683.8 9.0 %collective-permute-done.1 = f32[2,64,64]{2,1,0:T(8,128)S(1)} collective-permute-done((f32[2,64,64]{2,1,0:T(8,128)S(1)}, f32[2,64,64]{2,1,0:T(8,128)S(1)}, u32[]{:S(2)}, u32[]{:S(2)}) %collective-permute-start.1) | collective-permute-done | bytes 32800 | tf_op jit(solution)/shard_map/while/body/eval_jaxpr/ppermute | solution.py:18
  696.5 9.0 %collective-permute-done.1 = f32[2,64,64]{2,1,0:T(8,128)S(1)} collective-permute-done((f32[2,64,64]{2,1,0:T(8,128)S(1)}, f32[2,64,64]{2,1,0:T(8,128)S(1)}, u32[]{:S(2)}, u32[]{:S(2)}) %collective-permute-start.1) | collective-permute-done | bytes 32800 | tf_op jit(solution)/shard_map/while/body/eval_jaxpr/ppermute | solution.py:18
  709.2 9.0 %collective-permute-done.1 = f32[2,64,64]{2,1,0:T(8,128)S(1)} collective-permute-done((f32[2,64,64]{2,1,0:T(8,128)S(1)}, f32[2,64,64]{2,1,0:T(8,128)S(1)}, u32[]{:S(2)}, u32[]{:S(2)}) %collective-permute-start.1) | collective-permute-done | bytes 32800 | tf_op jit(solution)/shard_map/while/body/eval_jaxpr/ppermute | solution.py:18
  721.8 9.0 %collective-permute-done.1 = f32[2,64,64]{2,1,0:T(8,128)S(1)} collective-permute-done((f32[2,64,64]{2,1,0:T(8,128)S(1)}, f32[2,64,64]{2,1,0:T(8,128)S(1)}, u32[]{:S(2)}, u32[]{:S(2)}) %collective-permute-start.1) | collective-permute-done | bytes 32800 | tf_op jit(solution)/shard_map/while/body/eval_jaxpr/ppermute | solution.py:18
  732.5 1.9 collective-permute-start.1
  734.5 9.0 %collective-permute-done.1 = f32[2,64,64]{2,1,0:T(8,128)S(1)} collective-permute-done((f32[2,64,64]{2,1,0:T(8,128)S(1)}, f32[2,64,64]{2,1,0:T(8,128)S(1)}, u32[]{:S(2)}, u32[]{:S(2)}) %collective-permute-start.1) | collective-permute-done | bytes 32800 | tf_op jit(solution)/shard_map/while/body/eval_jaxpr/ppermute | solution.py:18
  747.2 9.0 %collective-permute-done.1 = f32[2,64,64]{2,1,0:T(8,128)S(1)} collective-permute-done((f32[2,64,64]{2,1,0:T(8,128)S(1)}, f32[2,64,64]{2,1,0:T(8,128)S(1)}, u32[]{:S(2)}, u32[]{:S(2)}) %collective-permute-start.1) | collective-permute-done | bytes 32800 | tf_op jit(solution)/shard_map/while/body/eval_jaxpr/ppermute | solution.py:18
  759.8 9.0 %collective-permute-done.1 = f32[2,64,64]{2,1,0:T(8,128)S(1)} collective-permute-done((f32[2,64,64]{2,1,0:T(8,128)S(1)}, f32[2,64,64]{2,1,0:T(8,128)S(1)}, u32[]{:S(2)}, u32[]{:S(2)}) %collective-permute-start.1) | collective-permute-done | bytes 32800 | tf_op jit(solution)/shard_map/while/body/eval_jaxpr/ppermute | solution.py:18
  772.5 9.0 %collective-permute-done.1 = f32[2,64,64]{2,1,0:T(8,128)S(1)} collective-permute-done((f32[2,64,64]{2,1,0:T(8,128)S(1)}, f32[2,64,64]{2,1,0:T(8,128)S(1)}, u32[]{:S(2)}, u32[]{:S(2)}) %collective-permute-start.1) | collective-permute-done | bytes 32800 | tf_op jit(solution)/shard_map/while/body/eval_jaxpr/ppermute | solution.py:18
  785.2 9.0 %collective-permute-done.1 = f32[2,64,64]{2,1,0:T(8,128)S(1)} collective-permute-done((f32[2,64,64]{2,1,0:T(8,128)S(1)}, f32[2,64,64]{2,1,0:T(8,128)S(1)}, u32[]{:S(2)}, u32[]{:S(2)}) %collective-permute-start.1) | collective-permute-done | bytes 32800 | tf_op jit(solution)/shard_map/while/body/eval_jaxpr/ppermute | solution.py:18
  797.8 9.0 %collective-permute-done.1 = f32[2,64,64]{2,1,0:T(8,128)S(1)} collective-permute-done((f32[2,64,64]{2,1,0:T(8,128)S(1)}, f32[2,64,64]{2,1,0:T(8,128)S(1)}, u32[]{:S(2)}, u32[]{:S(2)}) %collective-permute-start.1) | collective-permute-done | bytes 32800 | tf_op jit(solution)/shard_map/while/body/eval_jaxpr/ppermute | solution.py:18
  810.5 9.0 %collective-permute-done.1 = f32[2,64,64]{2,1,0:T(8,128)S(1)} collective-permute-done((f32[2,64,64]{2,1,0:T(8,128)S(1)}, f32[2,64,64]{2,1,0:T(8,128)S(1)}, u32[]{:S(2)}, u32[]{:S(2)}) %collective-permute-start.1) | collective-permute-done | bytes 32800 | tf_op jit(solution)/shard_map/while/body/eval_jaxpr/ppermute | solution.py:18
  823.2 9.0 %collective-permute-done.1 = f32[2,64,64]{2,1,0:T(8,128)S(1)} collective-permute-done((f32[2,64,64]{2,1,0:T(8,128)S(1)}, f32[2,64,64]{2,1,0:T(8,128)S(1)}, u32[]{:S(2)}, u32[]{:S(2)}) %collective-permute-start.1) | collective-permute-done | bytes 32800 | tf_op jit(solution)/shard_map/while/body/eval_jaxpr/ppermute | solution.py:18
  836.4 8.4 collective-permute-done.4
  844.9 5.1 while.120
  (536 shorter events, 240.1 us)
Async XLA Ops:
  7.2 542.9 %all-reduce.2.cloned.1.call-start = ((), (), s32[]{:S(2)}) async-start(), calls=%async_computation | async-start | bytes 4194304 | tf_op jit(solution)/shard_map/psum | solution.py:111
  7.2 14.6 %collective-permute-start.2 = (f32[2,64,64]{2,1,0:T(8,128)}, f32[2,64,64]{2,1,0:T(8,128)S(1)}, u32[]{:S(2)}, u32[]{:S(2)}) collective-permute-start(f32[2,64,64]{2,1,0:T(8,128)} %bitcast.593), channel_id=1, source_target_pairs={{0,1},{1,2},{2,3},{3,4},{4,5},{5,6},{6,7},{7,8},{8,9},{9,10},{10,1... | collective-permute-start | bytes 98312 | tf_op jit(solution)/shard_map/ppermute | solution.py:18
  21.8 23.5 %copy-start.1 = (f32[2,64,64]{2,1,0:T(8,128)S(1)}, f32[2,64,64]{2,1,0:T(8,128)}, u32[]{:S(2)}) copy-start(f32[2,64,64]{2,1,0:T(8,128)} %param.27) | copy-start | bytes 98308
  21.9 24.8 %copy-start.4 = (f32[2]{0:T(128)S(1)}, f32[2]{0:T(128)}, u32[]{:S(2)}) copy-start(f32[2]{0:T(128)} %constant.321) | copy-start | bytes 28
  34.3 11.0 %collective-permute-start.3 = (f32[2,64,64]{2,1,0:T(8,128)S(1)}, f32[2,64,64]{2,1,0:T(8,128)S(1)}, u32[]{:S(2)}, u32[]{:S(2)}) collective-permute-start(f32[2,64,64]{2,1,0:T(8,128)S(1)} %get-tuple-element.2622), channel_id=1, source_target_pairs={{0,1},{1,2},{2,3},{3,4},{4,5},{5,6},{6,7},{7,8},{8,9},{9,10},{10,1... | collective-permute-start | bytes 98312 | tf_op jit(solution)/shard_map/ppermute | solution.py:18
  47.4 12.9 %copy-start.5 = (f32[2]{0:T(128)S(1)}, f32[2]{0:T(128)}, u32[]{:S(2)}) copy-start(f32[2]{0:T(128)} %constant.322) | copy-start | bytes 28
  61.9 11.0 %collective-permute-start = (f32[2,64,64]{2,1,0:T(8,128)S(1)}, f32[2,64,64]{2,1,0:T(8,128)S(1)}, u32[]{:S(2)}, u32[]{:S(2)}) collective-permute-start(f32[2,64,64]{2,1,0:T(8,128)S(1)} %get-tuple-element.2638), channel_id=1, source_target_pairs={{0,1},{1,2},{2,3},{3,4},{4,5},{5,6},{6,7},{7,8},{8,9},{9,10},{10,1... | collective-permute-start | bytes 98312 | tf_op jit(solution)/shard_map/while/body/eval_jaxpr/ppermute | solution.py:18
  75.4 11.0 %collective-permute-start = (f32[2,64,64]{2,1,0:T(8,128)S(1)}, f32[2,64,64]{2,1,0:T(8,128)S(1)}, u32[]{:S(2)}, u32[]{:S(2)}) collective-permute-start(f32[2,64,64]{2,1,0:T(8,128)S(1)} %get-tuple-element.2638), channel_id=1, source_target_pairs={{0,1},{1,2},{2,3},{3,4},{4,5},{5,6},{6,7},{7,8},{8,9},{9,10},{10,1... | collective-permute-start | bytes 98312 | tf_op jit(solution)/shard_map/while/body/eval_jaxpr/ppermute | solution.py:18
  88.8 11.0 %collective-permute-start = (f32[2,64,64]{2,1,0:T(8,128)S(1)}, f32[2,64,64]{2,1,0:T(8,128)S(1)}, u32[]{:S(2)}, u32[]{:S(2)}) collective-permute-start(f32[2,64,64]{2,1,0:T(8,128)S(1)} %get-tuple-element.2638), channel_id=1, source_target_pairs={{0,1},{1,2},{2,3},{3,4},{4,5},{5,6},{6,7},{7,8},{8,9},{9,10},{10,1... | collective-permute-start | bytes 98312 | tf_op jit(solution)/shard_map/while/body/eval_jaxpr/ppermute | solution.py:18
  102.2 11.0 %collective-permute-start = (f32[2,64,64]{2,1,0:T(8,128)S(1)}, f32[2,64,64]{2,1,0:T(8,128)S(1)}, u32[]{:S(2)}, u32[]{:S(2)}) collective-permute-start(f32[2,64,64]{2,1,0:T(8,128)S(1)} %get-tuple-element.2638), channel_id=1, source_target_pairs={{0,1},{1,2},{2,3},{3,4},{4,5},{5,6},{6,7},{7,8},{8,9},{9,10},{10,1... | collective-permute-start | bytes 98312 | tf_op jit(solution)/shard_map/while/body/eval_jaxpr/ppermute | solution.py:18
  115.6 11.0 %collective-permute-start = (f32[2,64,64]{2,1,0:T(8,128)S(1)}, f32[2,64,64]{2,1,0:T(8,128)S(1)}, u32[]{:S(2)}, u32[]{:S(2)}) collective-permute-start(f32[2,64,64]{2,1,0:T(8,128)S(1)} %get-tuple-element.2638), channel_id=1, source_target_pairs={{0,1},{1,2},{2,3},{3,4},{4,5},{5,6},{6,7},{7,8},{8,9},{9,10},{10,1... | collective-permute-start | bytes 98312 | tf_op jit(solution)/shard_map/while/body/eval_jaxpr/ppermute | solution.py:18
  129.0 11.0 %collective-permute-start = (f32[2,64,64]{2,1,0:T(8,128)S(1)}, f32[2,64,64]{2,1,0:T(8,128)S(1)}, u32[]{:S(2)}, u32[]{:S(2)}) collective-permute-start(f32[2,64,64]{2,1,0:T(8,128)S(1)} %get-tuple-element.2638), channel_id=1, source_target_pairs={{0,1},{1,2},{2,3},{3,4},{4,5},{5,6},{6,7},{7,8},{8,9},{9,10},{10,1... | collective-permute-start | bytes 98312 | tf_op jit(solution)/shard_map/while/body/eval_jaxpr/ppermute | solution.py:18
  142.5 11.0 %collective-permute-start = (f32[2,64,64]{2,1,0:T(8,128)S(1)}, f32[2,64,64]{2,1,0:T(8,128)S(1)}, u32[]{:S(2)}, u32[]{:S(2)}) collective-permute-start(f32[2,64,64]{2,1,0:T(8,128)S(1)} %get-tuple-element.2638), channel_id=1, source_target_pairs={{0,1},{1,2},{2,3},{3,4},{4,5},{5,6},{6,7},{7,8},{8,9},{9,10},{10,1... | collective-permute-start | bytes 98312 | tf_op jit(solution)/shard_map/while/body/eval_jaxpr/ppermute | solution.py:18
  155.9 11.0 %collective-permute-start = (f32[2,64,64]{2,1,0:T(8,128)S(1)}, f32[2,64,64]{2,1,0:T(8,128)S(1)}, u32[]{:S(2)}, u32[]{:S(2)}) collective-permute-start(f32[2,64,64]{2,1,0:T(8,128)S(1)} %get-tuple-element.2638), channel_id=1, source_target_pairs={{0,1},{1,2},{2,3},{3,4},{4,5},{5,6},{6,7},{7,8},{8,9},{9,10},{10,1... | collective-permute-start | bytes 98312 | tf_op jit(solution)/shard_map/while/body/eval_jaxpr/ppermute | solution.py:18
  169.3 11.0 %collective-permute-start = (f32[2,64,64]{2,1,0:T(8,128)S(1)}, f32[2,64,64]{2,1,0:T(8,128)S(1)}, u32[]{:S(2)}, u32[]{:S(2)}) collective-permute-start(f32[2,64,64]{2,1,0:T(8,128)S(1)} %get-tuple-element.2638), channel_id=1, source_target_pairs={{0,1},{1,2},{2,3},{3,4},{4,5},{5,6},{6,7},{7,8},{8,9},{9,10},{10,1... | collective-permute-start | bytes 98312 | tf_op jit(solution)/shard_map/while/body/eval_jaxpr/ppermute | solution.py:18
  182.7 11.0 %collective-permute-start = (f32[2,64,64]{2,1,0:T(8,128)S(1)}, f32[2,64,64]{2,1,0:T(8,128)S(1)}, u32[]{:S(2)}, u32[]{:S(2)}) collective-permute-start(f32[2,64,64]{2,1,0:T(8,128)S(1)} %get-tuple-element.2638), channel_id=1, source_target_pairs={{0,1},{1,2},{2,3},{3,4},{4,5},{5,6},{6,7},{7,8},{8,9},{9,10},{10,1... | collective-permute-start | bytes 98312 | tf_op jit(solution)/shard_map/while/body/eval_jaxpr/ppermute | solution.py:18
  196.1 11.0 %collective-permute-start = (f32[2,64,64]{2,1,0:T(8,128)S(1)}, f32[2,64,64]{2,1,0:T(8,128)S(1)}, u32[]{:S(2)}, u32[]{:S(2)}) collective-permute-start(f32[2,64,64]{2,1,0:T(8,128)S(1)} %get-tuple-element.2638), channel_id=1, source_target_pairs={{0,1},{1,2},{2,3},{3,4},{4,5},{5,6},{6,7},{7,8},{8,9},{9,10},{10,1... | collective-permute-start | bytes 98312 | tf_op jit(solution)/shard_map/while/body/eval_jaxpr/ppermute | solution.py:18
  209.6 11.0 %collective-permute-start = (f32[2,64,64]{2,1,0:T(8,128)S(1)}, f32[2,64,64]{2,1,0:T(8,128)S(1)}, u32[]{:S(2)}, u32[]{:S(2)}) collective-permute-start(f32[2,64,64]{2,1,0:T(8,128)S(1)} %get-tuple-element.2638), channel_id=1, source_target_pairs={{0,1},{1,2},{2,3},{3,4},{4,5},{5,6},{6,7},{7,8},{8,9},{9,10},{10,1... | collective-permute-start | bytes 98312 | tf_op jit(solution)/shard_map/while/body/eval_jaxpr/ppermute | solution.py:18
  223.0 11.0 %collective-permute-start = (f32[2,64,64]{2,1,0:T(8,128)S(1)}, f32[2,64,64]{2,1,0:T(8,128)S(1)}, u32[]{:S(2)}, u32[]{:S(2)}) collective-permute-start(f32[2,64,64]{2,1,0:T(8,128)S(1)} %get-tuple-element.2638), channel_id=1, source_target_pairs={{0,1},{1,2},{2,3},{3,4},{4,5},{5,6},{6,7},{7,8},{8,9},{9,10},{10,1... | collective-permute-start | bytes 98312 | tf_op jit(solution)/shard_map/while/body/eval_jaxpr/ppermute | solution.py:18
  236.4 11.0 %collective-permute-start = (f32[2,64,64]{2,1,0:T(8,128)S(1)}, f32[2,64,64]{2,1,0:T(8,128)S(1)}, u32[]{:S(2)}, u32[]{:S(2)}) collective-permute-start(f32[2,64,64]{2,1,0:T(8,128)S(1)} %get-tuple-element.2638), channel_id=1, source_target_pairs={{0,1},{1,2},{2,3},{3,4},{4,5},{5,6},{6,7},{7,8},{8,9},{9,10},{10,1... | collective-permute-start | bytes 98312 | tf_op jit(solution)/shard_map/while/body/eval_jaxpr/ppermute | solution.py:18
  249.8 11.0 %collective-permute-start = (f32[2,64,64]{2,1,0:T(8,128)S(1)}, f32[2,64,64]{2,1,0:T(8,128)S(1)}, u32[]{:S(2)}, u32[]{:S(2)}) collective-permute-start(f32[2,64,64]{2,1,0:T(8,128)S(1)} %get-tuple-element.2638), channel_id=1, source_target_pairs={{0,1},{1,2},{2,3},{3,4},{4,5},{5,6},{6,7},{7,8},{8,9},{9,10},{10,1... | collective-permute-start | bytes 98312 | tf_op jit(solution)/shard_map/while/body/eval_jaxpr/ppermute | solution.py:18
  263.2 11.0 %collective-permute-start = (f32[2,64,64]{2,1,0:T(8,128)S(1)}, f32[2,64,64]{2,1,0:T(8,128)S(1)}, u32[]{:S(2)}, u32[]{:S(2)}) collective-permute-start(f32[2,64,64]{2,1,0:T(8,128)S(1)} %get-tuple-element.2638), channel_id=1, source_target_pairs={{0,1},{1,2},{2,3},{3,4},{4,5},{5,6},{6,7},{7,8},{8,9},{9,10},{10,1... | collective-permute-start | bytes 98312 | tf_op jit(solution)/shard_map/while/body/eval_jaxpr/ppermute | solution.py:18
  278.3 273.6 %copy-start = (f32[64,64]{1,0:T(8,128)S(1)}, f32[64,64]{1,0:T(8,128)}, u32[]{:S(2)}) copy-start(f32[64,64]{1,0:T(8,128)} %get-tuple-element.2807) | copy-start | bytes 49156
  631.1 204.6 %copy-start.2 = (f32[2,64,64]{2,1,0:T(8,128)}, f32[2,64,64]{2,1,0:T(8,128)S(1)}, u32[]{:S(2)}) copy-start(f32[2,64,64]{2,1,0:T(8,128)S(1)} %get-tuple-element.1347) | copy-start | bytes 98308
  631.2 213.7 %copy-start.3 = (f32[2]{0:T(128)S(1)}, f32[2]{0:T(128)}, u32[]{:S(2)}) copy-start(f32[2]{0:T(128)} %get-tuple-element.2847) | copy-start | bytes 28
  631.2 11.0 %collective-permute-start.1 = (f32[2,64,64]{2,1,0:T(8,128)S(1)}, f32[2,64,64]{2,1,0:T(8,128)S(1)}, u32[]{:S(2)}, u32[]{:S(2)}) collective-permute-start(f32[2,64,64]{2,1,0:T(8,128)S(1)} %get-tuple-element.2743), channel_id=1, source_target_pairs={{0,1},{1,2},{2,3},{3,4},{4,5},{5,6},{6,7},{7,8},{8,9},{9,10},{10,1... | collective-permute-start | bytes 98312 | tf_op jit(solution)/shard_map/while/body/eval_jaxpr/ppermute | solution.py:18
  643.8 11.0 %collective-permute-start.1 = (f32[2,64,64]{2,1,0:T(8,128)S(1)}, f32[2,64,64]{2,1,0:T(8,128)S(1)}, u32[]{:S(2)}, u32[]{:S(2)}) collective-permute-start(f32[2,64,64]{2,1,0:T(8,128)S(1)} %get-tuple-element.2743), channel_id=1, source_target_pairs={{0,1},{1,2},{2,3},{3,4},{4,5},{5,6},{6,7},{7,8},{8,9},{9,10},{10,1... | collective-permute-start | bytes 98312 | tf_op jit(solution)/shard_map/while/body/eval_jaxpr/ppermute | solution.py:18
  656.5 11.0 %collective-permute-start.1 = (f32[2,64,64]{2,1,0:T(8,128)S(1)}, f32[2,64,64]{2,1,0:T(8,128)S(1)}, u32[]{:S(2)}, u32[]{:S(2)}) collective-permute-start(f32[2,64,64]{2,1,0:T(8,128)S(1)} %get-tuple-element.2743), channel_id=1, source_target_pairs={{0,1},{1,2},{2,3},{3,4},{4,5},{5,6},{6,7},{7,8},{8,9},{9,10},{10,1... | collective-permute-start | bytes 98312 | tf_op jit(solution)/shard_map/while/body/eval_jaxpr/ppermute | solution.py:18
  669.2 11.0 %collective-permute-start.1 = (f32[2,64,64]{2,1,0:T(8,128)S(1)}, f32[2,64,64]{2,1,0:T(8,128)S(1)}, u32[]{:S(2)}, u32[]{:S(2)}) collective-permute-start(f32[2,64,64]{2,1,0:T(8,128)S(1)} %get-tuple-element.2743), channel_id=1, source_target_pairs={{0,1},{1,2},{2,3},{3,4},{4,5},{5,6},{6,7},{7,8},{8,9},{9,10},{10,1... | collective-permute-start | bytes 98312 | tf_op jit(solution)/shard_map/while/body/eval_jaxpr/ppermute | solution.py:18
  681.8 11.0 %collective-permute-start.1 = (f32[2,64,64]{2,1,0:T(8,128)S(1)}, f32[2,64,64]{2,1,0:T(8,128)S(1)}, u32[]{:S(2)}, u32[]{:S(2)}) collective-permute-start(f32[2,64,64]{2,1,0:T(8,128)S(1)} %get-tuple-element.2743), channel_id=1, source_target_pairs={{0,1},{1,2},{2,3},{3,4},{4,5},{5,6},{6,7},{7,8},{8,9},{9,10},{10,1... | collective-permute-start | bytes 98312 | tf_op jit(solution)/shard_map/while/body/eval_jaxpr/ppermute | solution.py:18
  694.5 11.0 %collective-permute-start.1 = (f32[2,64,64]{2,1,0:T(8,128)S(1)}, f32[2,64,64]{2,1,0:T(8,128)S(1)}, u32[]{:S(2)}, u32[]{:S(2)}) collective-permute-start(f32[2,64,64]{2,1,0:T(8,128)S(1)} %get-tuple-element.2743), channel_id=1, source_target_pairs={{0,1},{1,2},{2,3},{3,4},{4,5},{5,6},{6,7},{7,8},{8,9},{9,10},{10,1... | collective-permute-start | bytes 98312 | tf_op jit(solution)/shard_map/while/body/eval_jaxpr/ppermute | solution.py:18
  707.2 11.0 %collective-permute-start.1 = (f32[2,64,64]{2,1,0:T(8,128)S(1)}, f32[2,64,64]{2,1,0:T(8,128)S(1)}, u32[]{:S(2)}, u32[]{:S(2)}) collective-permute-start(f32[2,64,64]{2,1,0:T(8,128)S(1)} %get-tuple-element.2743), channel_id=1, source_target_pairs={{0,1},{1,2},{2,3},{3,4},{4,5},{5,6},{6,7},{7,8},{8,9},{9,10},{10,1... | collective-permute-start | bytes 98312 | tf_op jit(solution)/shard_map/while/body/eval_jaxpr/ppermute | solution.py:18
  719.8 11.0 %collective-permute-start.1 = (f32[2,64,64]{2,1,0:T(8,128)S(1)}, f32[2,64,64]{2,1,0:T(8,128)S(1)}, u32[]{:S(2)}, u32[]{:S(2)}) collective-permute-start(f32[2,64,64]{2,1,0:T(8,128)S(1)} %get-tuple-element.2743), channel_id=1, source_target_pairs={{0,1},{1,2},{2,3},{3,4},{4,5},{5,6},{6,7},{7,8},{8,9},{9,10},{10,1... | collective-permute-start | bytes 98312 | tf_op jit(solution)/shard_map/while/body/eval_jaxpr/ppermute | solution.py:18
  732.5 11.0 %collective-permute-start.1 = (f32[2,64,64]{2,1,0:T(8,128)S(1)}, f32[2,64,64]{2,1,0:T(8,128)S(1)}, u32[]{:S(2)}, u32[]{:S(2)}) collective-permute-start(f32[2,64,64]{2,1,0:T(8,128)S(1)} %get-tuple-element.2743), channel_id=1, source_target_pairs={{0,1},{1,2},{2,3},{3,4},{4,5},{5,6},{6,7},{7,8},{8,9},{9,10},{10,1... | collective-permute-start | bytes 98312 | tf_op jit(solution)/shard_map/while/body/eval_jaxpr/ppermute | solution.py:18
  745.2 11.0 %collective-permute-start.1 = (f32[2,64,64]{2,1,0:T(8,128)S(1)}, f32[2,64,64]{2,1,0:T(8,128)S(1)}, u32[]{:S(2)}, u32[]{:S(2)}) collective-permute-start(f32[2,64,64]{2,1,0:T(8,128)S(1)} %get-tuple-element.2743), channel_id=1, source_target_pairs={{0,1},{1,2},{2,3},{3,4},{4,5},{5,6},{6,7},{7,8},{8,9},{9,10},{10,1... | collective-permute-start | bytes 98312 | tf_op jit(solution)/shard_map/while/body/eval_jaxpr/ppermute | solution.py:18
  757.8 11.0 %collective-permute-start.1 = (f32[2,64,64]{2,1,0:T(8,128)S(1)}, f32[2,64,64]{2,1,0:T(8,128)S(1)}, u32[]{:S(2)}, u32[]{:S(2)}) collective-permute-start(f32[2,64,64]{2,1,0:T(8,128)S(1)} %get-tuple-element.2743), channel_id=1, source_target_pairs={{0,1},{1,2},{2,3},{3,4},{4,5},{5,6},{6,7},{7,8},{8,9},{9,10},{10,1... | collective-permute-start | bytes 98312 | tf_op jit(solution)/shard_map/while/body/eval_jaxpr/ppermute | solution.py:18
  770.5 11.0 %collective-permute-start.1 = (f32[2,64,64]{2,1,0:T(8,128)S(1)}, f32[2,64,64]{2,1,0:T(8,128)S(1)}, u32[]{:S(2)}, u32[]{:S(2)}) collective-permute-start(f32[2,64,64]{2,1,0:T(8,128)S(1)} %get-tuple-element.2743), channel_id=1, source_target_pairs={{0,1},{1,2},{2,3},{3,4},{4,5},{5,6},{6,7},{7,8},{8,9},{9,10},{10,1... | collective-permute-start | bytes 98312 | tf_op jit(solution)/shard_map/while/body/eval_jaxpr/ppermute | solution.py:18
  783.2 11.0 %collective-permute-start.1 = (f32[2,64,64]{2,1,0:T(8,128)S(1)}, f32[2,64,64]{2,1,0:T(8,128)S(1)}, u32[]{:S(2)}, u32[]{:S(2)}) collective-permute-start(f32[2,64,64]{2,1,0:T(8,128)S(1)} %get-tuple-element.2743), channel_id=1, source_target_pairs={{0,1},{1,2},{2,3},{3,4},{4,5},{5,6},{6,7},{7,8},{8,9},{9,10},{10,1... | collective-permute-start | bytes 98312 | tf_op jit(solution)/shard_map/while/body/eval_jaxpr/ppermute | solution.py:18
  795.8 11.0 %collective-permute-start.1 = (f32[2,64,64]{2,1,0:T(8,128)S(1)}, f32[2,64,64]{2,1,0:T(8,128)S(1)}, u32[]{:S(2)}, u32[]{:S(2)}) collective-permute-start(f32[2,64,64]{2,1,0:T(8,128)S(1)} %get-tuple-element.2743), channel_id=1, source_target_pairs={{0,1},{1,2},{2,3},{3,4},{4,5},{5,6},{6,7},{7,8},{8,9},{9,10},{10,1... | collective-permute-start | bytes 98312 | tf_op jit(solution)/shard_map/while/body/eval_jaxpr/ppermute | solution.py:18
  808.5 11.0 %collective-permute-start.1 = (f32[2,64,64]{2,1,0:T(8,128)S(1)}, f32[2,64,64]{2,1,0:T(8,128)S(1)}, u32[]{:S(2)}, u32[]{:S(2)}) collective-permute-start(f32[2,64,64]{2,1,0:T(8,128)S(1)} %get-tuple-element.2743), channel_id=1, source_target_pairs={{0,1},{1,2},{2,3},{3,4},{4,5},{5,6},{6,7},{7,8},{8,9},{9,10},{10,1... | collective-permute-start | bytes 98312 | tf_op jit(solution)/shard_map/while/body/eval_jaxpr/ppermute | solution.py:18
  821.2 11.0 %collective-permute-start.1 = (f32[2,64,64]{2,1,0:T(8,128)S(1)}, f32[2,64,64]{2,1,0:T(8,128)S(1)}, u32[]{:S(2)}, u32[]{:S(2)}) collective-permute-start(f32[2,64,64]{2,1,0:T(8,128)S(1)} %get-tuple-element.2743), channel_id=1, source_target_pairs={{0,1},{1,2},{2,3},{3,4},{4,5},{5,6},{6,7},{7,8},{8,9},{9,10},{10,1... | collective-permute-start | bytes 98312 | tf_op jit(solution)/shard_map/while/body/eval_jaxpr/ppermute | solution.py:18
  833.8 11.0 %collective-permute-start.4 = (f32[2,64,64]{2,1,0:T(8,128)S(1)}, f32[2,64,64]{2,1,0:T(8,128)S(1)}, u32[]{:S(2)}, u32[]{:S(2)}) collective-permute-start(f32[2,64,64]{2,1,0:T(8,128)S(1)} %get-tuple-element.1348), channel_id=1, source_target_pairs={{0,1},{1,2},{2,3},{3,4},{4,5},{5,6},{6,7},{7,8},{8,9},{9,10},{10,1... | collective-permute-start | bytes 98312 | tf_op jit(solution)/shard_map/ppermute | solution.py:18
Sparse Core Ops, SparseCore 0:
  278.4 271.5 all-reduce.1
where the time goes:
time: 862 us; the launch traced here: 858 us
  waiting for transfers between devices  587 us (68%)
  matrix products  155 us (18%)
  starting transfers between devices  67.3 us (8%)
  other arithmetic  29.1 us (3%)
  between operations  14.4 us (2%)
    ppermute x35, waiting for transfers between devices, shifted_2(): return lax.ppermute(block, axis, route)  317 us
    psum x1, waiting for transfers between devices, shards(): coarse_rhs = lax.psum(slot_terms, 'tm')  270 us
    ppermute x35, starting transfers between devices, shifted_2(): return lax.ppermute(block, axis, route)  67.2 us
    dot_general x78, matrix products, advance(): jnp.matmul(jnp.matmul(basis_rows, spectral, precision=highest), basis_col...  59.9 us
    dot_general x78, matrix products, advance(): jnp.matmul(jnp.matmul(basis_rows.T, reacted, precision=highest), basis_co...  35.8 us
    dot_general x78, matrix products, advance(): jnp.matmul(basis_rows.T, reacted, precision=highest)  30.5 us
    dot_general x78, matrix products, advance(): jnp.matmul(basis_rows, spectral, precision=highest)  28.9 us
    add x75, other arithmetic, advance(): substrate + time_step * (feed_rate * (1.0 - substrate) - uptake)  19.6 us
  transfers between devices with their start and end apart: 36, of which 36 were waited for; matrix products, arithmetic and copies ran while one was open for 1% of the time, Pallas kernels for 0%

commit v1 on v0

v1 whole, which is shorter than its diff:
```python
import functools

import jax
import jax.numpy as jnp
import ml_dtypes
import numpy as np
from jax import lax
from jax.experimental import pallas as pl
from jax.experimental.pallas import tpu as pltpu
from jax.sharding import PartitionSpec as P

GRID = 64
GROUP = 16
STEPS_DEV = 4
LANES = 2 * GRID
diffusion = (0.2, 0.1)
interval_time = 0.03125
fine_step = interval_time / STEPS_DEV
level_step = interval_time
coarse_step = interval_time * GROUP


def basis_tables():
    positions = np.arange(GRID, dtype=np.float32)
    angles = np.float32(np.pi) * (positions[:, None] + np.float32(0.5)) * positions[None] / np.float32(GRID)
    weight = np.where(positions == 0, np.sqrt(np.float32(1 / GRID)), np.sqrt(np.float32(2 / GRID)))
    cosines = np.cos(angles.astype(np.float64)).astype(np.float32)
    basis = cosines * weight[None].astype(np.float32)
    sines = np.sin((np.float32(np.pi) * positions / np.float32(2 * GRID)).astype(np.float64)).astype(np.float32)
    return basis.astype(np.float64), (np.float32(-4) * sines * sines).astype(np.float64)


def solve_terms(time_step, rate, rank):
    basis, values = basis_tables()
    inverse = 1 / (1 - time_step * rate * (values[:, None] + values[None]))
    side = inverse[:, 0] - 1
    rest = inverse - 1 - side[:, None] - side[None]
    weights, vectors = np.linalg.eigh(rest)
    order = np.argsort(-np.abs(weights))[:rank]
    first = (basis * side) @ basis.T + basis @ basis.T - np.eye(GRID)
    cross = [(basis * (vectors[:, k] * np.sqrt(np.abs(weights[k])))) @ basis.T for k in order]
    return first, cross, [np.sign(weights[k]) for k in order]


def halves(matrix):
    high = matrix.astype(np.float32).astype(ml_dtypes.bfloat16)
    low = (matrix - high.astype(np.float64)).astype(np.float32).astype(ml_dtypes.bfloat16)
    return high, low


def both(left, right):
    zero = np.zeros((GRID, GRID))
    return np.block([[left, zero], [zero, right]])


@functools.lru_cache(None)
def level_tables(time_step, rank, fine_cross):
    sub_first, sub_cross, sub_sign = solve_terms(time_step, diffusion[0], rank)
    cat_first, cat_cross, cat_sign = solve_terms(time_step, diffusion[1], rank)
    right = [both(sub_first, cat_first)] + [both(a, b) for a, b in zip(sub_cross, cat_cross)]
    high, low = zip(*[halves(m) for m in right])
    right_high = np.concatenate([np.concatenate(high, 1)] * 2, 0)
    right_low = np.concatenate(low if fine_cross else low[:1], 1)
    left_high, left_low = halves(np.concatenate([sub_first, cat_first], 0))
    left_side = np.concatenate([left_high, left_high, left_low], 1)
    stacked = [
        np.concatenate([a * p, b * q], 0) for a, b, p, q in zip(sub_cross, cat_cross, sub_sign, cat_sign)
    ]
    cross_high, cross_low = halves(np.concatenate(stacked, 1))
    tables = [right_high, right_low, left_side, cross_high]
    return tables + ([cross_low] if fine_cross else [])


def product(left, right):
    return jnp.dot(left, right, preferred_element_type=jnp.float32)


def rounded(value):
    high = value.astype(jnp.bfloat16)
    return high, (value - high.astype(jnp.float32)).astype(jnp.bfloat16)


class Level:
    def __init__(self, time_step, rank, fine_cross):
        self.time_step, self.rank, self.fine_cross = time_step, rank, fine_cross
        self.tables = level_tables(time_step, rank, fine_cross)
        self.count = len(self.tables)

    def bind(self, refs, feed, kill):
        tables = [r[...] for r in refs]
        h = jnp.float32(self.time_step)
        second = lax.broadcasted_iota(jnp.int32, (GRID, LANES), 1) >= GRID
        decay = h * jnp.where(second, feed + kill, feed)
        supply = jnp.where(second, jnp.float32(0), h * feed)
        sign = jnp.where(second, h, -h)

        def step(state):
            other = pltpu.roll(state, GRID, 1)
            uptake = state * other * jnp.where(second, state, other)
            reacted = state + (supply - decay * state + sign * uptake)
            high, low = rounded(reacted)
            right = product(jnp.concatenate([high, low], 1), tables[0])
            right_low = product(high, tables[1])
            side = product(tables[2], jnp.concatenate([high, low, high], 0))
            mixed = []
            for k in range(1, self.rank + 1):
                part = right[:, LANES * k : LANES * (k + 1)]
                if self.fine_cross:
                    part = part + right_low[:, LANES * k : LANES * (k + 1)]
                mixed.append(part)
            mixed = jnp.concatenate(mixed, 0)
            if self.fine_cross:
                mixed_high, mixed_low = rounded(mixed)
                cross = product(tables[3], mixed_high) + product(tables[3], mixed_low) + product(tables[4], mixed_high)
            else:
                cross = product(tables[3], mixed.astype(jnp.bfloat16))
            left = side + cross
            left = jnp.where(second, left[GRID:], left[:GRID])
            return reacted + (right[:, :LANES] + right_low[:, :LANES] + left)

        return step


FINE = Level(fine_step, 1, False)
MIDDLE = Level(level_step, 1, True)
COARSE = Level(coarse_step, 3, True)


def packed(pair):
    return jnp.concatenate([pair[0], pair[1]], 1)


def unpack_to(ref, state):
    ref[0] = state[:, :GRID]
    ref[1] = state[:, GRID:]


def steppers(levels, refs, feed_ref, kill_ref):
    feed, kill = packed([feed_ref[...]] * 2), packed([kill_ref[...]] * 2)
    made, start = [], 0
    for level in levels:
        made.append(level.bind(refs[start : start + level.count], feed, kill))
        start += level.count
    return made, refs[start:]


def relax_kernel(near_ref, far_ref, initial_ref, feed_ref, kill_ref, *refs):
    (fine, middle), (share_ref, residual_ref) = steppers([FINE, MIDDLE], refs, feed_ref, kill_ref)
    position = lax.axis_index("tm")
    initial = packed(initial_ref[...])
    own = jnp.where(position == 0, initial, packed(near_ref[...]))
    prior = jnp.where(position == 1, initial, packed(far_ref[...]))

    def relax(turn, states):
        return fine(states[0]), fine(states[1])

    relaxed, shifted = lax.fori_loop(0, STEPS_DEV, relax, (own, prior))
    shifted = jnp.where(position == 0, initial, shifted)
    leap = middle(shifted)
    arrived = lax.fori_loop(0, STEPS_DEV, lambda turn, state: fine(state), shifted)
    share_ref[...] = jnp.where(position % GROUP == 0, shifted, arrived - leap)
    unpack_to(residual_ref, arrived - relaxed)


def group_kernel(shares_ref, feed_ref, kill_ref, *refs):
    (fine, middle, coarse), (first_ref, rhs_ref) = steppers([FINE, MIDDLE, COARSE], refs, feed_ref, kill_ref)
    start = shares_ref[0]
    leap, handed = middle(start), coarse(start)
    state = lax.fori_loop(0, STEPS_DEV, lambda turn, state: fine(state), start)
    first_ref[...] = state - leap
    state = lax.fori_loop(1, GROUP, lambda j, state: middle(state) + shares_ref[j], state)
    leading = lax.axis_index("tm") < GROUP
    rhs_ref[...] = jnp.where(leading, state, state - handed)


def correct_kernel(rhs_ref, shares_ref, first_ref, initial_ref, feed_ref, kill_ref, *refs):
    (fine, middle, coarse), (points_ref, value_ref, defect_ref) = steppers(
        [FINE, MIDDLE, COARSE], refs, feed_ref, kill_ref
    )
    position = lax.axis_index("tm")
    member, group_id = position % GROUP, position // GROUP

    def coarse_turn(g, states):
        return states[1], coarse(states[1]) + rhs_ref[g]

    earlier, value = lax.fori_loop(1, group_id + 1, coarse_turn, (packed(initial_ref[...]), rhs_ref[0]))
    unpack_to(value_ref.at[0], value)

    def right_side(j):
        return jnp.where(j == 0, first_ref[...], shares_ref[j])

    prior = lax.fori_loop(0, member, lambda j, state: middle(state) + right_side(j), earlier)
    updated = middle(prior) + right_side(member)
    closing = member == GROUP - 1
    unpack_to(points_ref.at[STEPS_DEV - 1], jnp.where(closing, value, updated))
    unpack_to(defect_ref.at[0], jnp.where(closing, updated - value, jnp.zeros_like(value)))
    state = prior
    for i in range(STEPS_DEV - 1):
        state = fine(state)
        unpack_to(points_ref.at[i], state)


def call(kernel, shapes, levels, *operands):
    tables = [jnp.asarray(t) for level in levels for t in level.tables]
    where = pl.BlockSpec(memory_space=pltpu.VMEM)
    return pl.pallas_call(
        kernel,
        out_shape=[jax.ShapeDtypeStruct(s, jnp.float32) for s in shapes],
        in_specs=[where] * (len(operands) + len(tables)),
        out_specs=[where] * len(shapes),
        compiler_params=pltpu.CompilerParams(vmem_limit_bytes=48 * 2**20),
    )(*operands, *tables)


def shards(initial, coarse_guess, feed_rate, kill_rate):
    devices = lax.axis_size("tm")
    groups = devices // GROUP
    field = (GRID, LANES)
    pair = (2, GRID, GRID)
    own = coarse_guess[0]
    near = lax.ppermute(own, "tm", [(i, i + 1) for i in range(devices - 1)])
    far = lax.ppermute(own, "tm", [(i, i + 2) for i in range(devices - 2)])
    share, residual = call(
        relax_kernel, [field, pair], [FINE, MIDDLE], near, far, initial, feed_rate, kill_rate
    )
    inside = [[g * GROUP + m for m in range(GROUP)] for g in range(groups)]
    shares = lax.all_gather(share, "tm", axis_index_groups=inside)
    first, rhs = call(group_kernel, [field, field], [FINE, MIDDLE, COARSE], shares, feed_rate, kill_rate)
    across = [[g * GROUP + m for g in range(groups)] for m in range(GROUP)]
    rhs = lax.all_to_all(jnp.broadcast_to(rhs[None], (groups,) + field), "tm", 0, 0, axis_index_groups=across)
    points, value, defect = call(
        correct_kernel,
        [(STEPS_DEV,) + pair, (1,) + pair, (1,) + pair],
        [FINE, MIDDLE, COARSE],
        rhs,
        shares,
        first,
        initial,
        feed_rate,
        kill_rate,
    )
    return points, residual[None], value, defect


def solution(mesh):
    in_specs = (P(), P("tm", None, None, None), P(), P())
    out_specs = (P("tm", None, None, None),) * 4
    return jax.shard_map(shards, mesh=mesh, in_specs=in_specs, out_specs=out_specs, check_vma=False)
```

time: 862 us -> 110 us (0.13)
  the two profiles are of different devices: /device:TPU:32 before, /device:TPU:62 now
where the time goes in v1:
time: 110 us; the launch traced here: 109 us
  blocking collectives  51.8 us (47%)
  Pallas kernels  31.9 us (29%)
  local copies, waits for them, and re-layouts  9.89 us (9%)
  waiting for transfers between devices  8.52 us (8%)
  starting transfers between devices  6.2 us (6%)
    all_to_all x1, blocking collectives, shards(): lax.all_to_all(jnp.broadcast_to(rhs[None], (groups,) + field), 'tm', 0, 0...  34.7 us
    pallas_call x3, Pallas kernels, call(): pl.pallas_call(kernel, out_shape=[jax.ShapeDtypeStruct(s, jnp.float32) fo...  31.9 us
    all_gather x1, blocking collectives, shards(): shares = lax.all_gather(share, 'tm', axis_index_groups=inside)  17.2 us
    unnamed x52, local copies, waits for them, and re-layouts  9.78 us
    ppermute x1, waiting for transfers between devices, shards(): far = lax.ppermute(own, 'tm', [(i, i + 2) for i in range(devices - 2)])  7.44 us
    ppermute x1, starting transfers between devices, shards(): far = lax.ppermute(own, 'tm', [(i, i + 2) for i in range(devices - 2)])  4.28 us
  transfers between devices with their start and end apart: 2, of which 2 were waited for; matrix products, arithmetic and copies ran while one was open for 0% of the time, Pallas kernels for 0%

profile of v1, /device:TPU:62, one launch (start us, length us, event | category | flops | bytes accessed | tf_op | source)
XLA Modules:
  0.0 109.2 jit_solution(8524688488922025026)
XLA Ops:
  0.6 4.3 %collective-permute-start.1 = (f32[2,64,64]{2,1,0:T(8,128)}, f32[2,64,64]{2,1,0:T(8,128)S(1)}, u32[]{:S(2)}, u32[]{:S(2)}) collective-permute-start(f32[2,64,64]{2,1,0:T(8,128)} %bitcast.5), channel_id=1, source_target_pairs={{0,2},{1,3},{2,4},{3,5},{4,6},{5,7},{6,8},{7,9},{8,10},{9,11},{10,... | collective-permute-start | bytes 98312 | tf_op jit(solution)/shard_map/ppermute | solution.py:222
  4.9 1.9 %collective-permute-start = (f32[2,64,64]{2,1,0:T(8,128)}, f32[2,64,64]{2,1,0:T(8,128)S(1)}, u32[]{:S(2)}, u32[]{:S(2)}) collective-permute-start(f32[2,64,64]{2,1,0:T(8,128)} %bitcast.6), channel_id=1, source_target_pairs={{0,1},{1,2},{2,3},{3,4},{4,5},{5,6},{6,7},{7,8},{8,9},{9,10},{10,1... | collective-permute-start | bytes 98312 | tf_op jit(solution)/shard_map/ppermute | solution.py:221
  6.8 7.4 %collective-permute-done.1.far_ref = f32[2,64,64]{2,1,0:T(8,128)S(1)} collective-permute-done((f32[2,64,64]{2,1,0:T(8,128)}, f32[2,64,64]{2,1,0:T(8,128)S(1)}, u32[]{:S(2)}, u32[]{:S(2)}) %collective-permute-start.1) | collective-permute-done | bytes 32800 | tf_op jit(solution)/shard_map/ppermute | solution.py:222
  14.3 1.1 collective-permute-done.near_ref
  15.4 0.0 copy-start
  15.4 0.9 copy-done
  16.3 0.0 copy-start.2
  16.3 0.9 copy-done.2
  17.2 0.0 copy-start.5
  17.2 0.8 copy-done.5
  18.0 0.0 copy-start.7
  18.0 0.8 copy-done.7
  18.9 0.0 copy-start.9
  18.9 0.8 copy-done.9
  19.7 0.0 copy-start.11
  19.7 0.8 copy-done.11
  20.5 0.8 copy-done.13
  21.2 0.8 copy-done.15
  22.0 0.8 copy-done.17
  22.7 0.8 copy-done.19
  23.5 0.8 copy-done.20
  24.2 0.8 copy-done.24
  25.1 0.0 copy-start.18
  25.1 0.0 copy-start.21
  25.1 0.0 copy-start.22
  25.1 0.0 copy-start.23
  25.1 5.0 %shard_map.201 = (f32[64,128]{1,0:T(8,128)S(1)}, f32[2,64,64]{2,1,0:T(8,128)}) custom-call(f32[2,64,64]{2,1,0:T(8,128)S(1)} %collective-permute-done.near_ref, f32[2,64,64]{2,1,0:T(8,128)S(1)} %collective-permute-done.1.far_ref, f32[2,64,64]{2,1,0:T(8,128)S(1)} %copy-done.24, f32[64,64]{1,0:T(8,128)S(1)} %copy-done.11, f32[64,64]{1,0:T(8,128)S(1)} %copy-done.13, ...), custom_call_target="tpu_custom_call" | custom-call | tf_op jit(solution)/shard_map/pallas_call | solution.py:206
  30.2 17.2 %all-gather = f32[1024,128]{1,0:T(8,128)S(1)} all-gather(f32[64,128]{1,0:T(8,128)S(1)} %get-tuple-element.11), channel_id=2, replica_groups={{0,1,2,3,4,5,6,7,8,9,10,11,12,13,14,15},{16,17,18,19,20,21,22,23,24,25,..., dimensions={0}, use_global_device_ids=true | all-gather | bytes 557056 | tf_op jit(solution)/shard_map/all_gather | solution.py:227
  47.3 0.0 copy-done.6
  47.3 0.0 copy-done.10
  47.3 0.0 copy-done.14
  47.3 0.0 copy-done.16
  47.3 0.0 copy-done.18
  47.3 0.0 copy-done.21
  47.4 0.0 copy-done.22
  47.4 0.0 copy-done.23
  47.4 0.0 copy-done.1
  47.4 0.0 copy-done.3
  47.4 0.0 copy-done.4
  47.4 0.0 copy-done.12
  47.4 8.7 %shard_map.202 = (f32[64,128]{1,0:T(8,128)S(1)}, f32[64,128]{1,0:T(8,128)S(1)}) custom-call(f32[16,64,128]{2,1,0:T(8,128)S(1)} %bitcast.3, f32[64,64]{1,0:T(8,128)S(1)} %copy-done.12, f32[64,64]{1,0:T(8,128)S(1)} %copy-done.14, bf16[256,256]{1,0:T(8,128)(2,1)S(1)} %copy-done.3, bf16[128,128]{1,0:T(8,128)(2,1)S(1)} %copy-done.20, ...), custom_call_target="tpu_custom_call" | custom-call | tf_op jit(solution)/shard_map/pallas_call | solution.py:206
  56.1 0.1 broadcast_in_dim.4
  56.3 0.0 copy-start.8
  56.3 0.0 copy-start.25
  56.3 34.7 %all_to_all.5.rhs_ref = f32[32,64,128]{2,1,0:T(8,128)S(1)} all-to-all(f32[32,64,128]{2,1,0:T(8,128)S(1)} %broadcast_in_dim.4), channel_id=1, replica_groups={{0,16,32,48,64,80,96,112,128,144,160,176,192,208,224,240,256,272,288,30..., dimensions={0} | all-to-all | bytes 2097152 | tf_op jit(solution)/shard_map/all_to_all | solution.py:230
  91.0 0.0 copy-done.8
  91.0 0.0 copy-done.25
  91.0 18.2 %shard_map.203 = (f32[4,2,64,64]{3,2,1,0:T(8,128)}, f32[1,2,64,64]{3,2,1,0:T(8,128)}, f32[1,2,64,64]{3,2,1,0:T(8,128)}) custom-call(f32[32,64,128]{2,1,0:T(8,128)S(1)} %all_to_all.5.rhs_ref, f32[16,64,128]{2,1,0:T(8,128)S(1)} %bitcast.4, f32[64,128]{1,0:T(8,128)S(1)} %get-tuple-element.13.first_ref, f32[2,64,64]{2,1,0:T(8,128)S(1)} %copy-done.25, ...), custom_call_target="tpu_custom_call" | custom-call | tf_op jit(solution)/shard_map/pallas_call | solution.py:206
  (14 shorter events, 0.0 us)
Async XLA Ops:
  0.6 13.7 %collective-permute-start.1 = (f32[2,64,64]{2,1,0:T(8,128)}, f32[2,64,64]{2,1,0:T(8,128)S(1)}, u32[]{:S(2)}, u32[]{:S(2)}) collective-permute-start(f32[2,64,64]{2,1,0:T(8,128)} %bitcast.5), channel_id=1, source_target_pairs={{0,2},{1,3},{2,4},{3,5},{4,6},{5,7},{6,8},{7,9},{8,10},{9,11},{10,... | collective-permute-start | bytes 98312 | tf_op jit(solution)/shard_map/ppermute | solution.py:222
  4.9 10.4 %collective-permute-start = (f32[2,64,64]{2,1,0:T(8,128)}, f32[2,64,64]{2,1,0:T(8,128)S(1)}, u32[]{:S(2)}, u32[]{:S(2)}) collective-permute-start(f32[2,64,64]{2,1,0:T(8,128)} %bitcast.6), channel_id=1, source_target_pairs={{0,1},{1,2},{2,3},{3,4},{4,5},{5,6},{6,7},{7,8},{8,9},{9,10},{10,1... | collective-permute-start | bytes 98312 | tf_op jit(solution)/shard_map/ppermute | solution.py:221
  15.4 0.9 copy-start
  16.3 0.9 copy-start.2
  17.2 0.8 copy-start.5
  18.0 0.8 copy-start.7
  18.9 0.8 copy-start.9
  19.7 0.8 copy-start.11
  20.5 0.8 copy-start.13
  21.2 0.8 copy-start.15
  22.0 0.8 copy-start.17
  22.7 0.8 copy-start.19
  23.5 0.8 copy-start.20
  24.2 0.8 copy-start.24
  25.1 22.2 %copy-start.6 = (bf16[128,192]{1,0:T(8,128)(2,1)S(1)}, bf16[128,192]{1,0:T(8,128)(2,1)}, u32[]{:S(2)}) copy-start(bf16[128,192]{1,0:T(8,128)(2,1)} %constant.34.clone.refs_6_) | copy-start | bytes 147460
  25.1 22.2 %copy-start.10 = (bf16[128,512]{1,0:T(8,128)(2,1)S(1)}, bf16[128,512]{1,0:T(8,128)(2,1)}, u32[]{:S(2)}) copy-start(bf16[128,512]{1,0:T(8,128)(2,1)} %constant.38.clone.refs_10_) | copy-start | bytes 393220
  25.1 22.2 %copy-start.14 = (f32[64,64]{1,0:T(8,128)S(1)}, f32[64,64]{1,0:T(8,128)}, u32[]{:S(2)}) copy-start(f32[64,64]{1,0:T(8,128)} %kill_ref.5) | copy-start | bytes 49156
  25.1 22.2 %copy-start.16 = (bf16[128,64]{1,0:T(8,128)(2,1)S(1)}, bf16[128,64]{1,0:T(8,128)(2,1)}, u32[]{:S(2)}) copy-start(bf16[128,64]{1,0:T(8,128)(2,1)} %constant.36.clone.refs_8_) | copy-start | bytes 49156
  25.1 22.2 %copy-start.18 = (bf16[128,64]{1,0:T(8,128)(2,1)S(1)}, bf16[128,64]{1,0:T(8,128)(2,1)}, u32[]{:S(2)}) copy-start(bf16[128,64]{1,0:T(8,128)(2,1)} %constant.35.clone.refs_7_) | copy-start | bytes 49156
  25.1 22.2 %copy-start.21 = (bf16[128,192]{1,0:T(8,128)(2,1)S(1)}, bf16[128,192]{1,0:T(8,128)(2,1)}, u32[]{:S(2)}) copy-start(bf16[128,192]{1,0:T(8,128)(2,1)} %constant.41.clone.refs_13_) | copy-start | bytes 147460
  25.1 22.2 %copy-start.22 = (bf16[128,192]{1,0:T(8,128)(2,1)S(1)}, bf16[128,192]{1,0:T(8,128)(2,1)}, u32[]{:S(2)}) copy-start(bf16[128,192]{1,0:T(8,128)(2,1)} %constant.40.clone.refs_12_) | copy-start | bytes 147460
  25.1 22.2 %copy-start.23 = (bf16[128,192]{1,0:T(8,128)(2,1)S(1)}, bf16[128,192]{1,0:T(8,128)(2,1)}, u32[]{:S(2)}) copy-start(bf16[128,192]{1,0:T(8,128)(2,1)} %constant.39.clone.refs_11_) | copy-start | bytes 147460
  30.2 17.2 %copy-start.1 = (bf16[256,256]{1,0:T(8,128)(2,1)S(1)}, bf16[256,256]{1,0:T(8,128)(2,1)}, u32[]{:S(2)}) copy-start(bf16[256,256]{1,0:T(8,128)(2,1)} %constant.32.clone.refs_4_) | copy-start | bytes 393220
  30.2 17.2 %copy-start.3 = (bf16[256,256]{1,0:T(8,128)(2,1)S(1)}, bf16[256,256]{1,0:T(8,128)(2,1)}, u32[]{:S(2)}) copy-start(bf16[256,256]{1,0:T(8,128)(2,1)} %constant.28.clone.refs_0_) | copy-start | bytes 393220
  30.2 17.2 %copy-start.4 = (bf16[256,512]{1,0:T(8,128)(2,1)S(1)}, bf16[256,512]{1,0:T(8,128)(2,1)}, u32[]{:S(2)}) copy-start(bf16[256,512]{1,0:T(8,128)(2,1)} %constant.37.clone.refs_9_) | copy-start | bytes 786436
  30.2 17.2 %copy-start.12 = (f32[64,64]{1,0:T(8,128)S(1)}, f32[64,64]{1,0:T(8,128)}, u32[]{:S(2)}) copy-start(f32[64,64]{1,0:T(8,128)} %feed_ref.5) | copy-start | bytes 49156
  56.3 34.7 %copy-start.8 = (bf16[128,256]{1,0:T(8,128)(2,1)S(1)}, bf16[128,256]{1,0:T(8,128)(2,1)}, u32[]{:S(2)}) copy-start(bf16[128,256]{1,0:T(8,128)(2,1)} %constant.33.clone.refs_5_) | copy-start | bytes 196612
  56.3 34.7 %copy-start.25 = (f32[2,64,64]{2,1,0:T(8,128)S(1)}, f32[2,64,64]{2,1,0:T(8,128)}, u32[]{:S(2)}) copy-start(f32[2,64,64]{2,1,0:T(8,128)} %initial_ref.3) | copy-start | bytes 98308

commit v2 on v1

v2 whole, which is shorter than its diff:
```python
import functools

import jax
import jax.numpy as jnp
import ml_dtypes
import numpy as np
from jax import lax
from jax.experimental import pallas as pl
from jax.experimental.pallas import tpu as pltpu
from jax.sharding import PartitionSpec as P

GRID = 64
GROUP = 16
STEPS_DEV = 4
LANES = 2 * GRID
diffusion = (0.2, 0.1)
interval_time = 0.03125
fine_step = interval_time / STEPS_DEV
level_step = interval_time
coarse_step = interval_time * GROUP


def basis_tables():
    positions = np.arange(GRID, dtype=np.float32)
    angles = np.float32(np.pi) * (positions[:, None] + np.float32(0.5)) * positions[None] / np.float32(GRID)
    weight = np.where(positions == 0, np.sqrt(np.float32(1 / GRID)), np.sqrt(np.float32(2 / GRID)))
    cosines = np.cos(angles.astype(np.float64)).astype(np.float32)
    basis = cosines * weight[None].astype(np.float32)
    sines = np.sin((np.float32(np.pi) * positions / np.float32(2 * GRID)).astype(np.float64)).astype(np.float32)
    return basis.astype(np.float64), (np.float32(-4) * sines * sines).astype(np.float64)


def solve_terms(time_step, rate, rank):
    basis, values = basis_tables()
    inverse = 1 / (1 - time_step * rate * (values[:, None] + values[None]))
    side = inverse[:, 0] - 1
    rest = inverse - 1 - side[:, None] - side[None]
    weights, vectors = np.linalg.eigh(rest)
    order = np.argsort(-np.abs(weights))[:rank]
    first = (basis * side) @ basis.T + basis @ basis.T - np.eye(GRID)
    cross = [(basis * (vectors[:, k] * np.sqrt(np.abs(weights[k])))) @ basis.T for k in order]
    return first, cross, [np.sign(weights[k]) for k in order]


def halves(matrix):
    high = matrix.astype(np.float32).astype(ml_dtypes.bfloat16)
    low = (matrix - high.astype(np.float64)).astype(np.float32).astype(ml_dtypes.bfloat16)
    return high, low


def twice(matrix):
    return np.concatenate([matrix, matrix], 1)


def species_tables(time_step, rate, rank, fine_cross):
    first, cross, signs = solve_terms(time_step, rate, rank)
    high, low = halves(first)
    right = np.concatenate([twice(high), twice(high), twice(low), np.zeros_like(twice(low))], 0)
    left = [high, high, low]
    cross_high, cross_low = zip(*[halves(m) for m in cross])
    cross_high = np.concatenate([twice(m) for m in cross_high], 1)
    cross_low = np.concatenate([twice(m) for m in cross_low], 1)
    parts = [cross_high, cross_high, cross_low] if fine_cross else [cross_high, cross_low]
    blank = np.zeros((4 * GRID - GRID * len(parts), cross_high.shape[1]), ml_dtypes.bfloat16)
    mixing = np.concatenate(parts + [blank], 0)
    signed_high, signed_low = halves(np.concatenate([m * s for m, s in zip(cross, signs)], 1))
    left += [signed_high, signed_high, signed_low] if fine_cross else [signed_high]
    return right, mixing, np.concatenate(left, 1)


@functools.lru_cache(None)
def level_tables(time_step, rank, fine_cross):
    sub = species_tables(time_step, diffusion[0], rank, fine_cross)
    cat = species_tables(time_step, diffusion[1], rank, fine_cross)
    left = np.concatenate([sub[2], cat[2]], 0)
    left = np.concatenate([left, np.zeros_like(left)], 0)
    return np.concatenate([sub[0], cat[0], sub[1], cat[1], left], 1)


def product(left, right):
    return jnp.dot(left, right, preferred_element_type=jnp.float32)


def second_half():
    return lax.broadcasted_iota(jnp.int32, (GRID, LANES), 1) >= GRID


def spread(fields):
    turned = pltpu.roll(fields, GRID, 1)
    second = second_half()
    return jnp.where(second, turned, fields), jnp.where(second, fields, turned)


def merge(state):
    return jnp.where(second_half(), state[1], state[0])


def loaded(pair):
    return tuple(jnp.concatenate([pair[i], pair[i]], 1) for i in range(2))


def unpack_to(ref, state):
    ref[0] = state[0][:, :GRID]
    ref[1] = state[1][:, :GRID]


def choose(condition, one, other):
    return tuple(jnp.where(condition, a, b) for a, b in zip(one, other))


def plus(one, other):
    return tuple(a + b for a, b in zip(one, other))


def minus(one, other):
    return tuple(a - b for a, b in zip(one, other))


class Level:
    def __init__(self, time_step, rank, fine_cross):
        self.time_step, self.rank, self.fine_cross = time_step, rank, fine_cross
        self.tables = level_tables(time_step, rank, fine_cross)
        self.width = self.tables.shape[1]

    def bind(self, table, start, feed, kill):
        h = jnp.float32(self.time_step)
        rank, fine_cross = self.rank, self.fine_cross
        cross = LANES * rank
        second = second_half()
        supply, decay = h * feed, h * (feed + kill)
        right_at, cross_at = start, start + 2 * LANES
        left_at = cross_at + 2 * cross
        deep = slice(0, 4 * GRID if fine_cross else 2 * GRID)

        def solve(values):
            made = []
            for i, value in enumerate(values):
                high = value.astype(jnp.bfloat16)
                rest = value - high.astype(jnp.float32)
                mixed = jnp.where(second, rest, value).astype(jnp.bfloat16)
                wide = jnp.concatenate([mixed, high], 1)
                weights = table[deep, cross_at + cross * i : cross_at + cross * (i + 1)]
                made.append((high, rest, wide, product(wide if fine_cross else high, weights)))
            solved = []
            for i, (value, (high, rest, wide, turned)) in enumerate(zip(values, made)):
                right = product(wide, table[:, right_at + LANES * i : right_at + LANES * (i + 1)])
                turned = jnp.concatenate([turned[:, LANES * k : LANES * (k + 1)] for k in range(rank)], 0)
                turned_high = turned.astype(jnp.bfloat16)
                stack = [high, rest.astype(jnp.bfloat16), high, turned_high]
                if fine_cross:
                    stack += [(turned - turned_high.astype(jnp.float32)).astype(jnp.bfloat16), turned_high]
                stack = jnp.concatenate(stack, 0)
                left = table[GRID * i : GRID * (i + 1), left_at : left_at + stack.shape[0]]
                solved.append((right, product(left, stack)))
            return solved

        def step(state, extra=None):
            sub, cat = state
            uptake = h * (sub * cat * cat)
            values = (sub + (supply - supply * sub - uptake), cat + (uptake - decay * cat))
            sums = [a + b for a, b in solve(values)]
            if extra is not None:
                sums = [a + b for a, b in zip(sums, extra)]
            return tuple(a + b for a, b in zip(values, sums))

        return step


FINE = Level(fine_step, 1, False)
MIDDLE = Level(level_step, 1, True)
COARSE = Level(coarse_step, 3, True)
near_tables = np.concatenate([FINE.tables, MIDDLE.tables], 1)
far_tables = COARSE.tables


def fetch_kernel(near_in, far_in, initial_in, feed_in, kill_in, near_out, far_out, initial, feed, kill, sems):
    pairs = [(near_in, near_out), (far_in, far_out), (initial_in, initial), (feed_in, feed), (kill_in, kill)]
    copies = [pltpu.make_async_copy(a, b, sems.at[i]) for i, (a, b) in enumerate(pairs)]
    for copy in copies:
        copy.start()
    for copy in copies:
        copy.wait()


def relax_kernel(near_ref, far_ref, table, initial, feed, kill, share_ref, residual_ref):
    rates = [jnp.concatenate([r[...]] * 2, 1) for r in (feed, kill)]
    fine = FINE.bind(table, 0, *rates)
    middle = MIDDLE.bind(table, FINE.width, *rates)
    position = lax.axis_index("tm")
    first = loaded(initial)
    own = choose(position == 0, first, loaded(near_ref))
    prior = choose(position == 1, first, loaded(far_ref))
    for _ in range(STEPS_DEV):
        own, prior = fine(own), fine(prior)
    shifted = choose(position == 0, first, prior)
    leap = middle(shifted)
    arrived = shifted
    for _ in range(STEPS_DEV):
        arrived = fine(arrived)
    share_ref[...] = merge(choose(position % GROUP == 0, shifted, minus(arrived, leap)))
    unpack_to(residual_ref, minus(arrived, own))


def bound(near_table, far_table, feed_ref, kill_ref):
    rates = [jnp.concatenate([r[...]] * 2, 1) for r in (feed_ref, kill_ref)]
    return (
        FINE.bind(near_table, 0, *rates),
        MIDDLE.bind(near_table, FINE.width, *rates),
        COARSE.bind(far_table, 0, *rates),
    )


def chain(step, load, state, start, stop, block, keep=None):
    def turn(t, state):
        for i in range(block):
            j = start + t * block + i
            state = step(state, spread(load(j)))
            if keep is not None:
                keep[j + 1] = merge(state)
        return state

    return lax.fori_loop(0, (stop - start) // block, turn, state)


def group_kernel(shares_ref, near_table, far_table, feed_ref, kill_ref, first_ref, rhs_ref):
    fine, middle, coarse = bound(near_table, far_table, feed_ref, kill_ref)
    start = spread(shares_ref[0])
    state = start
    for _ in range(STEPS_DEV):
        state = fine(state)
    leap, handed = middle(start), coarse(start)
    first_ref[...] = merge(minus(state, leap))
    state = chain(middle, lambda j: shares_ref[j], state, 1, GROUP, 5)
    position = lax.axis_index("tm")
    rhs = merge(choose(position < GROUP, state, minus(state, handed)))
    rhs_ref[...] = jnp.where(position % 2 == 0, rhs[: GRID // 2], rhs[GRID // 2 :])


def correct_kernel(
    mine_ref, other_ref, shares_ref, first_ref, initial_ref, near_table, far_table, feed_ref, kill_ref,
    points_ref, value_ref, defect_ref, coarse_kept, middle_kept,
):
    fine, middle, coarse = bound(near_table, far_table, feed_ref, kill_ref)
    position = lax.axis_index("tm")
    member, group_id = position % GROUP, position // GROUP
    upper = position % 2 == 0

    def coarse_side(g):
        mine, other = mine_ref[g], other_ref[g]
        return jnp.concatenate([jnp.where(upper, mine, other), jnp.where(upper, other, mine)], 0)

    groups = mine_ref.shape[0]
    coarse_kept[0] = merge(loaded(initial_ref))
    coarse_kept[1] = coarse_side(0)
    state = coarse(spread(coarse_side(0)), spread(coarse_side(1)))
    coarse_kept[2] = merge(state)
    chain(coarse, coarse_side, state, 2, groups, 5, coarse_kept)
    earlier, value = spread(coarse_kept[group_id]), spread(coarse_kept[group_id + 1])
    unpack_to(value_ref.at[0], value)
    middle_kept[0] = merge(earlier)
    state = middle(earlier, spread(first_ref[...]))
    middle_kept[1] = merge(state)
    chain(middle, lambda j: shares_ref[j], state, 1, GROUP - 1, 7, middle_kept)
    prior = spread(middle_kept[member])
    side = spread(jnp.where(member == 0, first_ref[...], shares_ref[member]))
    updated = middle(prior, side)
    closing = member == GROUP - 1
    state = prior
    for i in range(STEPS_DEV - 1):
        state = fine(state)
        unpack_to(points_ref.at[i], state)
    unpack_to(points_ref.at[STEPS_DEV - 1], choose(closing, value, updated))
    unpack_to(defect_ref.at[0], choose(closing, minus(updated, value), minus(value, value)))


VMEM = pl.BlockSpec(memory_space=pltpu.VMEM)
ANY = pl.BlockSpec(memory_space=pl.ANY)


def call(kernel, outs, in_specs, scratch, limit, *operands, cost=None):
    return pl.pallas_call(
        kernel,
        out_shape=[o if isinstance(o, jax.ShapeDtypeStruct) else jax.ShapeDtypeStruct(o, jnp.float32) for o in outs],
        in_specs=in_specs,
        out_specs=[VMEM] * len(outs),
        scratch_shapes=scratch,
        cost_estimate=cost,
        compiler_params=pltpu.CompilerParams(vmem_limit_bytes=limit * 2**20),
    )(*operands)


def shards(initial, coarse_guess, feed_rate, kill_rate):
    devices = lax.axis_size("tm")
    groups = devices // GROUP
    field, pair, half, plane = (GRID, LANES), (2, GRID, GRID), (GRID // 2, LANES), (GRID, GRID)
    own = coarse_guess[0]
    near = lax.ppermute(own, "tm", [(i, i + 1) for i in range(devices - 1)])
    far = lax.ppermute(own, "tm", [(i, i + 2) for i in range(devices - 2)])
    near_table, far_table, initial, feed_rate, kill_rate = call(
        fetch_kernel,
        [jax.ShapeDtypeStruct(t.shape, jnp.bfloat16) for t in (near_tables, far_tables)] + [pair, plane, plane],
        [ANY] * 5,
        [pltpu.SemaphoreType.DMA((5,))],
        16,
        jnp.asarray(near_tables), jnp.asarray(far_tables), initial, feed_rate, kill_rate,
        cost=pl.CostEstimate(flops=0, bytes_accessed=4 * near_tables.size + 4 * far_tables.size, transcendentals=0),
    )
    share, residual = call(
        relax_kernel, [field, pair], [VMEM] * 6, [], 16, near, far, near_table, initial, feed_rate, kill_rate
    )
    inside = [[g * GROUP + m for m in range(GROUP)] for g in range(groups)]
    shares = lax.all_gather(share, "tm", axis_index_groups=inside)
    first, rhs = call(
        group_kernel, [field, half], [VMEM] * 5, [], 16, shares, near_table, far_table, feed_rate, kill_rate
    )
    across = [[g * GROUP + m for g in range(groups)] for m in range(GROUP)]
    mine = lax.all_to_all(jnp.broadcast_to(rhs[None], (groups,) + half), "tm", 0, 0, axis_index_groups=across)
    other = lax.ppermute(mine, "tm", [(i, i ^ 1) for i in range(devices)])
    points, value, defect = call(
        correct_kernel,
        [(STEPS_DEV,) + pair, (1,) + pair, (1,) + pair],
        [VMEM] * 9,
        [pltpu.VMEM((groups + 1,) + field, jnp.float32), pltpu.VMEM((GROUP,) + field, jnp.float32)],
        16,
        mine, other, shares, first, initial, near_table, far_table, feed_rate, kill_rate,
    )
    return points, residual[None], value, defect


def solution(mesh):
    in_specs = (P(), P("tm", None, None, None), P(), P())
    out_specs = (P("tm", None, None, None),) * 4
    return jax.shard_map(shards, mesh=mesh, in_specs=in_specs, out_specs=out_specs, check_vma=False)
```

time: 110 us -> 96.5 us (0.88)
  the two profiles are of different devices: /device:TPU:62 before, /device:TPU:1 now
where the time goes in v2:
time: 96.5 us; the launch traced here: 96.1 us
  blocking collectives  46.3 us (48%)
  Pallas kernels  29.3 us (30%)
  starting transfers between devices  13.5 us (14%)
  local copies, waits for them, and re-layouts  4.73 us (5%)
  waiting for transfers between devices  1.52 us (2%)
    pallas_call x4, Pallas kernels, call(): pl.pallas_call(kernel, out_shape=[o if isinstance(o, jax.ShapeDtypeStruct...  29.3 us
    all_to_all x1, blocking collectives, shards(): lax.all_to_all(jnp.broadcast_to(rhs[None], (groups,) + half), 'tm', 0, 0,...  26.2 us
    all_gather x1, blocking collectives, shards(): shares = lax.all_gather(share, 'tm', axis_index_groups=inside)  20.1 us
    ppermute x1, starting transfers between devices, shards(): near = lax.ppermute(own, 'tm', [(i, i + 1) for i in range(devices - 1)])  4.84 us
    ppermute x1, starting transfers between devices, shards(): far = lax.ppermute(own, 'tm', [(i, i + 2) for i in range(devices - 2)])  4.83 us
    unnamed x10, local copies, waits for them, and re-layouts  4.68 us
    ppermute x1, starting transfers between devices, shards(): other = lax.ppermute(mine, 'tm', [(i, i ^ 1) for i in range(devices)])  3.84 us
  transfers between devices with their start and end apart: 3, of which 1 were waited for; matrix products, arithmetic and copies ran while one was open for 0% of the time, Pallas kernels for 1%

profile of v2, /device:TPU:1, one launch (start us, length us, event | category | flops | bytes accessed | tf_op | source)
XLA Modules:
  0.0 96.1 jit_solution(17611919679589930673)
XLA Ops:
  0.6 4.8 %collective-permute-start.1 = (f32[2,64,64]{2,1,0:T(8,128)}, f32[2,64,64]{2,1,0:T(8,128)S(1)}, u32[]{:S(2)}, u32[]{:S(2)}) collective-permute-start(f32[2,64,64]{2,1,0:T(8,128)} %bitcast.5), channel_id=1, source_target_pairs={{0,2},{1,3},{2,4},{3,5},{4,6},{5,7},{6,8},{7,9},{8,10},{9,11},{10,... | collective-permute-start | bytes 98312 | tf_op jit(solution)/shard_map/ppermute | solution.py:298
  5.5 4.8 %collective-permute-start = (f32[2,64,64]{2,1,0:T(8,128)}, f32[2,64,64]{2,1,0:T(8,128)S(1)}, u32[]{:S(2)}, u32[]{:S(2)}) collective-permute-start(f32[2,64,64]{2,1,0:T(8,128)} %bitcast.6), channel_id=1, source_target_pairs={{0,1},{1,2},{2,3},{3,4},{4,5},{5,6},{6,7},{7,8},{8,9},{9,10},{10,1... | collective-permute-start | bytes 98312 | tf_op jit(solution)/shard_map/ppermute | solution.py:297
  10.3 0.0 copy-start
  10.3 1.2 %copy-done = bf16[256,1792]{1,0:T(8,128)(2,1)S(1)} copy-done((bf16[256,1792]{1,0:T(8,128)(2,1)S(1)}, bf16[256,1792]{1,0:T(8,128)(2,1)}, u32[]{:S(2)}) %copy-start) | copy-done | bytes 917528
  11.5 0.0 copy-start.1
  11.5 1.2 %copy-done.1 = bf16[256,1664]{1,0:T(8,128)(2,1)S(1)} copy-done((bf16[256,1664]{1,0:T(8,128)(2,1)S(1)}, bf16[256,1664]{1,0:T(8,128)(2,1)}, u32[]{:S(2)}) %copy-start.1) | copy-done | bytes 851992
  12.7 0.0 copy-start.2
  12.7 0.8 copy-done.2
  13.5 0.0 copy-start.3
  13.5 0.8 copy-done.3
  14.3 0.0 copy-start.4
  14.3 0.8 copy-done.4
  15.0 0.6 shard_map.93
  15.6 0.0 collective-permute-done.1.far_ref
  15.6 0.0 collective-permute-done.near_ref
  15.6 3.7 %shard_map.94 = (f32[64,128]{1,0:T(8,128)S(1)}, f32[2,64,64]{2,1,0:T(8,128)}) custom-call(f32[2,64,64]{2,1,0:T(8,128)S(1)} %collective-permute-done.near_ref, f32[2,64,64]{2,1,0:T(8,128)S(1)} %collective-permute-done.1.far_ref, bf16[256,1664]{1,0:T(8,128)(2,1)S(1)} %get-tuple-element.16.table.near_table, ...), custom_call_target="tpu_custom_call" | custom-call | tf_op jit(solution)/shard_map/pallas_call | solution.py:281
  19.3 20.1 %all-gather = f32[1024,128]{1,0:T(8,128)S(1)} all-gather(f32[64,128]{1,0:T(8,128)S(1)} %get-tuple-element.20), channel_id=2, replica_groups={{0,1,2,3,4,5,6,7,8,9,10,11,12,13,14,15},{16,17,18,19,20,21,22,23,24,25,..., dimensions={0}, use_global_device_ids=true | all-gather | bytes 557056 | tf_op jit(solution)/shard_map/all_gather | solution.py:312
  39.4 6.8 %shard_map.95 = (f32[64,128]{1,0:T(8,128)S(1)}, f32[32,128]{1,0:T(8,128)S(1)}) custom-call(f32[16,64,128]{2,1,0:T(8,128)S(1)} %bitcast.3, bf16[256,1664]{1,0:T(8,128)(2,1)S(1)} %get-tuple-element.16.table.near_table, bf16[256,1792]{1,0:T(8,128)(2,1)S(1)} %get-tuple-element.21.far_table, f32[64,64]{1,0:T(8,128)S(1)} %get-tuple-element.18.feed.feed_ref, ...), custom_call_target="tpu_custom_call" | custom-call | tf_op jit(solution)/shard_map/pallas_call | solution.py:281
  46.1 0.1 broadcast_in_dim.4
  46.2 26.2 %all_to_all.5.mine_ref = f32[32,32,128]{2,1,0:T(8,128)S(1)} all-to-all(f32[32,32,128]{2,1,0:T(8,128)S(1)} %broadcast_in_dim.4), channel_id=1, replica_groups={{0,16,32,48,64,80,96,112,128,144,160,176,192,208,224,240,256,272,288,30..., dimensions={0} | all-to-all | bytes 1048576 | tf_op jit(solution)/shard_map/all_to_all | solution.py:317
  72.4 3.8 %collective-permute-start.2 = (f32[32,32,128]{2,1,0:T(8,128)S(1)}, f32[32,32,128]{2,1,0:T(8,128)S(1)}, u32[]{:S(2)}, u32[]{:S(2)}) collective-permute-start(f32[32,32,128]{2,1,0:T(8,128)S(1)} %all_to_all.5.mine_ref), channel_id=1, source_target_pairs={{0,1},{1,0},{2,3},{3,2},{4,5},{5,4},{6,7},{7,6},{8,9},{9,8},{10,11... | collective-permute-start | bytes 1572872 | tf_op jit(solution)/shard_map/ppermute | solution.py:318
  76.2 1.5 %collective-permute-done.2.other_ref = f32[32,32,128]{2,1,0:T(8,128)S(1)} collective-permute-done((f32[32,32,128]{2,1,0:T(8,128)S(1)}, f32[32,32,128]{2,1,0:T(8,128)S(1)}, u32[]{:S(2)}, u32[]{:S(2)}) %collective-permute-start.2) | collective-permute-done | bytes 524320 | tf_op jit(solution)/shard_map/ppermute | solution.py:318
  77.8 18.3 %shard_map.96 = (f32[4,2,64,64]{3,2,1,0:T(8,128)}, f32[1,2,64,64]{3,2,1,0:T(8,128)}, f32[1,2,64,64]{3,2,1,0:T(8,128)}) custom-call(f32[32,32,128]{2,1,0:T(8,128)S(1)} %all_to_all.5.mine_ref, f32[32,32,128]{2,1,0:T(8,128)S(1)} %collective-permute-done.2.other_ref, f32[16,64,128]{2,1,0:T(8,128)S(1)} %bitcast.4, f32[64,128]{1,0:T(8,128)S(1)} %get-tuple-element.23.first_ref, ...), custom_call_target="tpu_custom_call" | custom-call | tf_op jit(solution)/shard_map/pallas_call | solution.py:281
Async XLA Ops:
  0.6 15.0 %collective-permute-start.1 = (f32[2,64,64]{2,1,0:T(8,128)}, f32[2,64,64]{2,1,0:T(8,128)S(1)}, u32[]{:S(2)}, u32[]{:S(2)}) collective-permute-start(f32[2,64,64]{2,1,0:T(8,128)} %bitcast.5), channel_id=1, source_target_pairs={{0,2},{1,3},{2,4},{3,5},{4,6},{5,7},{6,8},{7,9},{8,10},{9,11},{10,... | collective-permute-start | bytes 98312 | tf_op jit(solution)/shard_map/ppermute | solution.py:298
  5.5 10.1 %collective-permute-start = (f32[2,64,64]{2,1,0:T(8,128)}, f32[2,64,64]{2,1,0:T(8,128)S(1)}, u32[]{:S(2)}, u32[]{:S(2)}) collective-permute-start(f32[2,64,64]{2,1,0:T(8,128)} %bitcast.6), channel_id=1, source_target_pairs={{0,1},{1,2},{2,3},{3,4},{4,5},{5,6},{6,7},{7,8},{8,9},{9,10},{10,1... | collective-permute-start | bytes 98312 | tf_op jit(solution)/shard_map/ppermute | solution.py:297
  10.3 1.2 %copy-start = (bf16[256,1792]{1,0:T(8,128)(2,1)S(1)}, bf16[256,1792]{1,0:T(8,128)(2,1)}, u32[]{:S(2)}) copy-start(bf16[256,1792]{1,0:T(8,128)(2,1)} %constant.5.clone.far_in) | copy-start | bytes 2752516
  11.5 1.2 %copy-start.1 = (bf16[256,1664]{1,0:T(8,128)(2,1)S(1)}, bf16[256,1664]{1,0:T(8,128)(2,1)}, u32[]{:S(2)}) copy-start(bf16[256,1664]{1,0:T(8,128)(2,1)} %constant.4.clone.near_in) | copy-start | bytes 2555908
  12.7 0.8 copy-start.2
  13.5 0.8 copy-start.3
  14.3 0.8 copy-start.4
  72.4 5.4 %collective-permute-start.2 = (f32[32,32,128]{2,1,0:T(8,128)S(1)}, f32[32,32,128]{2,1,0:T(8,128)S(1)}, u32[]{:S(2)}, u32[]{:S(2)}) collective-permute-start(f32[32,32,128]{2,1,0:T(8,128)S(1)} %all_to_all.5.mine_ref), channel_id=1, source_target_pairs={{0,1},{1,0},{2,3},{3,2},{4,5},{5,4},{6,7},{7,6},{8,9},{9,8},{10,11... | collective-permute-start | bytes 1572872 | tf_op jit(solution)/shard_map/ppermute | solution.py:318

commit v3 on v2

--- a/solution.py
+++ b/solution.py
@@ -63,8 +63,9 @@
     parts = [cross_high, cross_high, cross_low] if fine_cross else [cross_high, cross_low]
     blank = np.zeros((4 * GRID - GRID * len(parts), cross_high.shape[1]), ml_dtypes.bfloat16)
     mixing = np.concatenate(parts + [blank], 0)
-    signed_high, signed_low = halves(np.concatenate([m * s for m, s in zip(cross, signs)], 1))
-    left += [signed_high, signed_high, signed_low] if fine_cross else [signed_high]
+    for k, (matrix, sign) in enumerate(zip(cross, signs)):
+        high, low = halves(matrix * sign)
+        left += [high, high, low] if k < fine_cross else [high]
     return right, mixing, np.concatenate(left, 1)
 
 
@@ -144,11 +145,13 @@
             solved = []
             for i, (value, (high, rest, wide, turned)) in enumerate(zip(values, made)):
                 right = product(wide, table[:, right_at + LANES * i : right_at + LANES * (i + 1)])
-                turned = jnp.concatenate([turned[:, LANES * k : LANES * (k + 1)] for k in range(rank)], 0)
-                turned_high = turned.astype(jnp.bfloat16)
-                stack = [high, rest.astype(jnp.bfloat16), high, turned_high]
-                if fine_cross:
-                    stack += [(turned - turned_high.astype(jnp.float32)).astype(jnp.bfloat16), turned_high]
+                stack = [high, rest.astype(jnp.bfloat16), high]
+                for k in range(rank):
+                    part = turned[:, LANES * k : LANES * (k + 1)]
+                    part_high = part.astype(jnp.bfloat16)
+                    stack.append(part_high)
+                    if k < fine_cross:
+                        stack += [(part - part_high.astype(jnp.float32)).astype(jnp.bfloat16), part_high]
                 stack = jnp.concatenate(stack, 0)
                 left = table[GRID * i : GRID * (i + 1), left_at : left_at + stack.shape[0]]
                 solved.append((right, product(left, stack)))
@@ -166,9 +169,9 @@
         return step
 
 
-FINE = Level(fine_step, 1, False)
-MIDDLE = Level(level_step, 1, True)
-COARSE = Level(coarse_step, 3, True)
+FINE = Level(fine_step, 1, 0)
+MIDDLE = Level(level_step, 1, 1)
+COARSE = Level(coarse_step, 3, 1)
 near_tables = np.concatenate([FINE.tables, MIDDLE.tables], 1)
 far_tables = COARSE.tables
 
@@ -222,7 +225,7 @@
     return lax.fori_loop(0, (stop - start) // block, turn, state)
 
 
-def group_kernel(shares_ref, near_table, far_table, feed_ref, kill_ref, first_ref, rhs_ref):
+def group_kernel(shares_ref, near_table, far_table, feed_ref, kill_ref, first_ref, rhs_ref, half_ref):
     fine, middle, coarse = bound(near_table, far_table, feed_ref, kill_ref)
     start = spread(shares_ref[0])
     state = start
@@ -233,29 +236,27 @@
     state = chain(middle, lambda j: shares_ref[j], state, 1, GROUP, 5)
     position = lax.axis_index("tm")
     rhs = merge(choose(position < GROUP, state, minus(state, handed)))
-    rhs_ref[...] = jnp.where(position % 2 == 0, rhs[: GRID // 2], rhs[GRID // 2 :])
+    rhs_ref[...] = rhs
+    half_ref[...] = jnp.where(position % 2 == 0, rhs[: GRID // 2], rhs[GRID // 2 :])
 
 
 def correct_kernel(
-    mine_ref, other_ref, shares_ref, first_ref, initial_ref, near_table, far_table, feed_ref, kill_ref,
+    sides_ref, rhs_ref, shares_ref, first_ref, initial_ref, near_table, far_table, feed_ref, kill_ref,
     points_ref, value_ref, defect_ref, coarse_kept, middle_kept,
 ):
     fine, middle, coarse = bound(near_table, far_table, feed_ref, kill_ref)
     position = lax.axis_index("tm")
     member, group_id = position % GROUP, position // GROUP
-    upper = position % 2 == 0
 
     def coarse_side(g):
-        mine, other = mine_ref[g], other_ref[g]
-        return jnp.concatenate([jnp.where(upper, mine, other), jnp.where(upper, other, mine)], 0)
-
-    groups = mine_ref.shape[0]
+        return jnp.concatenate([sides_ref[0, g], sides_ref[1, g]], 0)
+
     coarse_kept[0] = merge(loaded(initial_ref))
     coarse_kept[1] = coarse_side(0)
-    state = coarse(spread(coarse_side(0)), spread(coarse_side(1)))
-    coarse_kept[2] = merge(state)
-    chain(coarse, coarse_side, state, 2, groups, 5, coarse_kept)
-    earlier, value = spread(coarse_kept[group_id]), spread(coarse_kept[group_id + 1])
+    chain(coarse, coarse_side, spread(coarse_side(0)), 1, sides_ref.shape[1], 5, coarse_kept)
+    earlier = spread(coarse_kept[group_id])
+    own_side = spread(rhs_ref[...])
+    value = choose(group_id == 0, own_side, coarse(earlier, own_side))
     unpack_to(value_ref.at[0], value)
     middle_kept[0] = merge(earlier)
     state = middle(earlier, spread(first_ref[...]))
@@ -274,7 +275,7 @@
 
 
 VMEM = pl.BlockSpec(memory_space=pltpu.VMEM)
-ANY = pl.BlockSpec(memory_space=pl.ANY)
+HBM = pl.BlockSpec(memory_space=pltpu.HBM)
 
 
 def call(kernel, outs, in_specs, scratch, limit, *operands, cost=None):
@@ -299,7 +300,7 @@
     near_table, far_table, initial, feed_rate, kill_rate = call(
         fetch_kernel,
         [jax.ShapeDtypeStruct(t.shape, jnp.bfloat16) for t in (near_tables, far_tables)] + [pair, plane, plane],
-        [ANY] * 5,
+        [HBM] * 5,
         [pltpu.SemaphoreType.DMA((5,))],
         16,
         jnp.asarray(near_tables), jnp.asarray(far_tables), initial, feed_rate, kill_rate,
@@ -310,19 +311,20 @@
     )
     inside = [[g * GROUP + m for m in range(GROUP)] for g in range(groups)]
     shares = lax.all_gather(share, "tm", axis_index_groups=inside)
-    first, rhs = call(
-        group_kernel, [field, half], [VMEM] * 5, [], 16, shares, near_table, far_table, feed_rate, kill_rate
+    first, rhs, part = call(
+        group_kernel, [field, field, half], [VMEM] * 5, [], 16, shares, near_table, far_table, feed_rate, kill_rate
     )
     across = [[g * GROUP + m for g in range(groups)] for m in range(GROUP)]
-    mine = lax.all_to_all(jnp.broadcast_to(rhs[None], (groups,) + half), "tm", 0, 0, axis_index_groups=across)
-    other = lax.ppermute(mine, "tm", [(i, i ^ 1) for i in range(devices)])
+    parts = lax.all_to_all(jnp.broadcast_to(part[None], (groups,) + half), "tm", 0, 0, axis_index_groups=across)
+    cores = [[2 * c, 2 * c + 1] for c in range(devices // 2)]
+    sides = lax.all_gather(parts[: groups - 1], "tm", axis_index_groups=cores)
     points, value, defect = call(
         correct_kernel,
         [(STEPS_DEV,) + pair, (1,) + pair, (1,) + pair],
         [VMEM] * 9,
-        [pltpu.VMEM((groups + 1,) + field, jnp.float32), pltpu.VMEM((GROUP,) + field, jnp.float32)],
+        [pltpu.VMEM((groups,) + field, jnp.float32), pltpu.VMEM((GROUP,) + field, jnp.float32)],
         16,
-        mine, other, shares, first, initial, near_table, far_table, feed_rate, kill_rate,
+        sides, rhs, shares, first, initial, near_table, far_table, feed_rate, kill_rate,
     )
     return points, residual[None], value, defect
 

time: 96.5 us -> 94.8 us (0.982)
  blocking collectives: 46.3 us -> 50.4 us
  starting transfers between devices: 13.5 us -> 9.67 us
  waiting for transfers between devices: 1.52 us -> 0.01 us
    all_gather x0 -> x1, blocking collectives: none -> 4.1 us  [shards(): sides = lax.all_gather(parts[:groups - 1], 'tm', axis_index_groups=cores)]
    ppermute x1 -> x0, starting transfers between devices: 3.84 us -> none  [shards(): other = lax.ppermute(mine, 'tm', [(i, i ^ 1) for i in range(devices)])]
    ppermute x1 -> x0, waiting for transfers between devices: 1.51 us -> none  [shards(): other = lax.ppermute(mine, 'tm', [(i, i ^ 1) for i in range(devices)])]
  transfers between devices with their start and end apart: 3 -> 2, of which waited for: 1 -> 0; matrix products, arithmetic and copies ran while one was open for 0% -> 0% of each run, Pallas kernels for 1% -> 0%
where the time goes in v3:
time: 94.8 us; the launch traced here: 94.3 us
  blocking collectives  50.4 us (53%)
  Pallas kernels  28.8 us (30%)
  starting transfers between devices  9.67 us (10%)
  local copies, waits for them, and re-layouts  4.72 us (5%)
    pallas_call x4, Pallas kernels, call(): pl.pallas_call(kernel, out_shape=[o if isinstance(o, jax.ShapeDtypeStruct...  28.8 us
    all_to_all x1, blocking collectives, shards(): lax.all_to_all(jnp.broadcast_to(part[None], (groups,) + half), 'tm', 0, 0...  26.2 us
    all_gather x1, blocking collectives, shards(): shares = lax.all_gather(share, 'tm', axis_index_groups=inside)  20.1 us
    ppermute x1, starting transfers between devices, shards(): near = lax.ppermute(own, 'tm', [(i, i + 1) for i in range(devices - 1)])  4.84 us
    ppermute x1, starting transfers between devices, shards(): far = lax.ppermute(own, 'tm', [(i, i + 2) for i in range(devices - 2)])  4.83 us
    unnamed x10, local copies, waits for them, and re-layouts  4.64 us
    all_gather x1, blocking collectives, shards(): sides = lax.all_gather(parts[:groups - 1], 'tm', axis_index_groups=cores)  4.1 us
  transfers between devices with their start and end apart: 2, of which 0 were waited for; matrix products, arithmetic and copies ran while one was open for 0% of the time, Pallas kernels for 0%

profile of v3, /device:TPU:1, one launch (start us, length us, event | category | flops | bytes accessed | tf_op | source)
XLA Modules:
  0.0 94.3 jit_solution(998094094472748306)
XLA Ops:
  0.6 4.8 %collective-permute-start.1 = (f32[2,64,64]{2,1,0:T(8,128)}, f32[2,64,64]{2,1,0:T(8,128)S(1)}, u32[]{:S(2)}, u32[]{:S(2)}) collective-permute-start(f32[2,64,64]{2,1,0:T(8,128)} %bitcast.7), channel_id=1, source_target_pairs={{0,2},{1,3},{2,4},{3,5},{4,6},{5,7},{6,8},{7,9},{8,10},{9,11},{10,... | collective-permute-start | bytes 98312 | tf_op jit(solution)/shard_map/ppermute | solution.py:299
  5.5 4.8 %collective-permute-start = (f32[2,64,64]{2,1,0:T(8,128)}, f32[2,64,64]{2,1,0:T(8,128)S(1)}, u32[]{:S(2)}, u32[]{:S(2)}) collective-permute-start(f32[2,64,64]{2,1,0:T(8,128)} %bitcast.8), channel_id=1, source_target_pairs={{0,1},{1,2},{2,3},{3,4},{4,5},{5,6},{6,7},{7,8},{8,9},{9,10},{10,1... | collective-permute-start | bytes 98312 | tf_op jit(solution)/shard_map/ppermute | solution.py:298
  10.3 0.0 copy-start
  10.3 1.1 %copy-done = bf16[256,1664]{1,0:T(8,128)(2,1)S(1)} copy-done((bf16[256,1664]{1,0:T(8,128)(2,1)S(1)}, bf16[256,1664]{1,0:T(8,128)(2,1)}, u32[]{:S(2)}) %copy-start) | copy-done | bytes 851992
  11.5 0.0 copy-start.1
  11.5 1.1 %copy-done.1 = bf16[256,1536]{1,0:T(8,128)(2,1)S(1)} copy-done((bf16[256,1536]{1,0:T(8,128)(2,1)S(1)}, bf16[256,1536]{1,0:T(8,128)(2,1)}, u32[]{:S(2)}) %copy-start.1) | copy-done | bytes 786456
  12.6 0.0 copy-start.2
  12.6 0.8 copy-done.2
  13.5 0.0 copy-start.3
  13.5 0.8 copy-done.3
  14.2 0.0 copy-start.4
  14.2 0.8 copy-done.4
  15.0 0.4 shard_map.93
  15.4 0.0 collective-permute-done.1.far_ref
  15.4 0.0 collective-permute-done.near_ref
  15.4 3.7 %shard_map.94 = (f32[64,128]{1,0:T(8,128)S(1)}, f32[2,64,64]{2,1,0:T(8,128)}) custom-call(f32[2,64,64]{2,1,0:T(8,128)S(1)} %collective-permute-done.near_ref, f32[2,64,64]{2,1,0:T(8,128)S(1)} %collective-permute-done.1.far_ref, bf16[256,1664]{1,0:T(8,128)(2,1)S(1)} %get-tuple-element.17.table.near_table, ...), custom_call_target="tpu_custom_call" | custom-call | tf_op jit(solution)/shard_map/pallas_call | solution.py:282
  19.1 20.1 %all-gather = f32[1024,128]{1,0:T(8,128)S(1)} all-gather(f32[64,128]{1,0:T(8,128)S(1)} %get-tuple-element.21), channel_id=2, replica_groups={{0,1,2,3,4,5,6,7,8,9,10,11,12,13,14,15},{16,17,18,19,20,21,22,23,24,25,..., dimensions={0}, use_global_device_ids=true | all-gather | bytes 557056 | tf_op jit(solution)/shard_map/all_gather | solution.py:313
  39.2 6.8 %shard_map.95 = (f32[64,128]{1,0:T(8,128)S(1)}, f32[64,128]{1,0:T(8,128)S(1)}, f32[32,128]{1,0:T(8,128)S(1)}) custom-call(f32[16,64,128]{2,1,0:T(8,128)S(1)} %bitcast.4, bf16[256,1664]{1,0:T(8,128)(2,1)S(1)} %get-tuple-element.17.table.near_table, bf16[256,1536]{1,0:T(8,128)(2,1)S(1)} %get-tuple-element.22.far_table, ...), custom_call_target="tpu_custom_call" | custom-call | tf_op jit(solution)/shard_map/pallas_call | solution.py:282
  45.9 0.1 broadcast_in_dim.4
  46.0 26.2 %all_to_all.5 = f32[32,32,128]{2,1,0:T(8,128)S(1)} all-to-all(f32[32,32,128]{2,1,0:T(8,128)S(1)} %broadcast_in_dim.4), channel_id=1, replica_groups={{0,16,32,48,64,80,96,112,128,144,160,176,192,208,224,240,256,272,288,30..., dimensions={0} | all-to-all | bytes 1048576 | tf_op jit(solution)/shard_map/all_to_all | solution.py:318
  72.2 4.1 %all-gather.1 = f32[62,32,128]{2,1,0:T(8,128)S(1)} all-gather(f32[31,32,128]{2,1,0:T(8,128)S(1)} %slice.4), channel_id=3, replica_groups={{0,1},{2,3},{4,5},{6,7},{8,9},{10,11},{12,13},{14,15},{16,17},{18,19},{..., dimensions={0}, use_global_device_ids=true | all-gather | bytes 1523712 | tf_op jit(solution)/shard_map/all_gather | solution.py:320
  76.3 18.0 %shard_map.96 = (f32[4,2,64,64]{3,2,1,0:T(8,128)}, f32[1,2,64,64]{3,2,1,0:T(8,128)}, f32[1,2,64,64]{3,2,1,0:T(8,128)}) custom-call(f32[2,31,32,128]{3,2,1,0:T(8,128)S(1)} %bitcast.6, f32[64,128]{1,0:T(8,128)S(1)} %get-tuple-element.24.rhs_ref, f32[16,64,128]{2,1,0:T(8,128)S(1)} %bitcast.5, f32[64,128]{1,0:T(8,128)S(1)} %get-tuple-element.25.first_ref, ...), custom_call_target="tpu_custom_call" | custom-call | tf_op jit(solution)/shard_map/pallas_call | solution.py:282
  (1 shorter events, 0.0 us)
Async XLA Ops:
  0.6 14.8 %collective-permute-start.1 = (f32[2,64,64]{2,1,0:T(8,128)}, f32[2,64,64]{2,1,0:T(8,128)S(1)}, u32[]{:S(2)}, u32[]{:S(2)}) collective-permute-start(f32[2,64,64]{2,1,0:T(8,128)} %bitcast.7), channel_id=1, source_target_pairs={{0,2},{1,3},{2,4},{3,5},{4,6},{5,7},{6,8},{7,9},{8,10},{9,11},{10,... | collective-permute-start | bytes 98312 | tf_op jit(solution)/shard_map/ppermute | solution.py:299
  5.5 9.9 %collective-permute-start = (f32[2,64,64]{2,1,0:T(8,128)}, f32[2,64,64]{2,1,0:T(8,128)S(1)}, u32[]{:S(2)}, u32[]{:S(2)}) collective-permute-start(f32[2,64,64]{2,1,0:T(8,128)} %bitcast.8), channel_id=1, source_target_pairs={{0,1},{1,2},{2,3},{3,4},{4,5},{5,6},{6,7},{7,8},{8,9},{9,10},{10,1... | collective-permute-start | bytes 98312 | tf_op jit(solution)/shard_map/ppermute | solution.py:298
  10.3 1.2 %copy-start = (bf16[256,1664]{1,0:T(8,128)(2,1)S(1)}, bf16[256,1664]{1,0:T(8,128)(2,1)}, u32[]{:S(2)}) copy-start(bf16[256,1664]{1,0:T(8,128)(2,1)} %constant.4.clone.near_in) | copy-start | bytes 2555908
  11.5 1.1 %copy-start.1 = (bf16[256,1536]{1,0:T(8,128)(2,1)S(1)}, bf16[256,1536]{1,0:T(8,128)(2,1)}, u32[]{:S(2)}) copy-start(bf16[256,1536]{1,0:T(8,128)(2,1)} %constant.5.clone.far_in) | copy-start | bytes 2359300
  12.6 0.8 copy-start.2
  13.5 0.8 copy-start.3
  14.2 0.8 copy-start.4

commit v4 on v3

--- a/solution.py
+++ b/solution.py
@@ -173,24 +173,18 @@
 MIDDLE = Level(level_step, 1, 1)
 COARSE = Level(coarse_step, 3, 1)
 near_tables = np.concatenate([FINE.tables, MIDDLE.tables], 1)
-far_tables = COARSE.tables
-
-
-def fetch_kernel(near_in, far_in, initial_in, feed_in, kill_in, near_out, far_out, initial, feed, kill, sems):
-    pairs = [(near_in, near_out), (far_in, far_out), (initial_in, initial), (feed_in, feed), (kill_in, kill)]
-    copies = [pltpu.make_async_copy(a, b, sems.at[i]) for i, (a, b) in enumerate(pairs)]
-    for copy in copies:
-        copy.start()
-    for copy in copies:
-        copy.wait()
-
-
-def relax_kernel(near_ref, far_ref, table, initial, feed, kill, share_ref, residual_ref):
-    rates = [jnp.concatenate([r[...]] * 2, 1) for r in (feed, kill)]
-    fine = FINE.bind(table, 0, *rates)
-    middle = MIDDLE.bind(table, FINE.width, *rates)
+
+
+def bound(fields, near_table, far_table=None):
+    rates = loaded(fields.at[2:])
+    fine, middle = FINE.bind(near_table, 0, *rates), MIDDLE.bind(near_table, FINE.width, *rates)
+    return fine, middle, None if far_table is None else COARSE.bind(far_table, 0, *rates)
+
+
+def relax_kernel(near_ref, far_ref, fields, near_table, share_ref, residual_ref):
+    fine, middle, _ = bound(fields, near_table)
     position = lax.axis_index("tm")
-    first = loaded(initial)
+    first = loaded(fields)
     own = choose(position == 0, first, loaded(near_ref))
     prior = choose(position == 1, first, loaded(far_ref))
     for _ in range(STEPS_DEV):
@@ -204,15 +198,6 @@
     unpack_to(residual_ref, minus(arrived, own))
 
 
-def bound(near_table, far_table, feed_ref, kill_ref):
-    rates = [jnp.concatenate([r[...]] * 2, 1) for r in (feed_ref, kill_ref)]
-    return (
-        FINE.bind(near_table, 0, *rates),
-        MIDDLE.bind(near_table, FINE.width, *rates),
-        COARSE.bind(far_table, 0, *rates),
-    )
-
-
 def chain(step, load, state, start, stop, block, keep=None):
     def turn(t, state):
         for i in range(block):
@@ -225,8 +210,8 @@
     return lax.fori_loop(0, (stop - start) // block, turn, state)
 
 
-def group_kernel(shares_ref, near_table, far_table, feed_ref, kill_ref, first_ref, rhs_ref, half_ref):
-    fine, middle, coarse = bound(near_table, far_table, feed_ref, kill_ref)
+def group_kernel(shares_ref, fields, near_table, far_table, first_ref, rhs_ref, half_ref):
+    fine, middle, coarse = bound(fields, near_table, far_table)
     start = spread(shares_ref[0])
     state = start
     for _ in range(STEPS_DEV):
@@ -241,17 +226,17 @@
 
 
 def correct_kernel(
-    sides_ref, rhs_ref, shares_ref, first_ref, initial_ref, near_table, far_table, feed_ref, kill_ref,
+    sides_ref, rhs_ref, shares_ref, first_ref, fields, near_table, far_table,
     points_ref, value_ref, defect_ref, coarse_kept, middle_kept,
 ):
-    fine, middle, coarse = bound(near_table, far_table, feed_ref, kill_ref)
+    fine, middle, coarse = bound(fields, near_table, far_table)
     position = lax.axis_index("tm")
     member, group_id = position % GROUP, position // GROUP
 
     def coarse_side(g):
         return jnp.concatenate([sides_ref[0, g], sides_ref[1, g]], 0)
 
-    coarse_kept[0] = merge(loaded(initial_ref))
+    coarse_kept[0] = merge(loaded(fields))
     coarse_kept[1] = coarse_side(0)
     chain(coarse, coarse_side, spread(coarse_side(0)), 1, sides_ref.shape[1], 5, coarse_kept)
     earlier = spread(coarse_kept[group_id])
@@ -275,17 +260,15 @@
 
 
 VMEM = pl.BlockSpec(memory_space=pltpu.VMEM)
-HBM = pl.BlockSpec(memory_space=pltpu.HBM)
-
-
-def call(kernel, outs, in_specs, scratch, limit, *operands, cost=None):
+
+
+def call(kernel, outs, in_specs, scratch, limit, *operands):
     return pl.pallas_call(
         kernel,
-        out_shape=[o if isinstance(o, jax.ShapeDtypeStruct) else jax.ShapeDtypeStruct(o, jnp.float32) for o in outs],
+        out_shape=[jax.ShapeDtypeStruct(o, jnp.float32) for o in outs],
         in_specs=in_specs,
         out_specs=[VMEM] * len(outs),
         scratch_shapes=scratch,
-        cost_estimate=cost,
         compiler_params=pltpu.CompilerParams(vmem_limit_bytes=limit * 2**20),
     )(*operands)
 
@@ -293,26 +276,17 @@
 def shards(initial, coarse_guess, feed_rate, kill_rate):
     devices = lax.axis_size("tm")
     groups = devices // GROUP
-    field, pair, half, plane = (GRID, LANES), (2, GRID, GRID), (GRID // 2, LANES), (GRID, GRID)
+    field, pair, half = (GRID, LANES), (2, GRID, GRID), (GRID // 2, LANES)
     own = coarse_guess[0]
     near = lax.ppermute(own, "tm", [(i, i + 1) for i in range(devices - 1)])
     far = lax.ppermute(own, "tm", [(i, i + 2) for i in range(devices - 2)])
-    near_table, far_table, initial, feed_rate, kill_rate = call(
-        fetch_kernel,
-        [jax.ShapeDtypeStruct(t.shape, jnp.bfloat16) for t in (near_tables, far_tables)] + [pair, plane, plane],
-        [HBM] * 5,
-        [pltpu.SemaphoreType.DMA((5,))],
-        16,
-        jnp.asarray(near_tables), jnp.asarray(far_tables), initial, feed_rate, kill_rate,
-        cost=pl.CostEstimate(flops=0, bytes_accessed=4 * near_tables.size + 4 * far_tables.size, transcendentals=0),
-    )
-    share, residual = call(
-        relax_kernel, [field, pair], [VMEM] * 6, [], 16, near, far, near_table, initial, feed_rate, kill_rate
-    )
+    near_table, far_table = jnp.asarray(near_tables), jnp.asarray(COARSE.tables)
+    fields = jnp.concatenate([initial, feed_rate[None], kill_rate[None]], 0)
+    share, residual = call(relax_kernel, [field, pair], [VMEM] * 4, [], 16, near, far, fields, near_table)
     inside = [[g * GROUP + m for m in range(GROUP)] for g in range(groups)]
     shares = lax.all_gather(share, "tm", axis_index_groups=inside)
     first, rhs, part = call(
-        group_kernel, [field, field, half], [VMEM] * 5, [], 16, shares, near_table, far_table, feed_rate, kill_rate
+        group_kernel, [field, field, half], [VMEM] * 4, [], 16, shares, fields, near_table, far_table
     )
     across = [[g * GROUP + m for g in range(groups)] for m in range(GROUP)]
     parts = lax.all_to_all(jnp.broadcast_to(part[None], (groups,) + half), "tm", 0, 0, axis_index_groups=across)
@@ -321,10 +295,10 @@
     points, value, defect = call(
         correct_kernel,
         [(STEPS_DEV,) + pair, (1,) + pair, (1,) + pair],
-        [VMEM] * 9,
+        [VMEM] * 7,
         [pltpu.VMEM((groups,) + field, jnp.float32), pltpu.VMEM((GROUP,) + field, jnp.float32)],
         16,
-        sides, rhs, shares, first, initial, near_table, far_table, feed_rate, kill_rate,
+        sides, rhs, shares, first, fields, near_table, far_table,
     )
     return points, residual[None], value, defect
 

time: 94.8 us -> 94.5 us (level)
  local copies, waits for them, and re-layouts: 4.72 us -> 1.25 us
  blocking collectives: 50.4 us -> 52.6 us
    unnamed x10 -> x6, local copies, waits for them, and re-layouts: 4.64 us -> 1.16 us
    all_gather x1, blocking collectives: 20.1 us -> 22.3 us  [shards(): shares = lax.all_gather(share, 'tm', axis_index_groups=inside)]
    pallas_call x4 -> x3, Pallas kernels: 28.8 us -> 28.4 us  [call(): pl.pallas_call(kernel, out_shape=[jax.ShapeDtypeStruct(o, jnp.float32) fo...]
  transfers between devices with their start and end apart: 2 -> 2, of which waited for: 0 -> 1; matrix products, arithmetic and copies ran while one was open for 0% -> 1% of each run, Pallas kernels for 0% -> 0%
where the time goes in v4:
time: 94.5 us; the launch traced here: 94.3 us
  blocking collectives  52.6 us (56%)
  Pallas kernels  28.4 us (30%)
  starting transfers between devices  9.67 us (10%)
  local copies, waits for them, and re-layouts  1.25 us (1%)
    pallas_call x3, Pallas kernels, call(): pl.pallas_call(kernel, out_shape=[jax.ShapeDtypeStruct(o, jnp.float32) fo...  28.4 us
    all_to_all x1, blocking collectives, shards(): lax.all_to_all(jnp.broadcast_to(part[None], (groups,) + half), 'tm', 0, 0...  26.2 us
    all_gather x1, blocking collectives, shards(): shares = lax.all_gather(share, 'tm', axis_index_groups=inside)  22.3 us
    ppermute x1, starting transfers between devices, shards(): near = lax.ppermute(own, 'tm', [(i, i + 1) for i in range(devices - 1)])  4.84 us
    ppermute x1, starting transfers between devices, shards(): far = lax.ppermute(own, 'tm', [(i, i + 2) for i in range(devices - 2)])  4.83 us
    all_gather x1, blocking collectives, shards(): sides = lax.all_gather(parts[:groups - 1], 'tm', axis_index_groups=cores)  4.1 us
  transfers between devices with their start and end apart: 2, of which 1 were waited for; matrix products, arithmetic and copies ran while one was open for 1% of the time, Pallas kernels for 0%

profile of v4, /device:TPU:1, one launch (start us, length us, event | category | flops | bytes accessed | tf_op | source)
XLA Modules:
  0.0 94.3 jit_solution(17045933370104860272)
XLA Ops:
  0.6 4.8 %collective-permute-start.1 = (f32[2,64,64]{2,1,0:T(8,128)}, f32[2,64,64]{2,1,0:T(8,128)S(1)}, u32[]{:S(2)}, u32[]{:S(2)}) collective-permute-start(f32[2,64,64]{2,1,0:T(8,128)} %bitcast.11), channel_id=1, source_target_pairs={{0,2},{1,3},{2,4},{3,5},{4,6},{5,7},{6,8},{7,9},{8,10},{9,11},{10,... | collective-permute-start | bytes 98312 | tf_op jit(solution)/shard_map/ppermute | solution.py:282
  5.5 4.8 %collective-permute-start = (f32[2,64,64]{2,1,0:T(8,128)}, f32[2,64,64]{2,1,0:T(8,128)S(1)}, u32[]{:S(2)}, u32[]{:S(2)}) collective-permute-start(f32[2,64,64]{2,1,0:T(8,128)} %bitcast.12), channel_id=1, source_target_pairs={{0,1},{1,2},{2,3},{3,4},{4,5},{5,6},{6,7},{7,8},{8,9},{9,10},{10,1... | collective-permute-start | bytes 98312 | tf_op jit(solution)/shard_map/ppermute | solution.py:281
  10.3 0.9 pad_maximum_fusion.fields
  11.2 0.0 collective-permute-done.1.far_ref
  11.2 0.7 collective-permute-done.near_ref
  11.9 0.0 copy-start
  11.9 1.2 %copy-done = bf16[256,1664]{1,0:T(8,128)(2,1)S(1)} copy-done((bf16[256,1664]{1,0:T(8,128)(2,1)S(1)}, bf16[256,1664]{1,0:T(8,128)(2,1)}, u32[]{:S(2)}) %copy-start) | copy-done | bytes 851992
  13.1 0.0 copy-start.1
  13.1 0.0 copy-start.2
  13.1 3.7 %shard_map.93 = (f32[64,128]{1,0:T(8,128)S(1)}, f32[2,64,64]{2,1,0:T(8,128)}) custom-call(f32[2,64,64]{2,1,0:T(8,128)S(1)} %collective-permute-done.near_ref, f32[2,64,64]{2,1,0:T(8,128)S(1)} %collective-permute-done.1.far_ref, f32[4,64,64]{2,1,0:T(8,128)S(1)} %pad_maximum_fusion.fields, bf16[256,1664]{1,0:T(8,128)(2,1)S(1)} %copy-done), custom_call_target="tpu_custom_call" | custom-call | tf_op jit(solution)/shard_map/pallas_call | solution.py:266
  16.8 22.3 %all-gather = f32[1024,128]{1,0:T(8,128)S(1)} all-gather(f32[64,128]{1,0:T(8,128)S(1)} %get-tuple-element.12), channel_id=2, replica_groups={{0,1,2,3,4,5,6,7,8,9,10,11,12,13,14,15},{16,17,18,19,20,21,22,23,24,25,..., dimensions={0}, use_global_device_ids=true | all-gather | bytes 557056 | tf_op jit(solution)/shard_map/all_gather | solution.py:287
  39.1 0.0 copy-done.1
  39.1 0.0 copy-done.2
  39.1 6.8 %shard_map.94 = (f32[64,128]{1,0:T(8,128)S(1)}, f32[64,128]{1,0:T(8,128)S(1)}, f32[32,128]{1,0:T(8,128)S(1)}) custom-call(f32[16,64,128]{2,1,0:T(8,128)S(1)} %bitcast.6, f32[4,64,64]{2,1,0:T(8,128)S(1)} %pad_maximum_fusion.fields, bf16[256,1664]{1,0:T(8,128)(2,1)S(1)} %copy-done.1, bf16[256,1536]{1,0:T(8,128)(2,1)S(1)} %copy-done.2), custom_call_target="tpu_custom_call" | custom-call | tf_op jit(solution)/shard_map/pallas_call | solution.py:266
  45.9 0.1 broadcast_in_dim.17
  45.9 26.2 %all_to_all.5 = f32[32,32,128]{2,1,0:T(8,128)S(1)} all-to-all(f32[32,32,128]{2,1,0:T(8,128)S(1)} %broadcast_in_dim.17), channel_id=1, replica_groups={{0,16,32,48,64,80,96,112,128,144,160,176,192,208,224,240,256,272,288,30..., dimensions={0} | all-to-all | bytes 1048576 | tf_op jit(solution)/shard_map/all_to_all | solution.py:292
  72.2 4.1 %all-gather.1 = f32[62,32,128]{2,1,0:T(8,128)S(1)} all-gather(f32[31,32,128]{2,1,0:T(8,128)S(1)} %slice.4), channel_id=3, replica_groups={{0,1},{2,3},{4,5},{6,7},{8,9},{10,11},{12,13},{14,15},{16,17},{18,19},{..., dimensions={0}, use_global_device_ids=true | all-gather | bytes 1523712 | tf_op jit(solution)/shard_map/all_gather | solution.py:294
  76.3 18.0 %shard_map.95 = (f32[4,2,64,64]{3,2,1,0:T(8,128)}, f32[1,2,64,64]{3,2,1,0:T(8,128)}, f32[1,2,64,64]{3,2,1,0:T(8,128)}) custom-call(f32[2,31,32,128]{3,2,1,0:T(8,128)S(1)} %bitcast.8, f32[64,128]{1,0:T(8,128)S(1)} %get-tuple-element.14.rhs_ref, f32[16,64,128]{2,1,0:T(8,128)S(1)} %bitcast.7, f32[64,128]{1,0:T(8,128)S(1)} %get-tuple-element.15.first_ref, ...), custom_call_target="tpu_custom_call" | custom-call | tf_op jit(solution)/shard_map/pallas_call | solution.py:266
  (1 shorter events, 0.0 us)
Async XLA Ops:
  0.6 10.6 %collective-permute-start.1 = (f32[2,64,64]{2,1,0:T(8,128)}, f32[2,64,64]{2,1,0:T(8,128)S(1)}, u32[]{:S(2)}, u32[]{:S(2)}) collective-permute-start(f32[2,64,64]{2,1,0:T(8,128)} %bitcast.11), channel_id=1, source_target_pairs={{0,2},{1,3},{2,4},{3,5},{4,6},{5,7},{6,8},{7,9},{8,10},{9,11},{10,... | collective-permute-start | bytes 98312 | tf_op jit(solution)/shard_map/ppermute | solution.py:282
  5.5 6.5 %collective-permute-start = (f32[2,64,64]{2,1,0:T(8,128)}, f32[2,64,64]{2,1,0:T(8,128)S(1)}, u32[]{:S(2)}, u32[]{:S(2)}) collective-permute-start(f32[2,64,64]{2,1,0:T(8,128)} %bitcast.12), channel_id=1, source_target_pairs={{0,1},{1,2},{2,3},{3,4},{4,5},{5,6},{6,7},{7,8},{8,9},{9,10},{10,1... | collective-permute-start | bytes 98312 | tf_op jit(solution)/shard_map/ppermute | solution.py:281
  11.9 1.2 %copy-start = (bf16[256,1664]{1,0:T(8,128)(2,1)S(1)}, bf16[256,1664]{1,0:T(8,128)(2,1)}, u32[]{:S(2)}) copy-start(bf16[256,1664]{1,0:T(8,128)(2,1)} %constant.4.clone.near_table) | copy-start | bytes 2555908
  13.1 26.0 %copy-start.1 = (bf16[256,1664]{1,0:T(8,128)(2,1)S(1)}, bf16[256,1664]{1,0:T(8,128)(2,1)}, u32[]{:S(2)}) copy-start(bf16[256,1664]{1,0:T(8,128)(2,1)} %constant.4.clone.near_table) | copy-start | bytes 2555908
  13.1 26.0 %copy-start.2 = (bf16[256,1536]{1,0:T(8,128)(2,1)S(1)}, bf16[256,1536]{1,0:T(8,128)(2,1)}, u32[]{:S(2)}) copy-start(bf16[256,1536]{1,0:T(8,128)(2,1)} %constant.5.clone.far_table) | copy-start | bytes 2359300

commit v5 on v4

--- a/solution.py
+++ b/solution.py
@@ -181,21 +181,24 @@
     return fine, middle, None if far_table is None else COARSE.bind(far_table, 0, *rates)
 
 
-def relax_kernel(near_ref, far_ref, fields, near_table, share_ref, residual_ref):
+def fetch_kernel(source, target):
+    target[...] = source[...]
+
+
+def relax_kernel(far_ref, fields, near_table, share_ref, arrived_ref):
     fine, middle, _ = bound(fields, near_table)
     position = lax.axis_index("tm")
     first = loaded(fields)
-    own = choose(position == 0, first, loaded(near_ref))
     prior = choose(position == 1, first, loaded(far_ref))
     for _ in range(STEPS_DEV):
-        own, prior = fine(own), fine(prior)
+        prior = fine(prior)
     shifted = choose(position == 0, first, prior)
     leap = middle(shifted)
     arrived = shifted
     for _ in range(STEPS_DEV):
         arrived = fine(arrived)
     share_ref[...] = merge(choose(position % GROUP == 0, shifted, minus(arrived, leap)))
-    unpack_to(residual_ref, minus(arrived, own))
+    arrived_ref[...] = merge(arrived)
 
 
 def chain(step, load, state, start, stop, block, keep=None):
@@ -210,16 +213,20 @@
     return lax.fori_loop(0, (stop - start) // block, turn, state)
 
 
-def group_kernel(shares_ref, fields, near_table, far_table, first_ref, rhs_ref, half_ref):
+def group_kernel(
+    shares_ref, near_ref, arrived_ref, fields, near_table, far_table, first_ref, rhs_ref, half_ref, residual_ref
+):
     fine, middle, coarse = bound(fields, near_table, far_table)
+    position = lax.axis_index("tm")
+    own = choose(position == 0, loaded(fields), loaded(near_ref))
     start = spread(shares_ref[0])
     state = start
     for _ in range(STEPS_DEV):
-        state = fine(state)
+        state, own = fine(state), fine(own)
+    unpack_to(residual_ref, minus(spread(arrived_ref[...]), own))
     leap, handed = middle(start), coarse(start)
     first_ref[...] = merge(minus(state, leap))
     state = chain(middle, lambda j: shares_ref[j], state, 1, GROUP, 5)
-    position = lax.axis_index("tm")
     rhs = merge(choose(position < GROUP, state, minus(state, handed)))
     rhs_ref[...] = rhs
     half_ref[...] = jnp.where(position % 2 == 0, rhs[: GRID // 2], rhs[GRID // 2 :])
@@ -278,15 +285,29 @@
     groups = devices // GROUP
     field, pair, half = (GRID, LANES), (2, GRID, GRID), (GRID // 2, LANES)
     own = coarse_guess[0]
+    far = lax.ppermute(own, "tm", [(i, i + 2) for i in range(devices - 2)])
+    far_table = jnp.asarray(COARSE.tables)
+    fields = jnp.concatenate([initial, feed_rate[None], kill_rate[None]], 0)
+    near_table = pl.pallas_call(
+        fetch_kernel,
+        out_shape=jax.ShapeDtypeStruct(near_tables.shape, jnp.bfloat16),
+        in_specs=[VMEM],
+        out_specs=VMEM,
+        cost_estimate=pl.CostEstimate(flops=0, bytes_accessed=4 * near_tables.size, transcendentals=0),
+        compiler_params=pltpu.CompilerParams(vmem_limit_bytes=16 * 2**20),
+    )(jnp.asarray(near_tables))
+    share, arrived = call(relax_kernel, [field, field], [VMEM] * 3, [], 16, far, fields, near_table)
+    share, own = lax.optimization_barrier((share, own))
     near = lax.ppermute(own, "tm", [(i, i + 1) for i in range(devices - 1)])
-    far = lax.ppermute(own, "tm", [(i, i + 2) for i in range(devices - 2)])
-    near_table, far_table = jnp.asarray(near_tables), jnp.asarray(COARSE.tables)
-    fields = jnp.concatenate([initial, feed_rate[None], kill_rate[None]], 0)
-    share, residual = call(relax_kernel, [field, pair], [VMEM] * 4, [], 16, near, far, fields, near_table)
     inside = [[g * GROUP + m for m in range(GROUP)] for g in range(groups)]
     shares = lax.all_gather(share, "tm", axis_index_groups=inside)
-    first, rhs, part = call(
-        group_kernel, [field, field, half], [VMEM] * 4, [], 16, shares, fields, near_table, far_table
+    first, rhs, part, residual = call(
+        group_kernel,
+        [field, field, half, pair],
+        [VMEM] * 6,
+        [],
+        16,
+        shares, near, arrived, fields, near_table, far_table,
     )
     across = [[g * GROUP + m for g in range(groups)] for m in range(GROUP)]
     parts = lax.all_to_all(jnp.broadcast_to(part[None], (groups,) + half), "tm", 0, 0, axis_index_groups=across)

time: 94.5 us -> 94.1 us (level)
  starting transfers between devices: 9.67 us -> 12 us
  blocking collectives: 52.6 us -> 50.8 us
    ppermute x1, starting transfers between devices: 4.84 us -> 7.16 us  [shards(): near = lax.ppermute(own, 'tm', [(i, i + 1) for i in range(devices - 1)])]
    all_gather x1, blocking collectives: 22.3 us -> 20.1 us  [shards(): shares = lax.all_gather(share, 'tm', axis_index_groups=inside)]
  transfers between devices with their start and end apart: 2 -> 2, of which waited for: 1 -> 0; matrix products, arithmetic and copies ran while one was open for 1% -> 1% of each run, Pallas kernels for 0% -> 0%
where the time goes in v5:
time: 94.1 us; the launch traced here: 93.8 us
  blocking collectives  50.8 us (54%)
  Pallas kernels  28.2 us (30%)
  starting transfers between devices  12 us (13%)
  local copies, waits for them, and re-layouts  1.25 us (1%)
    pallas_call x3, Pallas kernels, call(): pl.pallas_call(kernel, out_shape=[jax.ShapeDtypeStruct(o, jnp.float32) fo...  28.2 us
    all_to_all x1, blocking collectives, shards(): lax.all_to_all(jnp.broadcast_to(part[None], (groups,) + half), 'tm', 0, 0...  26.3 us
    all_gather x1, blocking collectives, shards(): shares = lax.all_gather(share, 'tm', axis_index_groups=inside)  20.1 us
    ppermute x1, starting transfers between devices, shards(): near = lax.ppermute(own, 'tm', [(i, i + 1) for i in range(devices - 1)])  7.16 us
    ppermute x1, starting transfers between devices, shards(): far = lax.ppermute(own, 'tm', [(i, i + 2) for i in range(devices - 2)])  4.83 us
    all_gather x1, blocking collectives, shards(): sides = lax.all_gather(parts[:groups - 1], 'tm', axis_index_groups=cores)  4.35 us
  transfers between devices with their start and end apart: 2, of which 0 were waited for; matrix products, arithmetic and copies ran while one was open for 1% of the time, Pallas kernels for 0%

profile of v5, /device:TPU:1, one launch (start us, length us, event | category | flops | bytes accessed | tf_op | source)
XLA Modules:
  0.0 93.8 jit_solution(6324660866075294164)
XLA Ops:
  0.6 4.8 %collective-permute-start = (f32[2,64,64]{2,1,0:T(8,128)}, f32[2,64,64]{2,1,0:T(8,128)S(1)}, u32[]{:S(2)}, u32[]{:S(2)}) collective-permute-start(f32[2,64,64]{2,1,0:T(8,128)} %bitcast.11), channel_id=1, source_target_pairs={{0,2},{1,3},{2,4},{3,5},{4,6},{5,7},{6,8},{7,9},{8,10},{9,11},{10,... | collective-permute-start | bytes 98312 | tf_op jit(solution)/shard_map/ppermute | solution.py:288
  5.5 0.9 pad_maximum_fusion.fields
  6.4 0.0 copy-start.1
  6.4 1.1 %copy-done.1 = bf16[256,1664]{1,0:T(8,128)(2,1)S(1)} copy-done((bf16[256,1664]{1,0:T(8,128)(2,1)S(1)}, bf16[256,1664]{1,0:T(8,128)(2,1)}, u32[]{:S(2)}) %copy-start.1) | copy-done | bytes 851992
  7.5 0.1 shard_map.93.near_table
  7.6 0.0 copy-start.2
  7.6 0.0 copy-start
  7.6 0.0 collective-permute-done.far_ref
  7.6 2.6 %shard_map.94 = (f32[64,128]{1,0:T(8,128)S(1)}, f32[64,128]{1,0:T(8,128)S(1)}) custom-call(f32[2,64,64]{2,1,0:T(8,128)S(1)} %collective-permute-done.far_ref, f32[4,64,64]{2,1,0:T(8,128)S(1)} %pad_maximum_fusion.fields, bf16[256,1664]{1,0:T(8,128)(2,1)S(1)} %shard_map.93.near_table), custom_call_target="tpu_custom_call" | custom-call | tf_op jit(solution)/shard_map/pallas_call | solution.py:273
  10.3 0.0 copy-done.2
  10.3 7.2 %collective-permute-start.1 = (f32[2,64,64]{2,1,0:T(8,128)S(1)}, f32[2,64,64]{2,1,0:T(8,128)S(1)}, u32[]{:S(2)}, u32[]{:S(2)}) collective-permute-start(f32[2,64,64]{2,1,0:T(8,128)S(1)} %bitcast.12), channel_id=1, source_target_pairs={{0,1},{1,2},{2,3},{3,4},{4,5},{5,6},{6,7},{7,8},{8,9},{9,10},{10,1... | collective-permute-start | bytes 98312 | tf_op jit(solution)/shard_map/ppermute | solution.py:301
  17.4 20.1 %all-gather = f32[1024,128]{1,0:T(8,128)S(1)} all-gather(f32[64,128]{1,0:T(8,128)S(1)} %get-tuple-element.16), channel_id=2, replica_groups={{0,1,2,3,4,5,6,7,8,9,10,11,12,13,14,15},{16,17,18,19,20,21,22,23,24,25,..., dimensions={0}, use_global_device_ids=true | all-gather | bytes 557056 | tf_op jit(solution)/shard_map/all_gather | solution.py:303
  37.5 0.0 collective-permute-done.1.near_ref
  37.5 0.0 copy-done
  37.5 7.5 %shard_map.95 = (f32[64,128]{1,0:T(8,128)S(1)}, f32[64,128]{1,0:T(8,128)S(1)}, f32[32,128]{1,0:T(8,128)S(1)}, f32[2,64,64]{2,1,0:T(8,128)}) custom-call(f32[16,64,128]{2,1,0:T(8,128)S(1)} %bitcast.6, f32[2,64,64]{2,1,0:T(8,128)S(1)} %collective-permute-done.1.near_ref, f32[64,128]{1,0:T(8,128)S(1)} %get-tuple-element.18.arrived_ref, ...), custom_call_target="tpu_custom_call" | custom-call | tf_op jit(solution)/shard_map/pallas_call | solution.py:273
  45.1 26.3 %all_to_all.5 = f32[32,32,128]{2,1,0:T(8,128)S(1)} all-to-all(f32[32,32,128]{2,1,0:T(8,128)S(1)} %broadcast_in_dim.17), channel_id=1, replica_groups={{0,16,32,48,64,80,96,112,128,144,160,176,192,208,224,240,256,272,288,30..., dimensions={0} | all-to-all | bytes 1048576 | tf_op jit(solution)/shard_map/all_to_all | solution.py:313
  71.5 4.3 %all-gather.1 = f32[62,32,128]{2,1,0:T(8,128)S(1)} all-gather(f32[31,32,128]{2,1,0:T(8,128)S(1)} %slice.4), channel_id=3, replica_groups={{0,1},{2,3},{4,5},{6,7},{8,9},{10,11},{12,13},{14,15},{16,17},{18,19},{..., dimensions={0}, use_global_device_ids=true | all-gather | bytes 1523712 | tf_op jit(solution)/shard_map/all_gather | solution.py:315
  75.8 18.0 %shard_map.96 = (f32[4,2,64,64]{3,2,1,0:T(8,128)}, f32[1,2,64,64]{3,2,1,0:T(8,128)}, f32[1,2,64,64]{3,2,1,0:T(8,128)}) custom-call(f32[2,31,32,128]{3,2,1,0:T(8,128)S(1)} %bitcast.8, f32[64,128]{1,0:T(8,128)S(1)} %get-tuple-element.20.rhs_ref, f32[16,64,128]{2,1,0:T(8,128)S(1)} %bitcast.7, f32[64,128]{1,0:T(8,128)S(1)} %get-tuple-element.21.first_ref, ...), custom_call_target="tpu_custom_call" | custom-call | tf_op jit(solution)/shard_map/pallas_call | solution.py:273
  (2 shorter events, 0.1 us)
Async XLA Ops:
  0.6 7.0 %collective-permute-start = (f32[2,64,64]{2,1,0:T(8,128)}, f32[2,64,64]{2,1,0:T(8,128)S(1)}, u32[]{:S(2)}, u32[]{:S(2)}) collective-permute-start(f32[2,64,64]{2,1,0:T(8,128)} %bitcast.11), channel_id=1, source_target_pairs={{0,2},{1,3},{2,4},{3,5},{4,6},{5,7},{6,8},{7,9},{8,10},{9,11},{10,... | collective-permute-start | bytes 98312 | tf_op jit(solution)/shard_map/ppermute | solution.py:288
  6.4 1.2 %copy-start.1 = (bf16[256,1664]{1,0:T(8,128)(2,1)S(1)}, bf16[256,1664]{1,0:T(8,128)(2,1)}, u32[]{:S(2)}) copy-start(bf16[256,1664]{1,0:T(8,128)(2,1)} %constant.5.clone.source) | copy-start | bytes 2555908
  7.6 2.7 %copy-start.2 = (f32[1,2,64,64]{3,2,1,0:T(8,128)S(1)}, f32[1,2,64,64]{3,2,1,0:T(8,128)}, u32[]{:S(2)}) copy-start(f32[1,2,64,64]{3,2,1,0:T(8,128)} %param.7) | copy-start | bytes 98308
  7.6 29.9 %copy-start = (bf16[256,1536]{1,0:T(8,128)(2,1)S(1)}, bf16[256,1536]{1,0:T(8,128)(2,1)}, u32[]{:S(2)}) copy-start(bf16[256,1536]{1,0:T(8,128)(2,1)} %constant.4.clone.far_table) | copy-start | bytes 2359300
  10.3 27.2 %collective-permute-start.1 = (f32[2,64,64]{2,1,0:T(8,128)S(1)}, f32[2,64,64]{2,1,0:T(8,128)S(1)}, u32[]{:S(2)}, u32[]{:S(2)}) collective-permute-start(f32[2,64,64]{2,1,0:T(8,128)S(1)} %bitcast.12), channel_id=1, source_target_pairs={{0,1},{1,2},{2,3},{3,4},{4,5},{5,6},{6,7},{7,8},{8,9},{9,10},{10,1... | collective-permute-start | bytes 98312 | tf_op jit(solution)/shard_map/ppermute | solution.py:301

commit v6 on v5

--- a/solution.py
+++ b/solution.py
@@ -75,7 +75,7 @@
     cat = species_tables(time_step, diffusion[1], rank, fine_cross)
     left = np.concatenate([sub[2], cat[2]], 0)
     left = np.concatenate([left, np.zeros_like(left)], 0)
-    return np.concatenate([sub[0], cat[0], sub[1], cat[1], left], 1)
+    return np.concatenate([sub[0], sub[1], cat[0], cat[1], left], 1)
 
 
 def product(left, right):
@@ -129,22 +129,31 @@
         cross = LANES * rank
         second = second_half()
         supply, decay = h * feed, h * (feed + kill)
-        right_at, cross_at = start, start + 2 * LANES
-        left_at = cross_at + 2 * cross
-        deep = slice(0, 4 * GRID if fine_cross else 2 * GRID)
+        wide_at = [start, start + LANES + cross]
+        left_at = start + 2 * (LANES + cross)
 
         def solve(values):
+            count = values[0].shape[0] // GRID
+            halves_of = second if count == 1 else jnp.concatenate([second] * count, 0)
+            rows = [slice(GRID * n, GRID * (n + 1)) for n in range(count)]
             made = []
             for i, value in enumerate(values):
                 high = value.astype(jnp.bfloat16)
                 rest = value - high.astype(jnp.float32)
-                mixed = jnp.where(second, rest, value).astype(jnp.bfloat16)
+                mixed = jnp.where(halves_of, rest, value).astype(jnp.bfloat16)
                 wide = jnp.concatenate([mixed, high], 1)
-                weights = table[deep, cross_at + cross * i : cross_at + cross * (i + 1)]
-                made.append((high, rest, wide, product(wide if fine_cross else high, weights)))
+                at, stop = wide_at[i], wide_at[i] + LANES + cross
+                if fine_cross:
+                    right = product(wide, table[:, at:stop])
+                    right, turned = right[:, :LANES], right[:, LANES:]
+                else:
+                    turned = product(high, table[: 2 * GRID, at + LANES : stop])
+                    right = None
+                made.append((high, rest, wide, turned, right))
             solved = []
-            for i, (value, (high, rest, wide, turned)) in enumerate(zip(values, made)):
-                right = product(wide, table[:, right_at + LANES * i : right_at + LANES * (i + 1)])
+            for i, (high, rest, wide, turned, right) in enumerate(made):
+                if not fine_cross:
+                    right = product(wide, table[:, wide_at[i] : wide_at[i] + LANES])
                 stack = [high, rest.astype(jnp.bfloat16), high]
                 for k in range(rank):
                     part = turned[:, LANES * k : LANES * (k + 1)]
@@ -152,20 +161,30 @@
                     stack.append(part_high)
                     if k < fine_cross:
                         stack += [(part - part_high.astype(jnp.float32)).astype(jnp.bfloat16), part_high]
-                stack = jnp.concatenate(stack, 0)
-                left = table[GRID * i : GRID * (i + 1), left_at : left_at + stack.shape[0]]
-                solved.append((right, product(left, stack)))
+                stack = jnp.concatenate([jnp.concatenate([p[r] for p in stack], 0) for r in rows], 1)
+                left = product(table[GRID * i : GRID * (i + 1), left_at : left_at + stack.shape[0]], stack)
+                left = jnp.concatenate([left[:, LANES * n : LANES * (n + 1)] for n in range(count)], 0)
+                solved.append((right, left))
             return solved
 
-        def step(state, extra=None):
+        def react(state):
             sub, cat = state
             uptake = h * (sub * cat * cat)
-            values = (sub + (supply - supply * sub - uptake), cat + (uptake - decay * cat))
+            return sub + (supply - supply * sub - uptake), cat + (uptake - decay * cat)
+
+        def step(state, extra=None):
+            values = react(state)
             sums = [a + b for a, b in solve(values)]
             if extra is not None:
                 sums = [a + b for a, b in zip(sums, extra)]
             return tuple(a + b for a, b in zip(values, sums))
 
+        def step_two(one, other):
+            values = [jnp.concatenate(pair, 0) for pair in zip(react(one), react(other))]
+            values = [a + (b + c) for a, (b, c) in zip(values, solve(values))]
+            return tuple(v[:GRID] for v in values), tuple(v[GRID:] for v in values)
+
+        step.two = step_two
         return step
 
 
@@ -176,7 +195,7 @@
 
 
 def bound(fields, near_table, far_table=None):
-    rates = loaded(fields.at[2:])
+    rates = loaded(fields.at[2:4])
     fine, middle = FINE.bind(near_table, 0, *rates), MIDDLE.bind(near_table, FINE.width, *rates)
     return fine, middle, None if far_table is None else COARSE.bind(far_table, 0, *rates)
 
@@ -185,10 +204,12 @@
     target[...] = source[...]
 
 
-def relax_kernel(far_ref, fields, near_table, share_ref, arrived_ref):
+def relax_kernel(far_ref, fields, near_table, share_ref, arrived_ref, swap_ref):
     fine, middle, _ = bound(fields, near_table)
     position = lax.axis_index("tm")
     first = loaded(fields)
+    sent = choose(position % 2 == 0, loaded(fields.at[4:]), loaded(far_ref))
+    swap_ref[...] = merge(sent)
     prior = choose(position == 1, first, loaded(far_ref))
     for _ in range(STEPS_DEV):
         prior = fine(prior)
@@ -218,11 +239,11 @@
 ):
     fine, middle, coarse = bound(fields, near_table, far_table)
     position = lax.axis_index("tm")
-    own = choose(position == 0, loaded(fields), loaded(near_ref))
+    own = choose(position == 0, loaded(fields), spread(near_ref[...]))
     start = spread(shares_ref[0])
     state = start
     for _ in range(STEPS_DEV):
-        state, own = fine(state), fine(own)
+        state, own = fine.two(state, own)
     unpack_to(residual_ref, minus(spread(arrived_ref[...]), own))
     leap, handed = middle(start), coarse(start)
     first_ref[...] = merge(minus(state, leap))
@@ -287,7 +308,7 @@
     own = coarse_guess[0]
     far = lax.ppermute(own, "tm", [(i, i + 2) for i in range(devices - 2)])
     far_table = jnp.asarray(COARSE.tables)
-    fields = jnp.concatenate([initial, feed_rate[None], kill_rate[None]], 0)
+    fields = jnp.concatenate([initial, feed_rate[None], kill_rate[None], own], 0)
     near_table = pl.pallas_call(
         fetch_kernel,
         out_shape=jax.ShapeDtypeStruct(near_tables.shape, jnp.bfloat16),
@@ -296,9 +317,8 @@
         cost_estimate=pl.CostEstimate(flops=0, bytes_accessed=4 * near_tables.size, transcendentals=0),
         compiler_params=pltpu.CompilerParams(vmem_limit_bytes=16 * 2**20),
     )(jnp.asarray(near_tables))
-    share, arrived = call(relax_kernel, [field, field], [VMEM] * 3, [], 16, far, fields, near_table)
-    share, own = lax.optimization_barrier((share, own))
-    near = lax.ppermute(own, "tm", [(i, i + 1) for i in range(devices - 1)])
+    share, arrived, swap = call(relax_kernel, [field] * 3, [VMEM] * 3, [], 16, far, fields, near_table)
+    near = lax.ppermute(swap, "tm", [(i, i ^ 1) for i in range(devices)])
     inside = [[g * GROUP + m for m in range(GROUP)] for g in range(groups)]
     shares = lax.all_gather(share, "tm", axis_index_groups=inside)
     first, rhs, part, residual = call(

time: 94.1 us -> 92.3 us (0.981)
  starting transfers between devices: 12 us -> 10.1 us
  blocking collectives: 50.8 us -> 52.2 us
  Pallas kernels: 28.2 us -> 26.8 us
    ppermute x1, starting transfers between devices: 7.16 us -> 5.28 us  [shards(): near = lax.ppermute(swap, 'tm', [(i, i ^ 1) for i in range(devices)])]
    all_gather x1, blocking collectives: 20.1 us -> 21.9 us  [shards(): shares = lax.all_gather(share, 'tm', axis_index_groups=inside)]
    pallas_call x3, Pallas kernels: 28.2 us -> 26.8 us  [call(): pl.pallas_call(kernel, out_shape=[jax.ShapeDtypeStruct(o, jnp.float32) fo...]
where the time goes in v6:
time: 92.3 us; the launch traced here: 92 us
  blocking collectives  52.2 us (57%)
  Pallas kernels  26.8 us (29%)
  starting transfers between devices  10.1 us (11%)
  local copies, waits for them, and re-layouts  1.24 us (1%)
  other arithmetic  0.93 us (1%)
    pallas_call x3, Pallas kernels, call(): pl.pallas_call(kernel, out_shape=[jax.ShapeDtypeStruct(o, jnp.float32) fo...  26.8 us
    all_to_all x1, blocking collectives, shards(): lax.all_to_all(jnp.broadcast_to(part[None], (groups,) + half), 'tm', 0, 0...  26.2 us
    all_gather x1, blocking collectives, shards(): shares = lax.all_gather(share, 'tm', axis_index_groups=inside)  21.9 us
    ppermute x1, starting transfers between devices, shards(): near = lax.ppermute(swap, 'tm', [(i, i ^ 1) for i in range(devices)])  5.28 us
    ppermute x1, starting transfers between devices, shards(): far = lax.ppermute(own, 'tm', [(i, i + 2) for i in range(devices - 2)])  4.83 us
    all_gather x1, blocking collectives, shards(): sides = lax.all_gather(parts[:groups - 1], 'tm', axis_index_groups=cores)  4.1 us
  transfers between devices with their start and end apart: 2, of which 0 were waited for; matrix products, arithmetic and copies ran while one was open for 1% of the time, Pallas kernels for 0%

profile of v6, /device:TPU:1, one launch (start us, length us, event | category | flops | bytes accessed | tf_op | source)
XLA Modules:
  0.0 92.0 jit_solution(8045778748323900272)
XLA Ops:
  0.6 4.8 %collective-permute-start = (f32[2,64,64]{2,1,0:T(8,128)}, f32[2,64,64]{2,1,0:T(8,128)S(1)}, u32[]{:S(2)}, u32[]{:S(2)}) collective-permute-start(f32[2,64,64]{2,1,0:T(8,128)} %bitcast.9), channel_id=1, source_target_pairs={{0,2},{1,3},{2,4},{3,5},{4,6},{5,7},{6,8},{7,9},{8,10},{9,11},{10,... | collective-permute-start | bytes 98312 | tf_op jit(solution)/shard_map/ppermute | solution.py:309
  5.5 0.9 %pad_maximum_fusion.fields = f32[6,64,64]{2,1,0:T(8,128)S(1)} fusion(f32[2,64,64]{2,1,0:T(8,128)} %bitcast.10, f32[1,64,64]{2,1,0:T(8,128)} %bitcast.11, f32[1,64,64]{2,1,0:T(8,128)} %bitcast.12, f32[2,64,64]{2,1,0:T(8,128)} %param.6), kind=kLoop, calls=%fused_computation | loop fusion | flops 73728 | bytes 196608 | tf_op jit(solution)/shard_map/concatenate | solution.py:311
  6.4 0.0 copy-start.1
  6.4 1.1 %copy-done.1 = bf16[256,1664]{1,0:T(8,128)(2,1)S(1)} copy-done((bf16[256,1664]{1,0:T(8,128)(2,1)S(1)}, bf16[256,1664]{1,0:T(8,128)(2,1)}, u32[]{:S(2)}) %copy-start.1) | copy-done | bytes 851992
  7.6 0.1 shard_map.93.near_table
  7.6 0.0 copy-start
  7.6 0.0 collective-permute-done.far_ref
  7.6 2.6 %shard_map.94 = (f32[64,128]{1,0:T(8,128)S(1)}, f32[64,128]{1,0:T(8,128)S(1)}, f32[64,128]{1,0:T(8,128)S(1)}) custom-call(f32[2,64,64]{2,1,0:T(8,128)S(1)} %collective-permute-done.far_ref, f32[6,64,64]{2,1,0:T(8,128)S(1)} %pad_maximum_fusion.fields, bf16[256,1664]{1,0:T(8,128)(2,1)S(1)} %shard_map.93.near_table), custom_call_target="tpu_custom_call" | custom-call | tf_op jit(solution)/shard_map/pallas_call | solution.py:294
  10.3 5.3 %collective-permute-start.1 = (f32[64,128]{1,0:T(8,128)S(1)}, f32[64,128]{1,0:T(8,128)S(1)}, u32[]{:S(2)}, u32[]{:S(2)}) collective-permute-start(f32[64,128]{1,0:T(8,128)S(1)} %get-tuple-element.15), channel_id=1, source_target_pairs={{0,1},{1,0},{2,3},{3,2},{4,5},{5,4},{6,7},{7,6},{8,9},{9,8},{10,11... | collective-permute-start | bytes 98312 | tf_op jit(solution)/shard_map/ppermute | solution.py:321
  15.5 21.9 %all-gather = f32[1024,128]{1,0:T(8,128)S(1)} all-gather(f32[64,128]{1,0:T(8,128)S(1)} %get-tuple-element.14), channel_id=2, replica_groups={{0,1,2,3,4,5,6,7,8,9,10,11,12,13,14,15},{16,17,18,19,20,21,22,23,24,25,..., dimensions={0}, use_global_device_ids=true | all-gather | bytes 557056 | tf_op jit(solution)/shard_map/all_gather | solution.py:323
  37.5 0.0 collective-permute-done.1.near_ref
  37.5 0.0 copy-done
  37.5 7.0 %shard_map.95 = (f32[64,128]{1,0:T(8,128)S(1)}, f32[64,128]{1,0:T(8,128)S(1)}, f32[32,128]{1,0:T(8,128)S(1)}, f32[2,64,64]{2,1,0:T(8,128)}) custom-call(f32[16,64,128]{2,1,0:T(8,128)S(1)} %bitcast.6, f32[64,128]{1,0:T(8,128)S(1)} %collective-permute-done.1.near_ref, f32[64,128]{1,0:T(8,128)S(1)} %get-tuple-element.16.arrived_ref, ...), custom_call_target="tpu_custom_call" | custom-call | tf_op jit(solution)/shard_map/pallas_call | solution.py:294
  44.6 26.2 %all_to_all.5 = f32[32,32,128]{2,1,0:T(8,128)S(1)} all-to-all(f32[32,32,128]{2,1,0:T(8,128)S(1)} %broadcast_in_dim.17), channel_id=1, replica_groups={{0,16,32,48,64,80,96,112,128,144,160,176,192,208,224,240,256,272,288,30..., dimensions={0} | all-to-all | bytes 1048576 | tf_op jit(solution)/shard_map/all_to_all | solution.py:333
  70.8 4.1 %all-gather.1 = f32[62,32,128]{2,1,0:T(8,128)S(1)} all-gather(f32[31,32,128]{2,1,0:T(8,128)S(1)} %slice.4), channel_id=3, replica_groups={{0,1},{2,3},{4,5},{6,7},{8,9},{10,11},{12,13},{14,15},{16,17},{18,19},{..., dimensions={0}, use_global_device_ids=true | all-gather | bytes 1523712 | tf_op jit(solution)/shard_map/all_gather | solution.py:335
  74.9 17.1 %shard_map.96 = (f32[4,2,64,64]{3,2,1,0:T(8,128)}, f32[1,2,64,64]{3,2,1,0:T(8,128)}, f32[1,2,64,64]{3,2,1,0:T(8,128)}) custom-call(f32[2,31,32,128]{3,2,1,0:T(8,128)S(1)} %bitcast.8, f32[64,128]{1,0:T(8,128)S(1)} %get-tuple-element.18.rhs_ref, f32[16,64,128]{2,1,0:T(8,128)S(1)} %bitcast.7, f32[64,128]{1,0:T(8,128)S(1)} %get-tuple-element.19.first_ref, ...), custom_call_target="tpu_custom_call" | custom-call | tf_op jit(solution)/shard_map/pallas_call | solution.py:294
  (2 shorter events, 0.1 us)
Async XLA Ops:
  0.6 7.0 %collective-permute-start = (f32[2,64,64]{2,1,0:T(8,128)}, f32[2,64,64]{2,1,0:T(8,128)S(1)}, u32[]{:S(2)}, u32[]{:S(2)}) collective-permute-start(f32[2,64,64]{2,1,0:T(8,128)} %bitcast.9), channel_id=1, source_target_pairs={{0,2},{1,3},{2,4},{3,5},{4,6},{5,7},{6,8},{7,9},{8,10},{9,11},{10,... | collective-permute-start | bytes 98312 | tf_op jit(solution)/shard_map/ppermute | solution.py:309
  6.4 1.2 %copy-start.1 = (bf16[256,1664]{1,0:T(8,128)(2,1)S(1)}, bf16[256,1664]{1,0:T(8,128)(2,1)}, u32[]{:S(2)}) copy-start(bf16[256,1664]{1,0:T(8,128)(2,1)} %constant.5.clone.source) | copy-start | bytes 2555908
  7.6 29.9 %copy-start = (bf16[256,1536]{1,0:T(8,128)(2,1)S(1)}, bf16[256,1536]{1,0:T(8,128)(2,1)}, u32[]{:S(2)}) copy-start(bf16[256,1536]{1,0:T(8,128)(2,1)} %constant.4.clone.far_table) | copy-start | bytes 2359300
  10.3 27.2 %collective-permute-start.1 = (f32[64,128]{1,0:T(8,128)S(1)}, f32[64,128]{1,0:T(8,128)S(1)}, u32[]{:S(2)}, u32[]{:S(2)}) collective-permute-start(f32[64,128]{1,0:T(8,128)S(1)} %get-tuple-element.15), channel_id=1, source_target_pairs={{0,1},{1,0},{2,3},{3,2},{4,5},{5,4},{6,7},{7,6},{8,9},{9,8},{10,11... | collective-permute-start | bytes 98312 | tf_op jit(solution)/shard_map/ppermute | solution.py:321

commit v7 on v6

--- a/solution.py
+++ b/solution.py
@@ -204,12 +204,10 @@
     target[...] = source[...]
 
 
-def relax_kernel(far_ref, fields, near_table, share_ref, arrived_ref, swap_ref):
+def relax_kernel(far_ref, fields, near_table, share_ref, arrived_ref):
     fine, middle, _ = bound(fields, near_table)
     position = lax.axis_index("tm")
     first = loaded(fields)
-    sent = choose(position % 2 == 0, loaded(fields.at[4:]), loaded(far_ref))
-    swap_ref[...] = merge(sent)
     prior = choose(position == 1, first, loaded(far_ref))
     for _ in range(STEPS_DEV):
         prior = fine(prior)
@@ -235,27 +233,33 @@
 
 
 def group_kernel(
-    shares_ref, near_ref, arrived_ref, fields, near_table, far_table, first_ref, rhs_ref, half_ref, residual_ref
+    shares_ref, near_ref, arrived_ref, fields, near_table, far_table,
+    first_ref, rhs_ref, parts_ref, residual_out, residual_ref, sems,
 ):
     fine, middle, coarse = bound(fields, near_table, far_table)
     position = lax.axis_index("tm")
-    own = choose(position == 0, loaded(fields), spread(near_ref[...]))
+    own = choose(position == 0, loaded(fields), loaded(near_ref))
     start = spread(shares_ref[0])
     state = start
     for _ in range(STEPS_DEV):
         state, own = fine.two(state, own)
     unpack_to(residual_ref, minus(spread(arrived_ref[...]), own))
+    residual_copy = pltpu.make_async_copy(residual_ref, residual_out, sems.at[0])
+    residual_copy.start()
     leap, handed = middle(start), coarse(start)
     first_ref[...] = merge(minus(state, leap))
     state = chain(middle, lambda j: shares_ref[j], state, 1, GROUP, 5)
     rhs = merge(choose(position < GROUP, state, minus(state, handed)))
     rhs_ref[...] = rhs
-    half_ref[...] = jnp.where(position % 2 == 0, rhs[: GRID // 2], rhs[GRID // 2 :])
+    part = jnp.where(position % 2 == 0, rhs[: GRID // 2], rhs[GRID // 2 :])
+    for g in range(parts_ref.shape[0]):
+        parts_ref[g] = part
+    residual_copy.wait()
 
 
 def correct_kernel(
     sides_ref, rhs_ref, shares_ref, first_ref, fields, near_table, far_table,
-    points_ref, value_ref, defect_ref, coarse_kept, middle_kept,
+    points_out, value_out, defect_out, points_ref, value_ref, defect_ref, coarse_kept, middle_kept, sems,
 ):
     fine, middle, coarse = bound(fields, near_table, far_table)
     position = lax.axis_index("tm")
@@ -270,7 +274,14 @@
     earlier = spread(coarse_kept[group_id])
     own_side = spread(rhs_ref[...])
     value = choose(group_id == 0, own_side, coarse(earlier, own_side))
-    unpack_to(value_ref.at[0], value)
+    copies = []
+
+    def emit(source, target):
+        copies.append(pltpu.make_async_copy(source, target, sems.at[len(copies)]))
+        copies[-1].start()
+
+    unpack_to(value_ref, value)
+    emit(value_ref, value_out.at[0])
     middle_kept[0] = merge(earlier)
     state = middle(earlier, spread(first_ref[...]))
     middle_kept[1] = merge(state)
@@ -279,25 +290,31 @@
     side = spread(jnp.where(member == 0, first_ref[...], shares_ref[member]))
     updated = middle(prior, side)
     closing = member == GROUP - 1
+    unpack_to(points_ref.at[STEPS_DEV - 1], choose(closing, value, updated))
+    emit(points_ref.at[STEPS_DEV - 1], points_out.at[STEPS_DEV - 1])
+    unpack_to(defect_ref, choose(closing, minus(updated, value), minus(value, value)))
+    emit(defect_ref, defect_out.at[0])
     state = prior
     for i in range(STEPS_DEV - 1):
         state = fine(state)
         unpack_to(points_ref.at[i], state)
-    unpack_to(points_ref.at[STEPS_DEV - 1], choose(closing, value, updated))
-    unpack_to(defect_ref.at[0], choose(closing, minus(updated, value), minus(value, value)))
+        emit(points_ref.at[i], points_out.at[i])
+    for copy in copies:
+        copy.wait()
 
 
 VMEM = pl.BlockSpec(memory_space=pltpu.VMEM)
-
-
-def call(kernel, outs, in_specs, scratch, limit, *operands):
+HBM = pl.BlockSpec(memory_space=pltpu.HBM)
+
+
+def call(kernel, shapes, in_specs, out_specs, scratch, *operands):
     return pl.pallas_call(
         kernel,
-        out_shape=[jax.ShapeDtypeStruct(o, jnp.float32) for o in outs],
+        out_shape=[jax.ShapeDtypeStruct(s, jnp.float32) for s in shapes],
         in_specs=in_specs,
-        out_specs=[VMEM] * len(outs),
+        out_specs=out_specs,
         scratch_shapes=scratch,
-        compiler_params=pltpu.CompilerParams(vmem_limit_bytes=limit * 2**20),
+        compiler_params=pltpu.CompilerParams(vmem_limit_bytes=16 * 2**20),
     )(*operands)
 
 
@@ -308,7 +325,7 @@
     own = coarse_guess[0]
     far = lax.ppermute(own, "tm", [(i, i + 2) for i in range(devices - 2)])
     far_table = jnp.asarray(COARSE.tables)
-    fields = jnp.concatenate([initial, feed_rate[None], kill_rate[None], own], 0)
+    fields = jnp.concatenate([initial, feed_rate[None], kill_rate[None]], 0)
     near_table = pl.pallas_call(
         fetch_kernel,
         out_shape=jax.ShapeDtypeStruct(near_tables.shape, jnp.bfloat16),
@@ -317,28 +334,31 @@
         cost_estimate=pl.CostEstimate(flops=0, bytes_accessed=4 * near_tables.size, transcendentals=0),
         compiler_params=pltpu.CompilerParams(vmem_limit_bytes=16 * 2**20),
     )(jnp.asarray(near_tables))
-    share, arrived, swap = call(relax_kernel, [field] * 3, [VMEM] * 3, [], 16, far, fields, near_table)
-    near = lax.ppermute(swap, "tm", [(i, i ^ 1) for i in range(devices)])
+    near_table, own = lax.optimization_barrier((near_table, own))
+    near = lax.ppermute(own, "tm", [(i, i + 1) for i in range(devices - 1)])
+    share, arrived = call(relax_kernel, [field] * 2, [VMEM] * 3, [VMEM] * 2, [], far, fields, near_table)
     inside = [[g * GROUP + m for m in range(GROUP)] for g in range(groups)]
     shares = lax.all_gather(share, "tm", axis_index_groups=inside)
-    first, rhs, part, residual = call(
+    parts_shape = (groups,) + half
+    first, rhs, parts, residual = call(
         group_kernel,
-        [field, field, half, pair],
+        [field, field, parts_shape, pair],
         [VMEM] * 6,
-        [],
-        16,
+        [VMEM] * 3 + [HBM],
+        [pltpu.VMEM(pair, jnp.float32), pltpu.SemaphoreType.DMA((1,))],
         shares, near, arrived, fields, near_table, far_table,
     )
     across = [[g * GROUP + m for g in range(groups)] for m in range(GROUP)]
-    parts = lax.all_to_all(jnp.broadcast_to(part[None], (groups,) + half), "tm", 0, 0, axis_index_groups=across)
+    parts = lax.all_to_all(parts, "tm", 0, 0, axis_index_groups=across)
     cores = [[2 * c, 2 * c + 1] for c in range(devices // 2)]
     sides = lax.all_gather(parts[: groups - 1], "tm", axis_index_groups=cores)
+    shapes = [(STEPS_DEV,) + pair, pair, pair, (groups,) + field, (GROUP,) + field]
     points, value, defect = call(
         correct_kernel,
         [(STEPS_DEV,) + pair, (1,) + pair, (1,) + pair],
         [VMEM] * 7,
-        [pltpu.VMEM((groups,) + field, jnp.float32), pltpu.VMEM((GROUP,) + field, jnp.float32)],
-        16,
+        [HBM] * 3,
+        [pltpu.VMEM(s, jnp.float32) for s in shapes] + [pltpu.SemaphoreType.DMA((STEPS_DEV + 2,))],
         sides, rhs, shares, first, fields, near_table, far_table,
     )
     return points, residual[None], value, defect

time: 92.3 us -> 89.9 us (0.974)
  blocking collectives: 52.2 us -> 50.9 us
    all_gather x1, blocking collectives: 21.9 us -> 20.6 us  [shards(): shares = lax.all_gather(share, 'tm', axis_index_groups=inside)]
    unnamed x4 -> x12, local copies, waits for them, and re-layouts: 1.16 us -> 1.93 us
  transfers between devices with their start and end apart: 2 -> 2, of which waited for: 0 -> 0; matrix products, arithmetic and copies ran while one was open for 1% -> 0% of each run, Pallas kernels for 0% -> 3%
where the time goes in v7:
time: 89.9 us; the launch traced here: 89.6 us
  blocking collectives  50.9 us (57%)
  Pallas kernels  26.4 us (29%)
  starting transfers between devices  9.66 us (11%)
  local copies, waits for them, and re-layouts  1.96 us (2%)
    pallas_call x3, Pallas kernels, call(): pl.pallas_call(kernel, out_shape=[jax.ShapeDtypeStruct(s, jnp.float32) fo...  26.3 us
    all_to_all x1, blocking collectives, shards(): parts = lax.all_to_all(parts, 'tm', 0, 0, axis_index_groups=across)  26.2 us
    all_gather x1, blocking collectives, shards(): shares = lax.all_gather(share, 'tm', axis_index_groups=inside)  20.6 us
    ppermute x1, starting transfers between devices, shards(): near = lax.ppermute(own, 'tm', [(i, i + 1) for i in range(devices - 1)])  4.83 us
    ppermute x1, starting transfers between devices, shards(): far = lax.ppermute(own, 'tm', [(i, i + 2) for i in range(devices - 2)])  4.83 us
    all_gather x1, blocking collectives, shards(): sides = lax.all_gather(parts[:groups - 1], 'tm', axis_index_groups=cores)  4.1 us
    unnamed x12, local copies, waits for them, and re-layouts  1.93 us
  transfers between devices with their start and end apart: 2, of which 0 were waited for; matrix products, arithmetic and copies ran while one was open for 0% of the time, Pallas kernels for 3%

profile of v7, /device:TPU:1, one launch (start us, length us, event | category | flops | bytes accessed | tf_op | source)
XLA Modules:
  0.0 89.6 jit_solution(5030346430961623615)
XLA Ops:
  0.6 4.8 %collective-permute-start = (f32[2,64,64]{2,1,0:T(8,128)}, f32[2,64,64]{2,1,0:T(8,128)S(1)}, u32[]{:S(2)}, u32[]{:S(2)}) collective-permute-start(f32[2,64,64]{2,1,0:T(8,128)} %bitcast.11), channel_id=1, source_target_pairs={{0,2},{1,3},{2,4},{3,5},{4,6},{5,7},{6,8},{7,9},{8,10},{9,11},{10,... | collective-permute-start | bytes 98312 | tf_op jit(solution)/shard_map/ppermute | solution.py:326
  5.5 0.0 copy-start.1
  5.5 1.1 %copy-done.1 = bf16[256,1664]{1,0:T(8,128)(2,1)S(1)} copy-done((bf16[256,1664]{1,0:T(8,128)(2,1)S(1)}, bf16[256,1664]{1,0:T(8,128)(2,1)}, u32[]{:S(2)}) %copy-start.1) | copy-done | bytes 851992
  6.6 0.0 copy-start.5
  6.6 0.0 copy-start.2
  6.6 0.0 copy-start.3
  6.6 0.0 copy-start.4
  6.6 0.1 shard_map.93.near_table
  6.7 0.8 copy-done.5
  7.5 4.8 %collective-permute-start.1 = (f32[2,64,64]{2,1,0:T(8,128)S(1)}, f32[2,64,64]{2,1,0:T(8,128)S(1)}, u32[]{:S(2)}, u32[]{:S(2)}) collective-permute-start(f32[2,64,64]{2,1,0:T(8,128)S(1)} %bitcast.12), channel_id=1, source_target_pairs={{0,1},{1,2},{2,3},{3,4},{4,5},{5,6},{6,7},{7,8},{8,9},{9,10},{10,1... | collective-permute-start | bytes 98312 | tf_op jit(solution)/shard_map/ppermute | solution.py:338
  12.3 0.0 copy-done.2
  12.3 0.0 copy-done.3
  12.3 0.0 copy-done.4
  12.4 0.0 copy-start
  12.4 0.0 collective-permute-done.far_ref
  12.4 2.6 %shard_map.94 = (f32[64,128]{1,0:T(8,128)S(1)}, f32[64,128]{1,0:T(8,128)S(1)}) custom-call(f32[2,64,64]{2,1,0:T(8,128)S(1)} %collective-permute-done.far_ref, f32[4,64,64]{2,1,0:T(8,128)S(1)} %pad_maximum_fusion.fields, bf16[256,1664]{1,0:T(8,128)(2,1)S(1)} %shard_map.93.near_table), custom_call_target="tpu_custom_call" | custom-call | tf_op jit(solution)/shard_map/pallas_call | solution.py:311
  15.0 20.6 %all-gather = f32[1024,128]{1,0:T(8,128)S(1)} all-gather(f32[64,128]{1,0:T(8,128)S(1)} %get-tuple-element.16), channel_id=2, replica_groups={{0,1,2,3,4,5,6,7,8,9,10,11,12,13,14,15},{16,17,18,19,20,21,22,23,24,25,..., dimensions={0}, use_global_device_ids=true | all-gather | bytes 557056 | tf_op jit(solution)/shard_map/all_gather | solution.py:341
  35.5 0.0 collective-permute-done.1.near_ref
  35.6 0.0 copy-done
  35.6 6.6 %shard_map.95 = (f32[64,128]{1,0:T(8,128)S(1)}, f32[64,128]{1,0:T(8,128)S(1)}, f32[32,32,128]{2,1,0:T(8,128)S(1)}, f32[2,64,64]{2,1,0:T(8,128)}) custom-call(f32[16,64,128]{2,1,0:T(8,128)S(1)} %bitcast.6, f32[2,64,64]{2,1,0:T(8,128)S(1)} %collective-permute-done.1.near_ref, f32[64,128]{1,0:T(8,128)S(1)} %get-tuple-element.18.arrived_ref, ...), custom_call_target="tpu_custom_call" | custom-call | tf_op jit(solution)/shard_map/pallas_call | solution.py:311
  42.2 26.2 %all_to_all.5 = f32[32,32,128]{2,1,0:T(8,128)S(1)} all-to-all(f32[32,32,128]{2,1,0:T(8,128)S(1)} %get-tuple-element.19), channel_id=1, replica_groups={{0,16,32,48,64,80,96,112,128,144,160,176,192,208,224,240,256,272,288,30..., dimensions={0} | all-to-all | bytes 1048576 | tf_op jit(solution)/shard_map/all_to_all | solution.py:352
  68.4 4.1 %all-gather.1 = f32[62,32,128]{2,1,0:T(8,128)S(1)} all-gather(f32[31,32,128]{2,1,0:T(8,128)S(1)} %slice.4), channel_id=3, replica_groups={{0,1},{2,3},{4,5},{6,7},{8,9},{10,11},{12,13},{14,15},{16,17},{18,19},{..., dimensions={0}, use_global_device_ids=true | all-gather | bytes 1523712 | tf_op jit(solution)/shard_map/all_gather | solution.py:354
  72.5 17.1 %shard_map.96 = (f32[4,2,64,64]{3,2,1,0:T(8,128)}, f32[1,2,64,64]{3,2,1,0:T(8,128)}, f32[1,2,64,64]{3,2,1,0:T(8,128)}) custom-call(f32[2,31,32,128]{3,2,1,0:T(8,128)S(1)} %bitcast.8, f32[64,128]{1,0:T(8,128)S(1)} %get-tuple-element.20.rhs_ref, f32[16,64,128]{2,1,0:T(8,128)S(1)} %bitcast.7, f32[64,128]{1,0:T(8,128)S(1)} %get-tuple-element.21.first_ref, ...), custom_call_target="tpu_custom_call" | custom-call | tf_op jit(solution)/shard_map/pallas_call | solution.py:311
  (2 shorter events, 0.0 us)
Async XLA Ops:
  0.6 11.7 %collective-permute-start = (f32[2,64,64]{2,1,0:T(8,128)}, f32[2,64,64]{2,1,0:T(8,128)S(1)}, u32[]{:S(2)}, u32[]{:S(2)}) collective-permute-start(f32[2,64,64]{2,1,0:T(8,128)} %bitcast.11), channel_id=1, source_target_pairs={{0,2},{1,3},{2,4},{3,5},{4,6},{5,7},{6,8},{7,9},{8,10},{9,11},{10,... | collective-permute-start | bytes 98312 | tf_op jit(solution)/shard_map/ppermute | solution.py:326
  5.5 1.2 %copy-start.1 = (bf16[256,1664]{1,0:T(8,128)(2,1)S(1)}, bf16[256,1664]{1,0:T(8,128)(2,1)}, u32[]{:S(2)}) copy-start(bf16[256,1664]{1,0:T(8,128)(2,1)} %constant.5.clone.source) | copy-start | bytes 2555908
  6.6 0.8 copy-start.5
  6.6 5.7 %copy-start.2 = (f32[2,64,64]{2,1,0:T(8,128)S(1)}, f32[2,64,64]{2,1,0:T(8,128)}, u32[]{:S(2)}) copy-start(f32[2,64,64]{2,1,0:T(8,128)} %param.6) | copy-start | bytes 98308
  6.6 5.7 %copy-start.3 = (f32[64,64]{1,0:T(8,128)S(1)}, f32[64,64]{1,0:T(8,128)}, u32[]{:S(2)}) copy-start(f32[64,64]{1,0:T(8,128)} %param.9) | copy-start | bytes 49156
  6.6 5.7 %copy-start.4 = (f32[64,64]{1,0:T(8,128)S(1)}, f32[64,64]{1,0:T(8,128)}, u32[]{:S(2)}) copy-start(f32[64,64]{1,0:T(8,128)} %param.8) | copy-start | bytes 49156
  7.5 28.1 %collective-permute-start.1 = (f32[2,64,64]{2,1,0:T(8,128)S(1)}, f32[2,64,64]{2,1,0:T(8,128)S(1)}, u32[]{:S(2)}, u32[]{:S(2)}) collective-permute-start(f32[2,64,64]{2,1,0:T(8,128)S(1)} %bitcast.12), channel_id=1, source_target_pairs={{0,1},{1,2},{2,3},{3,4},{4,5},{5,6},{6,7},{7,8},{8,9},{9,10},{10,1... | collective-permute-start | bytes 98312 | tf_op jit(solution)/shard_map/ppermute | solution.py:338
  12.4 23.2 %copy-start = (bf16[256,1536]{1,0:T(8,128)(2,1)S(1)}, bf16[256,1536]{1,0:T(8,128)(2,1)}, u32[]{:S(2)}) copy-start(bf16[256,1536]{1,0:T(8,128)(2,1)} %constant.4.clone.far_table) | copy-start | bytes 2359300

commit v8 on v7

--- a/solution.py
+++ b/solution.py
@@ -55,12 +55,12 @@
 def species_tables(time_step, rate, rank, fine_cross):
     first, cross, signs = solve_terms(time_step, rate, rank)
     high, low = halves(first)
-    right = np.concatenate([twice(high), twice(high), twice(low), np.zeros_like(twice(low))], 0)
+    right = np.concatenate([twice(high), twice(low), twice(high), np.zeros_like(twice(low))], 0)
     left = [high, high, low]
     cross_high, cross_low = zip(*[halves(m) for m in cross])
     cross_high = np.concatenate([twice(m) for m in cross_high], 1)
     cross_low = np.concatenate([twice(m) for m in cross_low], 1)
-    parts = [cross_high, cross_high, cross_low] if fine_cross else [cross_high, cross_low]
+    parts = [cross_high, cross_low, cross_high] if fine_cross else [cross_high, cross_low]
     blank = np.zeros((4 * GRID - GRID * len(parts), cross_high.shape[1]), ml_dtypes.bfloat16)
     mixing = np.concatenate(parts + [blank], 0)
     for k, (matrix, sign) in enumerate(zip(cross, signs)):
@@ -127,21 +127,18 @@
         h = jnp.float32(self.time_step)
         rank, fine_cross = self.rank, self.fine_cross
         cross = LANES * rank
-        second = second_half()
         supply, decay = h * feed, h * (feed + kill)
         wide_at = [start, start + LANES + cross]
         left_at = start + 2 * (LANES + cross)
 
         def solve(values):
             count = values[0].shape[0] // GRID
-            halves_of = second if count == 1 else jnp.concatenate([second] * count, 0)
             rows = [slice(GRID * n, GRID * (n + 1)) for n in range(count)]
             made = []
             for i, value in enumerate(values):
                 high = value.astype(jnp.bfloat16)
-                rest = value - high.astype(jnp.float32)
-                mixed = jnp.where(halves_of, rest, value).astype(jnp.bfloat16)
-                wide = jnp.concatenate([mixed, high], 1)
+                rest = (value - high.astype(jnp.float32)).astype(jnp.bfloat16)
+                wide = jnp.concatenate([high, rest], 1)
                 at, stop = wide_at[i], wide_at[i] + LANES + cross
                 if fine_cross:
                     right = product(wide, table[:, at:stop])
@@ -154,7 +151,7 @@
             for i, (high, rest, wide, turned, right) in enumerate(made):
                 if not fine_cross:
                     right = product(wide, table[:, wide_at[i] : wide_at[i] + LANES])
-                stack = [high, rest.astype(jnp.bfloat16), high]
+                stack = [high, rest, high]
                 for k in range(rank):
                     part = turned[:, LANES * k : LANES * (k + 1)]
                     part_high = part.astype(jnp.bfloat16)
@@ -169,7 +166,7 @@
 
         def react(state):
             sub, cat = state
-            uptake = h * (sub * cat * cat)
+            uptake = (h * sub) * (cat * cat)
             return sub + (supply - supply * sub - uptake), cat + (uptake - decay * cat)
 
         def step(state, extra=None):
@@ -220,16 +217,19 @@
     arrived_ref[...] = merge(arrived)
 
 
-def chain(step, load, state, start, stop, block, keep=None):
-    def turn(t, state):
+def chain(step, load, state, start, count, block):
+    single = count % block
+
+    def turn(j, state):
+        return step(state, spread(load(j)))
+
+    def turns(t, state):
         for i in range(block):
-            j = start + t * block + i
-            state = step(state, spread(load(j)))
-            if keep is not None:
-                keep[j + 1] = merge(state)
+            state = turn(start + single + t * block + i, state)
         return state
 
-    return lax.fori_loop(0, (stop - start) // block, turn, state)
+    state = lax.fori_loop(start, start + single, turn, state) if not isinstance(single, int) or single else state
+    return lax.fori_loop(0, count // block, turns, state)
 
 
 def group_kernel(
@@ -248,7 +248,7 @@
     residual_copy.start()
     leap, handed = middle(start), coarse(start)
     first_ref[...] = merge(minus(state, leap))
-    state = chain(middle, lambda j: shares_ref[j], state, 1, GROUP, 5)
+    state = chain(middle, lambda j: shares_ref[j], state, 1, GROUP - 1, 5)
     rhs = merge(choose(position < GROUP, state, minus(state, handed)))
     rhs_ref[...] = rhs
     part = jnp.where(position % 2 == 0, rhs[: GRID // 2], rhs[GRID // 2 :])
@@ -259,7 +259,7 @@
 
 def correct_kernel(
     sides_ref, rhs_ref, shares_ref, first_ref, fields, near_table, far_table,
-    points_out, value_out, defect_out, points_ref, value_ref, defect_ref, coarse_kept, middle_kept, sems,
+    points_out, value_out, defect_out, points_ref, value_ref, defect_ref, sems,
 ):
     fine, middle, coarse = bound(fields, near_table, far_table)
     position = lax.axis_index("tm")
@@ -268,10 +268,9 @@
     def coarse_side(g):
         return jnp.concatenate([sides_ref[0, g], sides_ref[1, g]], 0)
 
-    coarse_kept[0] = merge(loaded(fields))
-    coarse_kept[1] = coarse_side(0)
-    chain(coarse, coarse_side, spread(coarse_side(0)), 1, sides_ref.shape[1], 5, coarse_kept)
-    earlier = spread(coarse_kept[group_id])
+    steps = jnp.maximum(group_id - 1, 0)
+    earlier = chain(coarse, coarse_side, spread(coarse_side(0)), 1, steps, 5)
+    earlier = choose(group_id == 0, loaded(fields), earlier)
     own_side = spread(rhs_ref[...])
     value = choose(group_id == 0, own_side, coarse(earlier, own_side))
     copies = []
@@ -282,12 +281,12 @@
 
     unpack_to(value_ref, value)
     emit(value_ref, value_out.at[0])
-    middle_kept[0] = merge(earlier)
-    state = middle(earlier, spread(first_ref[...]))
-    middle_kept[1] = merge(state)
-    chain(middle, lambda j: shares_ref[j], state, 1, GROUP - 1, 7, middle_kept)
-    prior = spread(middle_kept[member])
-    side = spread(jnp.where(member == 0, first_ref[...], shares_ref[member]))
+
+    def right_side(j):
+        return jnp.where(j == 0, first_ref[...], shares_ref[j])
+
+    prior = chain(middle, right_side, earlier, 0, member, 3)
+    side = spread(right_side(member))
     updated = middle(prior, side)
     closing = member == GROUP - 1
     unpack_to(points_ref.at[STEPS_DEV - 1], choose(closing, value, updated))
@@ -352,7 +351,7 @@
     parts = lax.all_to_all(parts, "tm", 0, 0, axis_index_groups=across)
     cores = [[2 * c, 2 * c + 1] for c in range(devices // 2)]
     sides = lax.all_gather(parts[: groups - 1], "tm", axis_index_groups=cores)
-    shapes = [(STEPS_DEV,) + pair, pair, pair, (groups,) + field, (GROUP,) + field]
+    shapes = [(STEPS_DEV,) + pair, pair, pair]
     points, value, defect = call(
         correct_kernel,
         [(STEPS_DEV,) + pair, (1,) + pair, (1,) + pair],

time: 89.9 us -> 80.3 us (0.89)
  the two profiles are of different devices: /device:TPU:1 before, /device:TPU:62 now
where the time goes in v8:
time: 80.3 us; the launch traced here: 79.2 us
  blocking collectives  43.4 us (54%)
  Pallas kernels  21.5 us (27%)
  starting transfers between devices  6.19 us (8%)
  waiting for transfers between devices  5.4 us (7%)
  local copies, waits for them, and re-layouts  1.96 us (2%)
    all_to_all x1, blocking collectives, shards(): parts = lax.all_to_all(parts, 'tm', 0, 0, axis_index_groups=across)  23.5 us
    pallas_call x3, Pallas kernels, call(): pl.pallas_call(kernel, out_shape=[jax.ShapeDtypeStruct(s, jnp.float32) fo...  21.5 us
    all_gather x1, blocking collectives, shards(): shares = lax.all_gather(share, 'tm', axis_index_groups=inside)  17.3 us
    ppermute x1, waiting for transfers between devices, shards(): far = lax.ppermute(own, 'tm', [(i, i + 2) for i in range(devices - 2)])  5.39 us
    ppermute x1, starting transfers between devices, shards(): far = lax.ppermute(own, 'tm', [(i, i + 2) for i in range(devices - 2)])  4.28 us
    all_gather x1, blocking collectives, shards(): sides = lax.all_gather(parts[:groups - 1], 'tm', axis_index_groups=cores)  2.53 us
    unnamed x12, local copies, waits for them, and re-layouts  1.93 us
    ppermute x1, starting transfers between devices, shards(): near = lax.ppermute(own, 'tm', [(i, i + 1) for i in range(devices - 1)])  1.91 us
  transfers between devices with their start and end apart: 2, of which 1 were waited for; matrix products, arithmetic and copies ran while one was open for 0% of the time, Pallas kernels for 3%

profile of v8, /device:TPU:62, one launch (start us, length us, event | category | flops | bytes accessed | tf_op | source)
XLA Modules:
  0.0 79.2 jit_solution(15493600577310975714)
XLA Ops:
  0.6 4.3 %collective-permute-start = (f32[2,64,64]{2,1,0:T(8,128)}, f32[2,64,64]{2,1,0:T(8,128)S(1)}, u32[]{:S(2)}, u32[]{:S(2)}) collective-permute-start(f32[2,64,64]{2,1,0:T(8,128)} %bitcast.11), channel_id=1, source_target_pairs={{0,2},{1,3},{2,4},{3,5},{4,6},{5,7},{6,8},{7,9},{8,10},{9,11},{10,... | collective-permute-start | bytes 98312 | tf_op jit(solution)/shard_map/ppermute | solution.py:325
  4.9 0.0 copy-start.1
  4.9 1.1 %copy-done.1 = bf16[256,1664]{1,0:T(8,128)(2,1)S(1)} copy-done((bf16[256,1664]{1,0:T(8,128)(2,1)S(1)}, bf16[256,1664]{1,0:T(8,128)(2,1)}, u32[]{:S(2)}) %copy-start.1) | copy-done | bytes 851992
  6.1 0.0 copy-start.5
  6.1 0.0 copy-start.2
  6.1 0.0 copy-start.3
  6.1 0.0 copy-start.4
  6.1 0.1 shard_map.93.near_table
  6.2 0.8 copy-done.5
  6.9 1.9 %collective-permute-start.1 = (f32[2,64,64]{2,1,0:T(8,128)S(1)}, f32[2,64,64]{2,1,0:T(8,128)S(1)}, u32[]{:S(2)}, u32[]{:S(2)}) collective-permute-start(f32[2,64,64]{2,1,0:T(8,128)S(1)} %bitcast.12), channel_id=1, source_target_pairs={{0,1},{1,2},{2,3},{3,4},{4,5},{5,6},{6,7},{7,8},{8,9},{9,10},{10,1... | collective-permute-start | bytes 98312 | tf_op jit(solution)/shard_map/ppermute | solution.py:337
  8.8 0.0 copy-done.2
  8.8 0.0 copy-done.3
  8.9 0.0 copy-done.4
  8.9 0.0 copy-start
  8.9 5.4 %collective-permute-done.far_ref = f32[2,64,64]{2,1,0:T(8,128)S(1)} collective-permute-done((f32[2,64,64]{2,1,0:T(8,128)}, f32[2,64,64]{2,1,0:T(8,128)S(1)}, u32[]{:S(2)}, u32[]{:S(2)}) %collective-permute-start) | collective-permute-done | bytes 32800 | tf_op jit(solution)/shard_map/ppermute | solution.py:325
  14.3 2.6 %shard_map.94 = (f32[64,128]{1,0:T(8,128)S(1)}, f32[64,128]{1,0:T(8,128)S(1)}) custom-call(f32[2,64,64]{2,1,0:T(8,128)S(1)} %collective-permute-done.far_ref, f32[4,64,64]{2,1,0:T(8,128)S(1)} %pad_maximum_fusion.fields, bf16[256,1664]{1,0:T(8,128)(2,1)S(1)} %shard_map.93.near_table), custom_call_target="tpu_custom_call" | custom-call | tf_op jit(solution)/shard_map/pallas_call | solution.py:310
  16.9 17.3 %all-gather = f32[1024,128]{1,0:T(8,128)S(1)} all-gather(f32[64,128]{1,0:T(8,128)S(1)} %get-tuple-element.16), channel_id=2, replica_groups={{0,1,2,3,4,5,6,7,8,9,10,11,12,13,14,15},{16,17,18,19,20,21,22,23,24,25,..., dimensions={0}, use_global_device_ids=true | all-gather | bytes 557056 | tf_op jit(solution)/shard_map/all_gather | solution.py:340
  34.2 0.0 collective-permute-done.1.near_ref
  34.2 0.0 copy-done
  34.2 6.5 %shard_map.95 = (f32[64,128]{1,0:T(8,128)S(1)}, f32[64,128]{1,0:T(8,128)S(1)}, f32[32,32,128]{2,1,0:T(8,128)S(1)}, f32[2,64,64]{2,1,0:T(8,128)}) custom-call(f32[16,64,128]{2,1,0:T(8,128)S(1)} %bitcast.6, f32[2,64,64]{2,1,0:T(8,128)S(1)} %collective-permute-done.1.near_ref, f32[64,128]{1,0:T(8,128)S(1)} %get-tuple-element.18.arrived_ref, ...), custom_call_target="tpu_custom_call" | custom-call | tf_op jit(solution)/shard_map/pallas_call | solution.py:310
  40.8 23.5 %all_to_all.5 = f32[32,32,128]{2,1,0:T(8,128)S(1)} all-to-all(f32[32,32,128]{2,1,0:T(8,128)S(1)} %get-tuple-element.19), channel_id=1, replica_groups={{0,16,32,48,64,80,96,112,128,144,160,176,192,208,224,240,256,272,288,30..., dimensions={0} | all-to-all | bytes 1048576 | tf_op jit(solution)/shard_map/all_to_all | solution.py:351
  64.4 2.5 %all-gather.1 = f32[62,32,128]{2,1,0:T(8,128)S(1)} all-gather(f32[31,32,128]{2,1,0:T(8,128)S(1)} %slice.4), channel_id=3, replica_groups={{0,1},{2,3},{4,5},{6,7},{8,9},{10,11},{12,13},{14,15},{16,17},{18,19},{..., dimensions={0}, use_global_device_ids=true | all-gather | bytes 1523712 | tf_op jit(solution)/shard_map/all_gather | solution.py:353
  66.9 12.3 %shard_map.96 = (f32[4,2,64,64]{3,2,1,0:T(8,128)}, f32[1,2,64,64]{3,2,1,0:T(8,128)}, f32[1,2,64,64]{3,2,1,0:T(8,128)}) custom-call(f32[2,31,32,128]{3,2,1,0:T(8,128)S(1)} %bitcast.8, f32[64,128]{1,0:T(8,128)S(1)} %get-tuple-element.20.rhs_ref, f32[16,64,128]{2,1,0:T(8,128)S(1)} %bitcast.7, f32[64,128]{1,0:T(8,128)S(1)} %get-tuple-element.21.first_ref, ...), custom_call_target="tpu_custom_call" | custom-call | tf_op jit(solution)/shard_map/pallas_call | solution.py:310
  (2 shorter events, 0.0 us)
Async XLA Ops:
  0.6 13.7 %collective-permute-start = (f32[2,64,64]{2,1,0:T(8,128)}, f32[2,64,64]{2,1,0:T(8,128)S(1)}, u32[]{:S(2)}, u32[]{:S(2)}) collective-permute-start(f32[2,64,64]{2,1,0:T(8,128)} %bitcast.11), channel_id=1, source_target_pairs={{0,2},{1,3},{2,4},{3,5},{4,6},{5,7},{6,8},{7,9},{8,10},{9,11},{10,... | collective-permute-start | bytes 98312 | tf_op jit(solution)/shard_map/ppermute | solution.py:325
  4.9 1.2 %copy-start.1 = (bf16[256,1664]{1,0:T(8,128)(2,1)S(1)}, bf16[256,1664]{1,0:T(8,128)(2,1)}, u32[]{:S(2)}) copy-start(bf16[256,1664]{1,0:T(8,128)(2,1)} %constant.5.clone.source) | copy-start | bytes 2555908
  6.1 0.8 %copy-start.5 = (f32[1,2,64,64]{3,2,1,0:T(8,128)S(1)}, f32[1,2,64,64]{3,2,1,0:T(8,128)}, u32[]{:S(2)}) copy-start(f32[1,2,64,64]{3,2,1,0:T(8,128)} %param.7) | copy-start | bytes 98308
  6.1 2.8 %copy-start.2 = (f32[2,64,64]{2,1,0:T(8,128)S(1)}, f32[2,64,64]{2,1,0:T(8,128)}, u32[]{:S(2)}) copy-start(f32[2,64,64]{2,1,0:T(8,128)} %param.6) | copy-start | bytes 98308
  6.1 2.8 %copy-start.3 = (f32[64,64]{1,0:T(8,128)S(1)}, f32[64,64]{1,0:T(8,128)}, u32[]{:S(2)}) copy-start(f32[64,64]{1,0:T(8,128)} %param.9) | copy-start | bytes 49156
  6.1 2.8 %copy-start.4 = (f32[64,64]{1,0:T(8,128)S(1)}, f32[64,64]{1,0:T(8,128)}, u32[]{:S(2)}) copy-start(f32[64,64]{1,0:T(8,128)} %param.8) | copy-start | bytes 49156
  6.9 27.3 %collective-permute-start.1 = (f32[2,64,64]{2,1,0:T(8,128)S(1)}, f32[2,64,64]{2,1,0:T(8,128)S(1)}, u32[]{:S(2)}, u32[]{:S(2)}) collective-permute-start(f32[2,64,64]{2,1,0:T(8,128)S(1)} %bitcast.12), channel_id=1, source_target_pairs={{0,1},{1,2},{2,3},{3,4},{4,5},{5,6},{6,7},{7,8},{8,9},{9,10},{10,1... | collective-permute-start | bytes 98312 | tf_op jit(solution)/shard_map/ppermute | solution.py:337
  8.9 25.3 %copy-start = (bf16[256,1536]{1,0:T(8,128)(2,1)S(1)}, bf16[256,1536]{1,0:T(8,128)(2,1)}, u32[]{:S(2)}) copy-start(bf16[256,1536]{1,0:T(8,128)(2,1)} %constant.4.clone.far_table) | copy-start | bytes 2359300

commit v9 on v8

--- a/solution.py
+++ b/solution.py
@@ -269,35 +269,34 @@
         return jnp.concatenate([sides_ref[0, g], sides_ref[1, g]], 0)
 
     steps = jnp.maximum(group_id - 1, 0)
-    earlier = chain(coarse, coarse_side, spread(coarse_side(0)), 1, steps, 5)
+    earlier = chain(coarse, coarse_side, spread(coarse_side(0)), 1, steps, 10)
     earlier = choose(group_id == 0, loaded(fields), earlier)
-    own_side = spread(rhs_ref[...])
-    value = choose(group_id == 0, own_side, coarse(earlier, own_side))
     copies = []
 
     def emit(source, target):
         copies.append(pltpu.make_async_copy(source, target, sems.at[len(copies)]))
         copies[-1].start()
 
-    unpack_to(value_ref, value)
-    emit(value_ref, value_out.at[0])
-
     def right_side(j):
         return jnp.where(j == 0, first_ref[...], shares_ref[j])
 
     prior = chain(middle, right_side, earlier, 0, member, 3)
-    side = spread(right_side(member))
-    updated = middle(prior, side)
+    updated = middle(prior, spread(right_side(member)))
+    own_side = spread(rhs_ref[...])
+    value = choose(group_id == 0, own_side, coarse(earlier, own_side))
     closing = member == GROUP - 1
-    unpack_to(points_ref.at[STEPS_DEV - 1], choose(closing, value, updated))
-    emit(points_ref.at[STEPS_DEV - 1], points_out.at[STEPS_DEV - 1])
-    unpack_to(defect_ref, choose(closing, minus(updated, value), minus(value, value)))
-    emit(defect_ref, defect_out.at[0])
     state = prior
     for i in range(STEPS_DEV - 1):
         state = fine(state)
         unpack_to(points_ref.at[i], state)
         emit(points_ref.at[i], points_out.at[i])
+        if i == 0:
+            unpack_to(value_ref, value)
+            emit(value_ref, value_out.at[0])
+            unpack_to(points_ref.at[STEPS_DEV - 1], choose(closing, value, updated))
+            emit(points_ref.at[STEPS_DEV - 1], points_out.at[STEPS_DEV - 1])
+            unpack_to(defect_ref, choose(closing, minus(updated, value), minus(value, value)))
+            emit(defect_ref, defect_out.at[0])
     for copy in copies:
         copy.wait()
 

time: 80.3 us -> 80.3 us (level)
  no operation moved by 1% of the time
where the time goes in v9:
time: 80.3 us; the launch traced here: 79 us
  blocking collectives  43.4 us (54%)
  Pallas kernels  21.3 us (27%)
  starting transfers between devices  6.19 us (8%)
  waiting for transfers between devices  5.4 us (7%)
  local copies, waits for them, and re-layouts  1.96 us (2%)
    all_to_all x1, blocking collectives, shards(): parts = lax.all_to_all(parts, 'tm', 0, 0, axis_index_groups=across)  23.5 us
    pallas_call x3, Pallas kernels, call(): pl.pallas_call(kernel, out_shape=[jax.ShapeDtypeStruct(s, jnp.float32) fo...  21.2 us
    all_gather x1, blocking collectives, shards(): shares = lax.all_gather(share, 'tm', axis_index_groups=inside)  17.3 us
    ppermute x1, waiting for transfers between devices, shards(): far = lax.ppermute(own, 'tm', [(i, i + 2) for i in range(devices - 2)])  5.39 us
    ppermute x1, starting transfers between devices, shards(): far = lax.ppermute(own, 'tm', [(i, i + 2) for i in range(devices - 2)])  4.28 us
    all_gather x1, blocking collectives, shards(): sides = lax.all_gather(parts[:groups - 1], 'tm', axis_index_groups=cores)  2.53 us
    unnamed x12, local copies, waits for them, and re-layouts  1.93 us
    ppermute x1, starting transfers between devices, shards(): near = lax.ppermute(own, 'tm', [(i, i + 1) for i in range(devices - 1)])  1.91 us
  transfers between devices with their start and end apart: 2, of which 1 were waited for; matrix products, arithmetic and copies ran while one was open for 0% of the time, Pallas kernels for 3%

profile of v9, /device:TPU:62, one launch (start us, length us, event | category | flops | bytes accessed | tf_op | source)
XLA Modules:
  0.0 79.0 jit_solution(4676239108826382150)
XLA Ops:
  0.6 4.3 %collective-permute-start = (f32[2,64,64]{2,1,0:T(8,128)}, f32[2,64,64]{2,1,0:T(8,128)S(1)}, u32[]{:S(2)}, u32[]{:S(2)}) collective-permute-start(f32[2,64,64]{2,1,0:T(8,128)} %bitcast.11), channel_id=1, source_target_pairs={{0,2},{1,3},{2,4},{3,5},{4,6},{5,7},{6,8},{7,9},{8,10},{9,11},{10,... | collective-permute-start | bytes 98312 | tf_op jit(solution)/shard_map/ppermute | solution.py:324
  4.9 0.0 copy-start.1
  4.9 1.1 %copy-done.1 = bf16[256,1664]{1,0:T(8,128)(2,1)S(1)} copy-done((bf16[256,1664]{1,0:T(8,128)(2,1)S(1)}, bf16[256,1664]{1,0:T(8,128)(2,1)}, u32[]{:S(2)}) %copy-start.1) | copy-done | bytes 851992
  6.1 0.0 copy-start.5
  6.1 0.0 copy-start.2
  6.1 0.0 copy-start.3
  6.1 0.0 copy-start.4
  6.1 0.1 shard_map.93.near_table
  6.2 0.8 copy-done.5
  6.9 1.9 %collective-permute-start.1 = (f32[2,64,64]{2,1,0:T(8,128)S(1)}, f32[2,64,64]{2,1,0:T(8,128)S(1)}, u32[]{:S(2)}, u32[]{:S(2)}) collective-permute-start(f32[2,64,64]{2,1,0:T(8,128)S(1)} %bitcast.12), channel_id=1, source_target_pairs={{0,1},{1,2},{2,3},{3,4},{4,5},{5,6},{6,7},{7,8},{8,9},{9,10},{10,1... | collective-permute-start | bytes 98312 | tf_op jit(solution)/shard_map/ppermute | solution.py:336
  8.8 0.0 copy-done.2
  8.8 0.0 copy-done.3
  8.9 0.0 copy-done.4
  8.9 0.0 copy-start
  8.9 5.4 %collective-permute-done.far_ref = f32[2,64,64]{2,1,0:T(8,128)S(1)} collective-permute-done((f32[2,64,64]{2,1,0:T(8,128)}, f32[2,64,64]{2,1,0:T(8,128)S(1)}, u32[]{:S(2)}, u32[]{:S(2)}) %collective-permute-start) | collective-permute-done | bytes 32800 | tf_op jit(solution)/shard_map/ppermute | solution.py:324
  14.3 2.6 %shard_map.94 = (f32[64,128]{1,0:T(8,128)S(1)}, f32[64,128]{1,0:T(8,128)S(1)}) custom-call(f32[2,64,64]{2,1,0:T(8,128)S(1)} %collective-permute-done.far_ref, f32[4,64,64]{2,1,0:T(8,128)S(1)} %pad_maximum_fusion.fields, bf16[256,1664]{1,0:T(8,128)(2,1)S(1)} %shard_map.93.near_table), custom_call_target="tpu_custom_call" | custom-call | tf_op jit(solution)/shard_map/pallas_call | solution.py:309
  16.9 17.3 %all-gather = f32[1024,128]{1,0:T(8,128)S(1)} all-gather(f32[64,128]{1,0:T(8,128)S(1)} %get-tuple-element.16), channel_id=2, replica_groups={{0,1,2,3,4,5,6,7,8,9,10,11,12,13,14,15},{16,17,18,19,20,21,22,23,24,25,..., dimensions={0}, use_global_device_ids=true | all-gather | bytes 557056 | tf_op jit(solution)/shard_map/all_gather | solution.py:339
  34.2 0.0 collective-permute-done.1.near_ref
  34.2 0.0 copy-done
  34.2 6.5 %shard_map.95 = (f32[64,128]{1,0:T(8,128)S(1)}, f32[64,128]{1,0:T(8,128)S(1)}, f32[32,32,128]{2,1,0:T(8,128)S(1)}, f32[2,64,64]{2,1,0:T(8,128)}) custom-call(f32[16,64,128]{2,1,0:T(8,128)S(1)} %bitcast.6, f32[2,64,64]{2,1,0:T(8,128)S(1)} %collective-permute-done.1.near_ref, f32[64,128]{1,0:T(8,128)S(1)} %get-tuple-element.18.arrived_ref, ...), custom_call_target="tpu_custom_call" | custom-call | tf_op jit(solution)/shard_map/pallas_call | solution.py:309
  40.8 23.5 %all_to_all.5 = f32[32,32,128]{2,1,0:T(8,128)S(1)} all-to-all(f32[32,32,128]{2,1,0:T(8,128)S(1)} %get-tuple-element.19), channel_id=1, replica_groups={{0,16,32,48,64,80,96,112,128,144,160,176,192,208,224,240,256,272,288,30..., dimensions={0} | all-to-all | bytes 1048576 | tf_op jit(solution)/shard_map/all_to_all | solution.py:350
  64.4 2.5 %all-gather.1 = f32[62,32,128]{2,1,0:T(8,128)S(1)} all-gather(f32[31,32,128]{2,1,0:T(8,128)S(1)} %slice.4), channel_id=3, replica_groups={{0,1},{2,3},{4,5},{6,7},{8,9},{10,11},{12,13},{14,15},{16,17},{18,19},{..., dimensions={0}, use_global_device_ids=true | all-gather | bytes 1523712 | tf_op jit(solution)/shard_map/all_gather | solution.py:352
  66.9 12.1 %shard_map.96 = (f32[4,2,64,64]{3,2,1,0:T(8,128)}, f32[1,2,64,64]{3,2,1,0:T(8,128)}, f32[1,2,64,64]{3,2,1,0:T(8,128)}) custom-call(f32[2,31,32,128]{3,2,1,0:T(8,128)S(1)} %bitcast.8, f32[64,128]{1,0:T(8,128)S(1)} %get-tuple-element.20.rhs_ref, f32[16,64,128]{2,1,0:T(8,128)S(1)} %bitcast.7, f32[64,128]{1,0:T(8,128)S(1)} %get-tuple-element.21.first_ref, ...), custom_call_target="tpu_custom_call" | custom-call | tf_op jit(solution)/shard_map/pallas_call | solution.py:309
  (2 shorter events, 0.0 us)
Async XLA Ops:
  0.6 13.7 %collective-permute-start = (f32[2,64,64]{2,1,0:T(8,128)}, f32[2,64,64]{2,1,0:T(8,128)S(1)}, u32[]{:S(2)}, u32[]{:S(2)}) collective-permute-start(f32[2,64,64]{2,1,0:T(8,128)} %bitcast.11), channel_id=1, source_target_pairs={{0,2},{1,3},{2,4},{3,5},{4,6},{5,7},{6,8},{7,9},{8,10},{9,11},{10,... | collective-permute-start | bytes 98312 | tf_op jit(solution)/shard_map/ppermute | solution.py:324
  4.9 1.2 %copy-start.1 = (bf16[256,1664]{1,0:T(8,128)(2,1)S(1)}, bf16[256,1664]{1,0:T(8,128)(2,1)}, u32[]{:S(2)}) copy-start(bf16[256,1664]{1,0:T(8,128)(2,1)} %constant.5.clone.source) | copy-start | bytes 2555908
  6.1 0.8 %copy-start.5 = (f32[1,2,64,64]{3,2,1,0:T(8,128)S(1)}, f32[1,2,64,64]{3,2,1,0:T(8,128)}, u32[]{:S(2)}) copy-start(f32[1,2,64,64]{3,2,1,0:T(8,128)} %param.7) | copy-start | bytes 98308
  6.1 2.8 %copy-start.2 = (f32[2,64,64]{2,1,0:T(8,128)S(1)}, f32[2,64,64]{2,1,0:T(8,128)}, u32[]{:S(2)}) copy-start(f32[2,64,64]{2,1,0:T(8,128)} %param.6) | copy-start | bytes 98308
  6.1 2.8 %copy-start.3 = (f32[64,64]{1,0:T(8,128)S(1)}, f32[64,64]{1,0:T(8,128)}, u32[]{:S(2)}) copy-start(f32[64,64]{1,0:T(8,128)} %param.9) | copy-start | bytes 49156
  6.1 2.8 %copy-start.4 = (f32[64,64]{1,0:T(8,128)S(1)}, f32[64,64]{1,0:T(8,128)}, u32[]{:S(2)}) copy-start(f32[64,64]{1,0:T(8,128)} %param.8) | copy-start | bytes 49156
  6.9 27.3 %collective-permute-start.1 = (f32[2,64,64]{2,1,0:T(8,128)S(1)}, f32[2,64,64]{2,1,0:T(8,128)S(1)}, u32[]{:S(2)}, u32[]{:S(2)}) collective-permute-start(f32[2,64,64]{2,1,0:T(8,128)S(1)} %bitcast.12), channel_id=1, source_target_pairs={{0,1},{1,2},{2,3},{3,4},{4,5},{5,6},{6,7},{7,8},{8,9},{9,10},{10,1... | collective-permute-start | bytes 98312 | tf_op jit(solution)/shard_map/ppermute | solution.py:336
  8.9 25.3 %copy-start = (bf16[256,1536]{1,0:T(8,128)(2,1)S(1)}, bf16[256,1536]{1,0:T(8,128)(2,1)}, u32[]{:S(2)}) copy-start(bf16[256,1536]{1,0:T(8,128)(2,1)} %constant.4.clone.far_table) | copy-start | bytes 2359300

commit v10 on v9

--- a/solution.py
+++ b/solution.py
@@ -171,14 +171,14 @@
 
         def step(state, extra=None):
             values = react(state)
-            sums = [a + b for a, b in solve(values)]
+            solved = solve(values)
             if extra is not None:
-                sums = [a + b for a, b in zip(sums, extra)]
-            return tuple(a + b for a, b in zip(values, sums))
+                values = plus(values, extra)
+            return tuple((value + right) + left for value, (right, left) in zip(values, solved))
 
         def step_two(one, other):
             values = [jnp.concatenate(pair, 0) for pair in zip(react(one), react(other))]
-            values = [a + (b + c) for a, (b, c) in zip(values, solve(values))]
+            values = [(a + b) + c for a, (b, c) in zip(values, solve(values))]
             return tuple(v[:GRID] for v in values), tuple(v[GRID:] for v in values)
 
         step.two = step_two
@@ -248,7 +248,7 @@
     residual_copy.start()
     leap, handed = middle(start), coarse(start)
     first_ref[...] = merge(minus(state, leap))
-    state = chain(middle, lambda j: shares_ref[j], state, 1, GROUP - 1, 5)
+    state = chain(middle, lambda j: shares_ref[j], state, 1, GROUP - 1, GROUP - 1)
     rhs = merge(choose(position < GROUP, state, minus(state, handed)))
     rhs_ref[...] = rhs
     part = jnp.where(position % 2 == 0, rhs[: GRID // 2], rhs[GRID // 2 :])

time: 80.3 us -> 79.8 us (level)
  no operation moved by 1% of the time
where the time goes in v10:
time: 79.8 us; the launch traced here: 78.5 us
  blocking collectives  43.4 us (54%)
  Pallas kernels  20.8 us (26%)
  starting transfers between devices  6.19 us (8%)
  waiting for transfers between devices  5.4 us (7%)
  local copies, waits for them, and re-layouts  1.96 us (2%)
    all_to_all x1, blocking collectives, shards(): parts = lax.all_to_all(parts, 'tm', 0, 0, axis_index_groups=across)  23.5 us
    pallas_call x3, Pallas kernels, call(): pl.pallas_call(kernel, out_shape=[jax.ShapeDtypeStruct(s, jnp.float32) fo...  20.8 us
    all_gather x1, blocking collectives, shards(): shares = lax.all_gather(share, 'tm', axis_index_groups=inside)  17.3 us
    ppermute x1, waiting for transfers between devices, shards(): far = lax.ppermute(own, 'tm', [(i, i + 2) for i in range(devices - 2)])  5.39 us
    ppermute x1, starting transfers between devices, shards(): far = lax.ppermute(own, 'tm', [(i, i + 2) for i in range(devices - 2)])  4.28 us
    all_gather x1, blocking collectives, shards(): sides = lax.all_gather(parts[:groups - 1], 'tm', axis_index_groups=cores)  2.53 us
    unnamed x12, local copies, waits for them, and re-layouts  1.93 us
    ppermute x1, starting transfers between devices, shards(): near = lax.ppermute(own, 'tm', [(i, i + 1) for i in range(devices - 1)])  1.91 us
  transfers between devices with their start and end apart: 2, of which 1 were waited for; matrix products, arithmetic and copies ran while one was open for 0% of the time, Pallas kernels for 3%

profile of v10, /device:TPU:62, one launch (start us, length us, event | category | flops | bytes accessed | tf_op | source)
XLA Modules:
  0.0 78.5 jit_solution(8129543962271417412)
XLA Ops:
  0.6 4.3 %collective-permute-start = (f32[2,64,64]{2,1,0:T(8,128)}, f32[2,64,64]{2,1,0:T(8,128)S(1)}, u32[]{:S(2)}, u32[]{:S(2)}) collective-permute-start(f32[2,64,64]{2,1,0:T(8,128)} %bitcast.11), channel_id=1, source_target_pairs={{0,2},{1,3},{2,4},{3,5},{4,6},{5,7},{6,8},{7,9},{8,10},{9,11},{10,... | collective-permute-start | bytes 98312 | tf_op jit(solution)/shard_map/ppermute | solution.py:324
  4.9 0.0 copy-start.1
  4.9 1.1 %copy-done.1 = bf16[256,1664]{1,0:T(8,128)(2,1)S(1)} copy-done((bf16[256,1664]{1,0:T(8,128)(2,1)S(1)}, bf16[256,1664]{1,0:T(8,128)(2,1)}, u32[]{:S(2)}) %copy-start.1) | copy-done | bytes 851992
  6.1 0.0 copy-start.5
  6.1 0.0 copy-start.2
  6.1 0.0 copy-start.3
  6.1 0.0 copy-start.4
  6.1 0.1 shard_map.93.near_table
  6.2 0.8 copy-done.5
  6.9 1.9 %collective-permute-start.1 = (f32[2,64,64]{2,1,0:T(8,128)S(1)}, f32[2,64,64]{2,1,0:T(8,128)S(1)}, u32[]{:S(2)}, u32[]{:S(2)}) collective-permute-start(f32[2,64,64]{2,1,0:T(8,128)S(1)} %bitcast.12), channel_id=1, source_target_pairs={{0,1},{1,2},{2,3},{3,4},{4,5},{5,6},{6,7},{7,8},{8,9},{9,10},{10,1... | collective-permute-start | bytes 98312 | tf_op jit(solution)/shard_map/ppermute | solution.py:336
  8.8 0.0 copy-done.2
  8.8 0.0 copy-done.3
  8.9 0.0 copy-done.4
  8.9 0.0 copy-start
  8.9 5.4 %collective-permute-done.far_ref = f32[2,64,64]{2,1,0:T(8,128)S(1)} collective-permute-done((f32[2,64,64]{2,1,0:T(8,128)}, f32[2,64,64]{2,1,0:T(8,128)S(1)}, u32[]{:S(2)}, u32[]{:S(2)}) %collective-permute-start) | collective-permute-done | bytes 32800 | tf_op jit(solution)/shard_map/ppermute | solution.py:324
  14.3 2.5 %shard_map.94 = (f32[64,128]{1,0:T(8,128)S(1)}, f32[64,128]{1,0:T(8,128)S(1)}) custom-call(f32[2,64,64]{2,1,0:T(8,128)S(1)} %collective-permute-done.far_ref, f32[4,64,64]{2,1,0:T(8,128)S(1)} %pad_maximum_fusion.fields, bf16[256,1664]{1,0:T(8,128)(2,1)S(1)} %shard_map.93.near_table), custom_call_target="tpu_custom_call" | custom-call | tf_op jit(solution)/shard_map/pallas_call | solution.py:309
  16.8 17.3 %all-gather = f32[1024,128]{1,0:T(8,128)S(1)} all-gather(f32[64,128]{1,0:T(8,128)S(1)} %get-tuple-element.16), channel_id=2, replica_groups={{0,1,2,3,4,5,6,7,8,9,10,11,12,13,14,15},{16,17,18,19,20,21,22,23,24,25,..., dimensions={0}, use_global_device_ids=true | all-gather | bytes 557056 | tf_op jit(solution)/shard_map/all_gather | solution.py:339
  34.1 0.0 collective-permute-done.1.near_ref
  34.1 0.0 copy-done
  34.1 6.3 %shard_map.95 = (f32[64,128]{1,0:T(8,128)S(1)}, f32[64,128]{1,0:T(8,128)S(1)}, f32[32,32,128]{2,1,0:T(8,128)S(1)}, f32[2,64,64]{2,1,0:T(8,128)}) custom-call(f32[16,64,128]{2,1,0:T(8,128)S(1)} %bitcast.6, f32[2,64,64]{2,1,0:T(8,128)S(1)} %collective-permute-done.1.near_ref, f32[64,128]{1,0:T(8,128)S(1)} %get-tuple-element.18.arrived_ref, ...), custom_call_target="tpu_custom_call" | custom-call | tf_op jit(solution)/shard_map/pallas_call | solution.py:309
  40.4 23.5 %all_to_all.5 = f32[32,32,128]{2,1,0:T(8,128)S(1)} all-to-all(f32[32,32,128]{2,1,0:T(8,128)S(1)} %get-tuple-element.19), channel_id=1, replica_groups={{0,16,32,48,64,80,96,112,128,144,160,176,192,208,224,240,256,272,288,30..., dimensions={0} | all-to-all | bytes 1048576 | tf_op jit(solution)/shard_map/all_to_all | solution.py:350
  64.0 2.5 %all-gather.1 = f32[62,32,128]{2,1,0:T(8,128)S(1)} all-gather(f32[31,32,128]{2,1,0:T(8,128)S(1)} %slice.4), channel_id=3, replica_groups={{0,1},{2,3},{4,5},{6,7},{8,9},{10,11},{12,13},{14,15},{16,17},{18,19},{..., dimensions={0}, use_global_device_ids=true | all-gather | bytes 1523712 | tf_op jit(solution)/shard_map/all_gather | solution.py:352
  66.5 12.0 %shard_map.96 = (f32[4,2,64,64]{3,2,1,0:T(8,128)}, f32[1,2,64,64]{3,2,1,0:T(8,128)}, f32[1,2,64,64]{3,2,1,0:T(8,128)}) custom-call(f32[2,31,32,128]{3,2,1,0:T(8,128)S(1)} %bitcast.8, f32[64,128]{1,0:T(8,128)S(1)} %get-tuple-element.20.rhs_ref, f32[16,64,128]{2,1,0:T(8,128)S(1)} %bitcast.7, f32[64,128]{1,0:T(8,128)S(1)} %get-tuple-element.21.first_ref, ...), custom_call_target="tpu_custom_call" | custom-call | tf_op jit(solution)/shard_map/pallas_call | solution.py:309
  (2 shorter events, 0.0 us)
Async XLA Ops:
  0.6 13.7 %collective-permute-start = (f32[2,64,64]{2,1,0:T(8,128)}, f32[2,64,64]{2,1,0:T(8,128)S(1)}, u32[]{:S(2)}, u32[]{:S(2)}) collective-permute-start(f32[2,64,64]{2,1,0:T(8,128)} %bitcast.11), channel_id=1, source_target_pairs={{0,2},{1,3},{2,4},{3,5},{4,6},{5,7},{6,8},{7,9},{8,10},{9,11},{10,... | collective-permute-start | bytes 98312 | tf_op jit(solution)/shard_map/ppermute | solution.py:324
  4.9 1.2 %copy-start.1 = (bf16[256,1664]{1,0:T(8,128)(2,1)S(1)}, bf16[256,1664]{1,0:T(8,128)(2,1)}, u32[]{:S(2)}) copy-start(bf16[256,1664]{1,0:T(8,128)(2,1)} %constant.5.clone.source) | copy-start | bytes 2555908
  6.1 0.8 %copy-start.5 = (f32[1,2,64,64]{3,2,1,0:T(8,128)S(1)}, f32[1,2,64,64]{3,2,1,0:T(8,128)}, u32[]{:S(2)}) copy-start(f32[1,2,64,64]{3,2,1,0:T(8,128)} %param.7) | copy-start | bytes 98308
  6.1 2.8 %copy-start.2 = (f32[2,64,64]{2,1,0:T(8,128)S(1)}, f32[2,64,64]{2,1,0:T(8,128)}, u32[]{:S(2)}) copy-start(f32[2,64,64]{2,1,0:T(8,128)} %param.6) | copy-start | bytes 98308
  6.1 2.8 %copy-start.3 = (f32[64,64]{1,0:T(8,128)S(1)}, f32[64,64]{1,0:T(8,128)}, u32[]{:S(2)}) copy-start(f32[64,64]{1,0:T(8,128)} %param.9) | copy-start | bytes 49156
  6.1 2.8 %copy-start.4 = (f32[64,64]{1,0:T(8,128)S(1)}, f32[64,64]{1,0:T(8,128)}, u32[]{:S(2)}) copy-start(f32[64,64]{1,0:T(8,128)} %param.8) | copy-start | bytes 49156
  6.9 27.2 %collective-permute-start.1 = (f32[2,64,64]{2,1,0:T(8,128)S(1)}, f32[2,64,64]{2,1,0:T(8,128)S(1)}, u32[]{:S(2)}, u32[]{:S(2)}) collective-permute-start(f32[2,64,64]{2,1,0:T(8,128)S(1)} %bitcast.12), channel_id=1, source_target_pairs={{0,1},{1,2},{2,3},{3,4},{4,5},{5,6},{6,7},{7,8},{8,9},{9,10},{10,1... | collective-permute-start | bytes 98312 | tf_op jit(solution)/shard_map/ppermute | solution.py:336
  8.9 25.2 %copy-start = (bf16[256,1536]{1,0:T(8,128)(2,1)S(1)}, bf16[256,1536]{1,0:T(8,128)(2,1)}, u32[]{:S(2)}) copy-start(bf16[256,1536]{1,0:T(8,128)(2,1)} %constant.4.clone.far_table) | copy-start | bytes 2359300

commit v11 on v10

--- a/solution.py
+++ b/solution.py
@@ -259,7 +259,7 @@
 
 def correct_kernel(
     sides_ref, rhs_ref, shares_ref, first_ref, fields, near_table, far_table,
-    points_out, value_out, defect_out, points_ref, value_ref, defect_ref, sems,
+    points_ref, value_ref, defect_ref,
 ):
     fine, middle, coarse = bound(fields, near_table, far_table)
     position = lax.axis_index("tm")
@@ -271,12 +271,6 @@
     steps = jnp.maximum(group_id - 1, 0)
     earlier = chain(coarse, coarse_side, spread(coarse_side(0)), 1, steps, 10)
     earlier = choose(group_id == 0, loaded(fields), earlier)
-    copies = []
-
-    def emit(source, target):
-        copies.append(pltpu.make_async_copy(source, target, sems.at[len(copies)]))
-        copies[-1].start()
-
     def right_side(j):
         return jnp.where(j == 0, first_ref[...], shares_ref[j])
 
@@ -285,20 +279,13 @@
     own_side = spread(rhs_ref[...])
     value = choose(group_id == 0, own_side, coarse(earlier, own_side))
     closing = member == GROUP - 1
+    unpack_to(value_ref.at[0], value)
+    unpack_to(points_ref.at[STEPS_DEV - 1], choose(closing, value, updated))
+    unpack_to(defect_ref.at[0], choose(closing, minus(updated, value), minus(value, value)))
     state = prior
     for i in range(STEPS_DEV - 1):
         state = fine(state)
         unpack_to(points_ref.at[i], state)
-        emit(points_ref.at[i], points_out.at[i])
-        if i == 0:
-            unpack_to(value_ref, value)
-            emit(value_ref, value_out.at[0])
-            unpack_to(points_ref.at[STEPS_DEV - 1], choose(closing, value, updated))
-            emit(points_ref.at[STEPS_DEV - 1], points_out.at[STEPS_DEV - 1])
-            unpack_to(defect_ref, choose(closing, minus(updated, value), minus(value, value)))
-            emit(defect_ref, defect_out.at[0])
-    for copy in copies:
-        copy.wait()
 
 
 VMEM = pl.BlockSpec(memory_space=pltpu.VMEM)
@@ -350,13 +337,12 @@
     parts = lax.all_to_all(parts, "tm", 0, 0, axis_index_groups=across)
     cores = [[2 * c, 2 * c + 1] for c in range(devices // 2)]
     sides = lax.all_gather(parts[: groups - 1], "tm", axis_index_groups=cores)
-    shapes = [(STEPS_DEV,) + pair, pair, pair]
     points, value, defect = call(
         correct_kernel,
         [(STEPS_DEV,) + pair, (1,) + pair, (1,) + pair],
         [VMEM] * 7,
-        [HBM] * 3,
-        [pltpu.VMEM(s, jnp.float32) for s in shapes] + [pltpu.SemaphoreType.DMA((STEPS_DEV + 2,))],
+        [VMEM] * 3,
+        [],
         sides, rhs, shares, first, fields, near_table, far_table,
     )
     return points, residual[None], value, defect

time: 79.8 us -> 79.8 us (level)
  no operation moved by 1% of the time
where the time goes in v11:
time: 79.8 us; the launch traced here: 78.5 us
  blocking collectives  43.4 us (54%)
  Pallas kernels  20.9 us (26%)
  starting transfers between devices  6.19 us (8%)
  waiting for transfers between devices  5.4 us (7%)
  local copies, waits for them, and re-layouts  1.96 us (2%)
    all_to_all x1, blocking collectives, shards(): parts = lax.all_to_all(parts, 'tm', 0, 0, axis_index_groups=across)  23.5 us
    pallas_call x3, Pallas kernels, call(): pl.pallas_call(kernel, out_shape=[jax.ShapeDtypeStruct(s, jnp.float32) fo...  20.8 us
    all_gather x1, blocking collectives, shards(): shares = lax.all_gather(share, 'tm', axis_index_groups=inside)  17.3 us
    ppermute x1, waiting for transfers between devices, shards(): far = lax.ppermute(own, 'tm', [(i, i + 2) for i in range(devices - 2)])  5.39 us
    ppermute x1, starting transfers between devices, shards(): far = lax.ppermute(own, 'tm', [(i, i + 2) for i in range(devices - 2)])  4.28 us
    all_gather x1, blocking collectives, shards(): sides = lax.all_gather(parts[:groups - 1], 'tm', axis_index_groups=cores)  2.53 us
    unnamed x12, local copies, waits for them, and re-layouts  1.93 us
    ppermute x1, starting transfers between devices, shards(): near = lax.ppermute(own, 'tm', [(i, i + 1) for i in range(devices - 1)])  1.91 us
  transfers between devices with their start and end apart: 2, of which 1 were waited for; matrix products, arithmetic and copies ran while one was open for 0% of the time, Pallas kernels for 3%

profile of v11, /device:TPU:62, one launch (start us, length us, event | category | flops | bytes accessed | tf_op | source)
XLA Modules:
  0.0 78.5 jit_solution(9519605988705902477)
XLA Ops:
  0.6 4.3 %collective-permute-start = (f32[2,64,64]{2,1,0:T(8,128)}, f32[2,64,64]{2,1,0:T(8,128)S(1)}, u32[]{:S(2)}, u32[]{:S(2)}) collective-permute-start(f32[2,64,64]{2,1,0:T(8,128)} %bitcast.11), channel_id=1, source_target_pairs={{0,2},{1,3},{2,4},{3,5},{4,6},{5,7},{6,8},{7,9},{8,10},{9,11},{10,... | collective-permute-start | bytes 98312 | tf_op jit(solution)/shard_map/ppermute | solution.py:311
  4.9 0.0 copy-start.1
  4.9 1.1 %copy-done.1 = bf16[256,1664]{1,0:T(8,128)(2,1)S(1)} copy-done((bf16[256,1664]{1,0:T(8,128)(2,1)S(1)}, bf16[256,1664]{1,0:T(8,128)(2,1)}, u32[]{:S(2)}) %copy-start.1) | copy-done | bytes 851992
  6.1 0.0 copy-start.5
  6.1 0.0 copy-start.2
  6.1 0.0 copy-start.3
  6.1 0.0 copy-start.4
  6.1 0.1 shard_map.93.near_table
  6.2 0.8 copy-done.5
  6.9 1.9 %collective-permute-start.1 = (f32[2,64,64]{2,1,0:T(8,128)S(1)}, f32[2,64,64]{2,1,0:T(8,128)S(1)}, u32[]{:S(2)}, u32[]{:S(2)}) collective-permute-start(f32[2,64,64]{2,1,0:T(8,128)S(1)} %bitcast.12), channel_id=1, source_target_pairs={{0,1},{1,2},{2,3},{3,4},{4,5},{5,6},{6,7},{7,8},{8,9},{9,10},{10,1... | collective-permute-start | bytes 98312 | tf_op jit(solution)/shard_map/ppermute | solution.py:323
  8.8 0.0 copy-done.2
  8.8 0.0 copy-done.3
  8.9 0.0 copy-done.4
  8.9 0.0 copy-start
  8.9 5.4 %collective-permute-done.far_ref = f32[2,64,64]{2,1,0:T(8,128)S(1)} collective-permute-done((f32[2,64,64]{2,1,0:T(8,128)}, f32[2,64,64]{2,1,0:T(8,128)S(1)}, u32[]{:S(2)}, u32[]{:S(2)}) %collective-permute-start) | collective-permute-done | bytes 32800 | tf_op jit(solution)/shard_map/ppermute | solution.py:311
  14.3 2.5 %shard_map.94 = (f32[64,128]{1,0:T(8,128)S(1)}, f32[64,128]{1,0:T(8,128)S(1)}) custom-call(f32[2,64,64]{2,1,0:T(8,128)S(1)} %collective-permute-done.far_ref, f32[4,64,64]{2,1,0:T(8,128)S(1)} %pad_maximum_fusion.fields, bf16[256,1664]{1,0:T(8,128)(2,1)S(1)} %shard_map.93.near_table), custom_call_target="tpu_custom_call" | custom-call | tf_op jit(solution)/shard_map/pallas_call | solution.py:296
  16.8 17.3 %all-gather = f32[1024,128]{1,0:T(8,128)S(1)} all-gather(f32[64,128]{1,0:T(8,128)S(1)} %get-tuple-element.16), channel_id=2, replica_groups={{0,1,2,3,4,5,6,7,8,9,10,11,12,13,14,15},{16,17,18,19,20,21,22,23,24,25,..., dimensions={0}, use_global_device_ids=true | all-gather | bytes 557056 | tf_op jit(solution)/shard_map/all_gather | solution.py:326
  34.1 0.0 collective-permute-done.1.near_ref
  34.1 0.0 copy-done
  34.1 6.3 %shard_map.95 = (f32[64,128]{1,0:T(8,128)S(1)}, f32[64,128]{1,0:T(8,128)S(1)}, f32[32,32,128]{2,1,0:T(8,128)S(1)}, f32[2,64,64]{2,1,0:T(8,128)}) custom-call(f32[16,64,128]{2,1,0:T(8,128)S(1)} %bitcast.6, f32[2,64,64]{2,1,0:T(8,128)S(1)} %collective-permute-done.1.near_ref, f32[64,128]{1,0:T(8,128)S(1)} %get-tuple-element.18.arrived_ref, ...), custom_call_target="tpu_custom_call" | custom-call | tf_op jit(solution)/shard_map/pallas_call | solution.py:296
  40.4 23.5 %all_to_all.5 = f32[32,32,128]{2,1,0:T(8,128)S(1)} all-to-all(f32[32,32,128]{2,1,0:T(8,128)S(1)} %get-tuple-element.19), channel_id=1, replica_groups={{0,16,32,48,64,80,96,112,128,144,160,176,192,208,224,240,256,272,288,30..., dimensions={0} | all-to-all | bytes 1048576 | tf_op jit(solution)/shard_map/all_to_all | solution.py:337
  64.0 2.5 %all-gather.1 = f32[62,32,128]{2,1,0:T(8,128)S(1)} all-gather(f32[31,32,128]{2,1,0:T(8,128)S(1)} %slice.4), channel_id=3, replica_groups={{0,1},{2,3},{4,5},{6,7},{8,9},{10,11},{12,13},{14,15},{16,17},{18,19},{..., dimensions={0}, use_global_device_ids=true | all-gather | bytes 1523712 | tf_op jit(solution)/shard_map/all_gather | solution.py:339
  66.5 12.0 %shard_map.96 = (f32[4,2,64,64]{3,2,1,0:T(8,128)}, f32[1,2,64,64]{3,2,1,0:T(8,128)}, f32[1,2,64,64]{3,2,1,0:T(8,128)}) custom-call(f32[2,31,32,128]{3,2,1,0:T(8,128)S(1)} %bitcast.8, f32[64,128]{1,0:T(8,128)S(1)} %get-tuple-element.20.rhs_ref, f32[16,64,128]{2,1,0:T(8,128)S(1)} %bitcast.7, f32[64,128]{1,0:T(8,128)S(1)} %get-tuple-element.21.first_ref, ...), custom_call_target="tpu_custom_call" | custom-call | tf_op jit(solution)/shard_map/pallas_call | solution.py:296
  (2 shorter events, 0.0 us)
Async XLA Ops:
  0.6 13.7 %collective-permute-start = (f32[2,64,64]{2,1,0:T(8,128)}, f32[2,64,64]{2,1,0:T(8,128)S(1)}, u32[]{:S(2)}, u32[]{:S(2)}) collective-permute-start(f32[2,64,64]{2,1,0:T(8,128)} %bitcast.11), channel_id=1, source_target_pairs={{0,2},{1,3},{2,4},{3,5},{4,6},{5,7},{6,8},{7,9},{8,10},{9,11},{10,... | collective-permute-start | bytes 98312 | tf_op jit(solution)/shard_map/ppermute | solution.py:311
  4.9 1.2 %copy-start.1 = (bf16[256,1664]{1,0:T(8,128)(2,1)S(1)}, bf16[256,1664]{1,0:T(8,128)(2,1)}, u32[]{:S(2)}) copy-start(bf16[256,1664]{1,0:T(8,128)(2,1)} %constant.5.clone.source) | copy-start | bytes 2555908
  6.1 0.8 %copy-start.5 = (f32[1,2,64,64]{3,2,1,0:T(8,128)S(1)}, f32[1,2,64,64]{3,2,1,0:T(8,128)}, u32[]{:S(2)}) copy-start(f32[1,2,64,64]{3,2,1,0:T(8,128)} %param.7) | copy-start | bytes 98308
  6.1 2.8 %copy-start.2 = (f32[2,64,64]{2,1,0:T(8,128)S(1)}, f32[2,64,64]{2,1,0:T(8,128)}, u32[]{:S(2)}) copy-start(f32[2,64,64]{2,1,0:T(8,128)} %param.6) | copy-start | bytes 98308
  6.1 2.8 %copy-start.3 = (f32[64,64]{1,0:T(8,128)S(1)}, f32[64,64]{1,0:T(8,128)}, u32[]{:S(2)}) copy-start(f32[64,64]{1,0:T(8,128)} %param.9) | copy-start | bytes 49156
  6.1 2.8 %copy-start.4 = (f32[64,64]{1,0:T(8,128)S(1)}, f32[64,64]{1,0:T(8,128)}, u32[]{:S(2)}) copy-start(f32[64,64]{1,0:T(8,128)} %param.8) | copy-start | bytes 49156
  6.9 27.2 %collective-permute-start.1 = (f32[2,64,64]{2,1,0:T(8,128)S(1)}, f32[2,64,64]{2,1,0:T(8,128)S(1)}, u32[]{:S(2)}, u32[]{:S(2)}) collective-permute-start(f32[2,64,64]{2,1,0:T(8,128)S(1)} %bitcast.12), channel_id=1, source_target_pairs={{0,1},{1,2},{2,3},{3,4},{4,5},{5,6},{6,7},{7,8},{8,9},{9,10},{10,1... | collective-permute-start | bytes 98312 | tf_op jit(solution)/shard_map/ppermute | solution.py:323
  8.9 25.2 %copy-start = (bf16[256,1536]{1,0:T(8,128)(2,1)S(1)}, bf16[256,1536]{1,0:T(8,128)(2,1)}, u32[]{:S(2)}) copy-start(bf16[256,1536]{1,0:T(8,128)(2,1)} %constant.4.clone.far_table) | copy-start | bytes 2359300

commit v12 on v10

--- a/solution.py
+++ b/solution.py
@@ -130,12 +130,14 @@
         supply, decay = h * feed, h * (feed + kill)
         wide_at = [start, start + LANES + cross]
         left_at = start + 2 * (LANES + cross)
+        order = (0, 1) if (rank, fine_cross) == (1, 1) else (1, 0)
 
         def solve(values):
             count = values[0].shape[0] // GRID
             rows = [slice(GRID * n, GRID * (n + 1)) for n in range(count)]
             made = []
-            for i, value in enumerate(values):
+            for i in order:
+                value = values[i]
                 high = value.astype(jnp.bfloat16)
                 rest = (value - high.astype(jnp.float32)).astype(jnp.bfloat16)
                 wide = jnp.concatenate([high, rest], 1)
@@ -148,7 +150,7 @@
                     right = None
                 made.append((high, rest, wide, turned, right))
             solved = []
-            for i, (high, rest, wide, turned, right) in enumerate(made):
+            for i, (high, rest, wide, turned, right) in zip(order, made):
                 if not fine_cross:
                     right = product(wide, table[:, wide_at[i] : wide_at[i] + LANES])
                 stack = [high, rest, high]
@@ -162,7 +164,7 @@
                 left = product(table[GRID * i : GRID * (i + 1), left_at : left_at + stack.shape[0]], stack)
                 left = jnp.concatenate([left[:, LANES * n : LANES * (n + 1)] for n in range(count)], 0)
                 solved.append((right, left))
-            return solved
+            return solved[:: order[1] - order[0]]
 
         def react(state):
             sub, cat = state

time: 79.8 us -> 79.8 us (level)
  no operation moved by 1% of the time
where the time goes in v12:
time: 79.8 us; the launch traced here: 78.5 us
  blocking collectives  43.4 us (54%)
  Pallas kernels  20.8 us (26%)
  starting transfers between devices  6.19 us (8%)
  waiting for transfers between devices  5.4 us (7%)
  local copies, waits for them, and re-layouts  1.96 us (2%)
    all_to_all x1, blocking collectives, shards(): parts = lax.all_to_all(parts, 'tm', 0, 0, axis_index_groups=across)  23.5 us
    pallas_call x3, Pallas kernels, call(): pl.pallas_call(kernel, out_shape=[jax.ShapeDtypeStruct(s, jnp.float32) fo...  20.8 us
    all_gather x1, blocking collectives, shards(): shares = lax.all_gather(share, 'tm', axis_index_groups=inside)  17.3 us
    ppermute x1, waiting for transfers between devices, shards(): far = lax.ppermute(own, 'tm', [(i, i + 2) for i in range(devices - 2)])  5.39 us
    ppermute x1, starting transfers between devices, shards(): far = lax.ppermute(own, 'tm', [(i, i + 2) for i in range(devices - 2)])  4.28 us
    all_gather x1, blocking collectives, shards(): sides = lax.all_gather(parts[:groups - 1], 'tm', axis_index_groups=cores)  2.53 us
    unnamed x12, local copies, waits for them, and re-layouts  1.93 us
    ppermute x1, starting transfers between devices, shards(): near = lax.ppermute(own, 'tm', [(i, i + 1) for i in range(devices - 1)])  1.91 us
  transfers between devices with their start and end apart: 2, of which 1 were waited for; matrix products, arithmetic and copies ran while one was open for 0% of the time, Pallas kernels for 3%

profile of v12, /device:TPU:62, one launch (start us, length us, event | category | flops | bytes accessed | tf_op | source)
XLA Modules:
  0.0 78.5 jit_solution(5183280345822443435)
XLA Ops:
  0.6 4.3 %collective-permute-start = (f32[2,64,64]{2,1,0:T(8,128)}, f32[2,64,64]{2,1,0:T(8,128)S(1)}, u32[]{:S(2)}, u32[]{:S(2)}) collective-permute-start(f32[2,64,64]{2,1,0:T(8,128)} %bitcast.11), channel_id=1, source_target_pairs={{0,2},{1,3},{2,4},{3,5},{4,6},{5,7},{6,8},{7,9},{8,10},{9,11},{10,... | collective-permute-start | bytes 98312 | tf_op jit(solution)/shard_map/ppermute | solution.py:326
  4.9 0.0 copy-start.1
  4.9 1.1 %copy-done.1 = bf16[256,1664]{1,0:T(8,128)(2,1)S(1)} copy-done((bf16[256,1664]{1,0:T(8,128)(2,1)S(1)}, bf16[256,1664]{1,0:T(8,128)(2,1)}, u32[]{:S(2)}) %copy-start.1) | copy-done | bytes 851992
  6.1 0.0 copy-start.5
  6.1 0.0 copy-start.2
  6.1 0.0 copy-start.3
  6.1 0.0 copy-start.4
  6.1 0.1 shard_map.93.near_table
  6.2 0.8 copy-done.5
  6.9 1.9 %collective-permute-start.1 = (f32[2,64,64]{2,1,0:T(8,128)S(1)}, f32[2,64,64]{2,1,0:T(8,128)S(1)}, u32[]{:S(2)}, u32[]{:S(2)}) collective-permute-start(f32[2,64,64]{2,1,0:T(8,128)S(1)} %bitcast.12), channel_id=1, source_target_pairs={{0,1},{1,2},{2,3},{3,4},{4,5},{5,6},{6,7},{7,8},{8,9},{9,10},{10,1... | collective-permute-start | bytes 98312 | tf_op jit(solution)/shard_map/ppermute | solution.py:338
  8.8 0.0 copy-done.2
  8.8 0.0 copy-done.3
  8.9 0.0 copy-done.4
  8.9 0.0 copy-start
  8.9 5.4 %collective-permute-done.far_ref = f32[2,64,64]{2,1,0:T(8,128)S(1)} collective-permute-done((f32[2,64,64]{2,1,0:T(8,128)}, f32[2,64,64]{2,1,0:T(8,128)S(1)}, u32[]{:S(2)}, u32[]{:S(2)}) %collective-permute-start) | collective-permute-done | bytes 32800 | tf_op jit(solution)/shard_map/ppermute | solution.py:326
  14.3 2.5 %shard_map.94 = (f32[64,128]{1,0:T(8,128)S(1)}, f32[64,128]{1,0:T(8,128)S(1)}) custom-call(f32[2,64,64]{2,1,0:T(8,128)S(1)} %collective-permute-done.far_ref, f32[4,64,64]{2,1,0:T(8,128)S(1)} %pad_maximum_fusion.fields, bf16[256,1664]{1,0:T(8,128)(2,1)S(1)} %shard_map.93.near_table), custom_call_target="tpu_custom_call" | custom-call | tf_op jit(solution)/shard_map/pallas_call | solution.py:311
  16.8 17.3 %all-gather = f32[1024,128]{1,0:T(8,128)S(1)} all-gather(f32[64,128]{1,0:T(8,128)S(1)} %get-tuple-element.16), channel_id=2, replica_groups={{0,1,2,3,4,5,6,7,8,9,10,11,12,13,14,15},{16,17,18,19,20,21,22,23,24,25,..., dimensions={0}, use_global_device_ids=true | all-gather | bytes 557056 | tf_op jit(solution)/shard_map/all_gather | solution.py:341
  34.1 0.0 collective-permute-done.1.near_ref
  34.1 0.0 copy-done
  34.1 6.3 %shard_map.95 = (f32[64,128]{1,0:T(8,128)S(1)}, f32[64,128]{1,0:T(8,128)S(1)}, f32[32,32,128]{2,1,0:T(8,128)S(1)}, f32[2,64,64]{2,1,0:T(8,128)}) custom-call(f32[16,64,128]{2,1,0:T(8,128)S(1)} %bitcast.6, f32[2,64,64]{2,1,0:T(8,128)S(1)} %collective-permute-done.1.near_ref, f32[64,128]{1,0:T(8,128)S(1)} %get-tuple-element.18.arrived_ref, ...), custom_call_target="tpu_custom_call" | custom-call | tf_op jit(solution)/shard_map/pallas_call | solution.py:311
  40.4 23.5 %all_to_all.5 = f32[32,32,128]{2,1,0:T(8,128)S(1)} all-to-all(f32[32,32,128]{2,1,0:T(8,128)S(1)} %get-tuple-element.19), channel_id=1, replica_groups={{0,16,32,48,64,80,96,112,128,144,160,176,192,208,224,240,256,272,288,30..., dimensions={0} | all-to-all | bytes 1048576 | tf_op jit(solution)/shard_map/all_to_all | solution.py:352
  64.0 2.5 %all-gather.1 = f32[62,32,128]{2,1,0:T(8,128)S(1)} all-gather(f32[31,32,128]{2,1,0:T(8,128)S(1)} %slice.4), channel_id=3, replica_groups={{0,1},{2,3},{4,5},{6,7},{8,9},{10,11},{12,13},{14,15},{16,17},{18,19},{..., dimensions={0}, use_global_device_ids=true | all-gather | bytes 1523712 | tf_op jit(solution)/shard_map/all_gather | solution.py:354
  66.5 12.0 %shard_map.96 = (f32[4,2,64,64]{3,2,1,0:T(8,128)}, f32[1,2,64,64]{3,2,1,0:T(8,128)}, f32[1,2,64,64]{3,2,1,0:T(8,128)}) custom-call(f32[2,31,32,128]{3,2,1,0:T(8,128)S(1)} %bitcast.8, f32[64,128]{1,0:T(8,128)S(1)} %get-tuple-element.20.rhs_ref, f32[16,64,128]{2,1,0:T(8,128)S(1)} %bitcast.7, f32[64,128]{1,0:T(8,128)S(1)} %get-tuple-element.21.first_ref, ...), custom_call_target="tpu_custom_call" | custom-call | tf_op jit(solution)/shard_map/pallas_call | solution.py:311
  (2 shorter events, 0.0 us)
Async XLA Ops:
  0.6 13.7 %collective-permute-start = (f32[2,64,64]{2,1,0:T(8,128)}, f32[2,64,64]{2,1,0:T(8,128)S(1)}, u32[]{:S(2)}, u32[]{:S(2)}) collective-permute-start(f32[2,64,64]{2,1,0:T(8,128)} %bitcast.11), channel_id=1, source_target_pairs={{0,2},{1,3},{2,4},{3,5},{4,6},{5,7},{6,8},{7,9},{8,10},{9,11},{10,... | collective-permute-start | bytes 98312 | tf_op jit(solution)/shard_map/ppermute | solution.py:326
  4.9 1.2 %copy-start.1 = (bf16[256,1664]{1,0:T(8,128)(2,1)S(1)}, bf16[256,1664]{1,0:T(8,128)(2,1)}, u32[]{:S(2)}) copy-start(bf16[256,1664]{1,0:T(8,128)(2,1)} %constant.5.clone.source) | copy-start | bytes 2555908
  6.1 0.8 %copy-start.5 = (f32[1,2,64,64]{3,2,1,0:T(8,128)S(1)}, f32[1,2,64,64]{3,2,1,0:T(8,128)}, u32[]{:S(2)}) copy-start(f32[1,2,64,64]{3,2,1,0:T(8,128)} %param.7) | copy-start | bytes 98308
  6.1 2.8 %copy-start.2 = (f32[2,64,64]{2,1,0:T(8,128)S(1)}, f32[2,64,64]{2,1,0:T(8,128)}, u32[]{:S(2)}) copy-start(f32[2,64,64]{2,1,0:T(8,128)} %param.6) | copy-start | bytes 98308
  6.1 2.8 %copy-start.3 = (f32[64,64]{1,0:T(8,128)S(1)}, f32[64,64]{1,0:T(8,128)}, u32[]{:S(2)}) copy-start(f32[64,64]{1,0:T(8,128)} %param.9) | copy-start | bytes 49156
  6.1 2.8 %copy-start.4 = (f32[64,64]{1,0:T(8,128)S(1)}, f32[64,64]{1,0:T(8,128)}, u32[]{:S(2)}) copy-start(f32[64,64]{1,0:T(8,128)} %param.8) | copy-start | bytes 49156
  6.9 27.2 %collective-permute-start.1 = (f32[2,64,64]{2,1,0:T(8,128)S(1)}, f32[2,64,64]{2,1,0:T(8,128)S(1)}, u32[]{:S(2)}, u32[]{:S(2)}) collective-permute-start(f32[2,64,64]{2,1,0:T(8,128)S(1)} %bitcast.12), channel_id=1, source_target_pairs={{0,1},{1,2},{2,3},{3,4},{4,5},{5,6},{6,7},{7,8},{8,9},{9,10},{10,1... | collective-permute-start | bytes 98312 | tf_op jit(solution)/shard_map/ppermute | solution.py:338
  8.9 25.3 %copy-start = (bf16[256,1536]{1,0:T(8,128)(2,1)S(1)}, bf16[256,1536]{1,0:T(8,128)(2,1)}, u32[]{:S(2)}) copy-start(bf16[256,1536]{1,0:T(8,128)(2,1)} %constant.4.clone.far_table) | copy-start | bytes 2359300

commit v13 on v10

--- a/solution.py
+++ b/solution.py
@@ -229,7 +229,7 @@
         return state
 
     state = lax.fori_loop(start, start + single, turn, state) if not isinstance(single, int) or single else state
-    return lax.fori_loop(0, count // block, turns, state)
+    return turns(0, state) if isinstance(count, int) and count == block else lax.fori_loop(0, count // block, turns, state)
 
 
 def group_kernel(

time: 79.8 us -> 79.8 us (level)
  no operation moved by 1% of the time
where the time goes in v13:
time: 79.8 us; the launch traced here: 78.5 us
  blocking collectives  43.4 us (54%)
  Pallas kernels  20.8 us (26%)
  starting transfers between devices  6.19 us (8%)
  waiting for transfers between devices  5.4 us (7%)
  local copies, waits for them, and re-layouts  1.96 us (2%)
    all_to_all x1, blocking collectives, shards(): parts = lax.all_to_all(parts, 'tm', 0, 0, axis_index_groups=across)  23.5 us
    pallas_call x3, Pallas kernels, call(): pl.pallas_call(kernel, out_shape=[jax.ShapeDtypeStruct(s, jnp.float32) fo...  20.8 us
    all_gather x1, blocking collectives, shards(): shares = lax.all_gather(share, 'tm', axis_index_groups=inside)  17.3 us
    ppermute x1, waiting for transfers between devices, shards(): far = lax.ppermute(own, 'tm', [(i, i + 2) for i in range(devices - 2)])  5.39 us
    ppermute x1, starting transfers between devices, shards(): far = lax.ppermute(own, 'tm', [(i, i + 2) for i in range(devices - 2)])  4.28 us
    all_gather x1, blocking collectives, shards(): sides = lax.all_gather(parts[:groups - 1], 'tm', axis_index_groups=cores)  2.53 us
    unnamed x12, local copies, waits for them, and re-layouts  1.93 us
    ppermute x1, starting transfers between devices, shards(): near = lax.ppermute(own, 'tm', [(i, i + 1) for i in range(devices - 1)])  1.91 us
  transfers between devices with their start and end apart: 2, of which 1 were waited for; matrix products, arithmetic and copies ran while one was open for 0% of the time, Pallas kernels for 3%

profile of v13, /device:TPU:62, one launch (start us, length us, event | category | flops | bytes accessed | tf_op | source)
XLA Modules:
  0.0 78.5 jit_solution(8129543962271417412)
XLA Ops:
  0.6 4.3 %collective-permute-start = (f32[2,64,64]{2,1,0:T(8,128)}, f32[2,64,64]{2,1,0:T(8,128)S(1)}, u32[]{:S(2)}, u32[]{:S(2)}) collective-permute-start(f32[2,64,64]{2,1,0:T(8,128)} %bitcast.11), channel_id=1, source_target_pairs={{0,2},{1,3},{2,4},{3,5},{4,6},{5,7},{6,8},{7,9},{8,10},{9,11},{10,... | collective-permute-start | bytes 98312 | tf_op jit(solution)/shard_map/ppermute | solution.py:324
  4.9 0.0 copy-start.1
  4.9 1.1 %copy-done.1 = bf16[256,1664]{1,0:T(8,128)(2,1)S(1)} copy-done((bf16[256,1664]{1,0:T(8,128)(2,1)S(1)}, bf16[256,1664]{1,0:T(8,128)(2,1)}, u32[]{:S(2)}) %copy-start.1) | copy-done | bytes 851992
  6.1 0.0 copy-start.5
  6.1 0.0 copy-start.2
  6.1 0.0 copy-start.3
  6.1 0.0 copy-start.4
  6.1 0.1 shard_map.93.near_table
  6.2 0.8 copy-done.5
  6.9 1.9 %collective-permute-start.1 = (f32[2,64,64]{2,1,0:T(8,128)S(1)}, f32[2,64,64]{2,1,0:T(8,128)S(1)}, u32[]{:S(2)}, u32[]{:S(2)}) collective-permute-start(f32[2,64,64]{2,1,0:T(8,128)S(1)} %bitcast.12), channel_id=1, source_target_pairs={{0,1},{1,2},{2,3},{3,4},{4,5},{5,6},{6,7},{7,8},{8,9},{9,10},{10,1... | collective-permute-start | bytes 98312 | tf_op jit(solution)/shard_map/ppermute | solution.py:336
  8.8 0.0 copy-done.2
  8.8 0.0 copy-done.3
  8.9 0.0 copy-done.4
  8.9 0.0 copy-start
  8.9 5.4 %collective-permute-done.far_ref = f32[2,64,64]{2,1,0:T(8,128)S(1)} collective-permute-done((f32[2,64,64]{2,1,0:T(8,128)}, f32[2,64,64]{2,1,0:T(8,128)S(1)}, u32[]{:S(2)}, u32[]{:S(2)}) %collective-permute-start) | collective-permute-done | bytes 32800 | tf_op jit(solution)/shard_map/ppermute | solution.py:324
  14.3 2.5 %shard_map.94 = (f32[64,128]{1,0:T(8,128)S(1)}, f32[64,128]{1,0:T(8,128)S(1)}) custom-call(f32[2,64,64]{2,1,0:T(8,128)S(1)} %collective-permute-done.far_ref, f32[4,64,64]{2,1,0:T(8,128)S(1)} %pad_maximum_fusion.fields, bf16[256,1664]{1,0:T(8,128)(2,1)S(1)} %shard_map.93.near_table), custom_call_target="tpu_custom_call" | custom-call | tf_op jit(solution)/shard_map/pallas_call | solution.py:309
  16.8 17.3 %all-gather = f32[1024,128]{1,0:T(8,128)S(1)} all-gather(f32[64,128]{1,0:T(8,128)S(1)} %get-tuple-element.16), channel_id=2, replica_groups={{0,1,2,3,4,5,6,7,8,9,10,11,12,13,14,15},{16,17,18,19,20,21,22,23,24,25,..., dimensions={0}, use_global_device_ids=true | all-gather | bytes 557056 | tf_op jit(solution)/shard_map/all_gather | solution.py:339
  34.1 0.0 collective-permute-done.1.near_ref
  34.1 0.0 copy-done
  34.1 6.3 %shard_map.95 = (f32[64,128]{1,0:T(8,128)S(1)}, f32[64,128]{1,0:T(8,128)S(1)}, f32[32,32,128]{2,1,0:T(8,128)S(1)}, f32[2,64,64]{2,1,0:T(8,128)}) custom-call(f32[16,64,128]{2,1,0:T(8,128)S(1)} %bitcast.6, f32[2,64,64]{2,1,0:T(8,128)S(1)} %collective-permute-done.1.near_ref, f32[64,128]{1,0:T(8,128)S(1)} %get-tuple-element.18.arrived_ref, ...), custom_call_target="tpu_custom_call" | custom-call | tf_op jit(solution)/shard_map/pallas_call | solution.py:309
  40.4 23.5 %all_to_all.5 = f32[32,32,128]{2,1,0:T(8,128)S(1)} all-to-all(f32[32,32,128]{2,1,0:T(8,128)S(1)} %get-tuple-element.19), channel_id=1, replica_groups={{0,16,32,48,64,80,96,112,128,144,160,176,192,208,224,240,256,272,288,30..., dimensions={0} | all-to-all | bytes 1048576 | tf_op jit(solution)/shard_map/all_to_all | solution.py:350
  64.0 2.5 %all-gather.1 = f32[62,32,128]{2,1,0:T(8,128)S(1)} all-gather(f32[31,32,128]{2,1,0:T(8,128)S(1)} %slice.4), channel_id=3, replica_groups={{0,1},{2,3},{4,5},{6,7},{8,9},{10,11},{12,13},{14,15},{16,17},{18,19},{..., dimensions={0}, use_global_device_ids=true | all-gather | bytes 1523712 | tf_op jit(solution)/shard_map/all_gather | solution.py:352
  66.5 12.0 %shard_map.96 = (f32[4,2,64,64]{3,2,1,0:T(8,128)}, f32[1,2,64,64]{3,2,1,0:T(8,128)}, f32[1,2,64,64]{3,2,1,0:T(8,128)}) custom-call(f32[2,31,32,128]{3,2,1,0:T(8,128)S(1)} %bitcast.8, f32[64,128]{1,0:T(8,128)S(1)} %get-tuple-element.20.rhs_ref, f32[16,64,128]{2,1,0:T(8,128)S(1)} %bitcast.7, f32[64,128]{1,0:T(8,128)S(1)} %get-tuple-element.21.first_ref, ...), custom_call_target="tpu_custom_call" | custom-call | tf_op jit(solution)/shard_map/pallas_call | solution.py:309
  (2 shorter events, 0.0 us)
Async XLA Ops:
  0.6 13.7 %collective-permute-start = (f32[2,64,64]{2,1,0:T(8,128)}, f32[2,64,64]{2,1,0:T(8,128)S(1)}, u32[]{:S(2)}, u32[]{:S(2)}) collective-permute-start(f32[2,64,64]{2,1,0:T(8,128)} %bitcast.11), channel_id=1, source_target_pairs={{0,2},{1,3},{2,4},{3,5},{4,6},{5,7},{6,8},{7,9},{8,10},{9,11},{10,... | collective-permute-start | bytes 98312 | tf_op jit(solution)/shard_map/ppermute | solution.py:324
  4.9 1.2 %copy-start.1 = (bf16[256,1664]{1,0:T(8,128)(2,1)S(1)}, bf16[256,1664]{1,0:T(8,128)(2,1)}, u32[]{:S(2)}) copy-start(bf16[256,1664]{1,0:T(8,128)(2,1)} %constant.5.clone.source) | copy-start | bytes 2555908
  6.1 0.8 %copy-start.5 = (f32[1,2,64,64]{3,2,1,0:T(8,128)S(1)}, f32[1,2,64,64]{3,2,1,0:T(8,128)}, u32[]{:S(2)}) copy-start(f32[1,2,64,64]{3,2,1,0:T(8,128)} %param.7) | copy-start | bytes 98308
  6.1 2.8 %copy-start.2 = (f32[2,64,64]{2,1,0:T(8,128)S(1)}, f32[2,64,64]{2,1,0:T(8,128)}, u32[]{:S(2)}) copy-start(f32[2,64,64]{2,1,0:T(8,128)} %param.6) | copy-start | bytes 98308
  6.1 2.8 %copy-start.3 = (f32[64,64]{1,0:T(8,128)S(1)}, f32[64,64]{1,0:T(8,128)}, u32[]{:S(2)}) copy-start(f32[64,64]{1,0:T(8,128)} %param.9) | copy-start | bytes 49156
  6.1 2.8 %copy-start.4 = (f32[64,64]{1,0:T(8,128)S(1)}, f32[64,64]{1,0:T(8,128)}, u32[]{:S(2)}) copy-start(f32[64,64]{1,0:T(8,128)} %param.8) | copy-start | bytes 49156
  6.9 27.2 %collective-permute-start.1 = (f32[2,64,64]{2,1,0:T(8,128)S(1)}, f32[2,64,64]{2,1,0:T(8,128)S(1)}, u32[]{:S(2)}, u32[]{:S(2)}) collective-permute-start(f32[2,64,64]{2,1,0:T(8,128)S(1)} %bitcast.12), channel_id=1, source_target_pairs={{0,1},{1,2},{2,3},{3,4},{4,5},{5,6},{6,7},{7,8},{8,9},{9,10},{10,1... | collective-permute-start | bytes 98312 | tf_op jit(solution)/shard_map/ppermute | solution.py:336
  8.9 25.2 %copy-start = (bf16[256,1536]{1,0:T(8,128)(2,1)S(1)}, bf16[256,1536]{1,0:T(8,128)(2,1)}, u32[]{:S(2)}) copy-start(bf16[256,1536]{1,0:T(8,128)(2,1)} %constant.4.clone.far_table) | copy-start | bytes 2359300
